TPU v7x, 32 devices: a whole 2x2x4 slice. The times are simulated.
32 devices in a mesh: dp: 2 (over x), sp: 4 (over z), tp: 4 (over y, core).
Axes of the slice: x: 2, y: 2, z: 4, core: 2. Of those that a mesh axis runs over, the one named last changes fastest.
Arguments:
- block_in: bfloat16 [8, 1024, 2048], P('dp', ('sp', 'tp')), may hold values from -6 to 6
- cotangent: bfloat16 [8, 1024, 2048], P('dp', ('sp', 'tp')), may hold values from -6 to 6
- qkv_weight: float32 [8, 2048, 384], P('tp', ('dp', 'sp')), may hold values from -0.125 to 0.125
- proj_weight: float32 [8, 256, 2048], P('tp', ('dp', 'sp')), may hold values from -1 to 1
- feed_weight: float32 [2, 2048, 8192], P(None, ('dp', 'sp'), 'tp'), may hold values from -0.125 to 0.125
- down_weight: float32 [32, 256, 2048], P('tp', ('dp', 'sp')), may hold values from -0.0625 to 0.0625
- norm_gains: float32 [2, 2048], P(None, ('dp', 'sp')), may hold values from 0.25 to 1.75
- qkv_first: float32 [8, 2048, 384], P('tp', ('dp', 'sp')), may hold values from -80 to 80
- proj_first: float32 [8, 256, 2048], P('tp', ('dp', 'sp')), may hold values from -6 to 6
- feed_first: float32 [2, 2048, 8192], P(None, ('dp', 'sp'), 'tp'), may hold values from -16 to 16
- down_first: float32 [32, 256, 2048], P('tp', ('dp', 'sp')), may hold values from -32 to 32
- gains_first: float32 [2, 2048], P(None, ('dp', 'sp')), may hold values from -64 to 64
- qkv_second: float32 [8, 2048, 384], P('tp', ('dp', 'sp')), may hold values from 573.44 to 7372.8
- proj_second: float32 [8, 256, 2048], P('tp', ('dp', 'sp')), may hold values from 4 to 51.2
- feed_second: float32 [2, 2048, 8192], P(None, ('dp', 'sp'), 'tp'), may hold values from 22.1184 to 294.912
- down_second: float32 [32, 256, 2048], P('tp', ('dp', 'sp')), may hold values from 90.112 to 1179.648
- gains_second: float32 [2, 2048], P(None, ('dp', 'sp')), may hold values from 352.256 to 4751.36
Outputs:
- block_out: float32 [8, 1024, 2048], P('dp', ('sp', 'tp'))
- input_grad: float32 [8, 1024, 2048], P('dp', ('sp', 'tp'))
- qkv_grad: float32 [8, 2048, 384], P('tp', ('dp', 'sp'))
- proj_grad: float32 [8, 256, 2048], P('tp', ('dp', 'sp'))
- feed_grad: float32 [2, 2048, 8192], P(None, ('dp', 'sp'), 'tp')
- down_grad: float32 [32, 256, 2048], P('tp', ('dp', 'sp'))
- gains_grad: float32 [2, 2048], P(None, ('dp', 'sp'))
- qkv_new: float32 [8, 2048, 384], P('tp', ('dp', 'sp'))
- proj_new: float32 [8, 256, 2048], P('tp', ('dp', 'sp'))
- feed_new: float32 [2, 2048, 8192], P(None, ('dp', 'sp'), 'tp')
- down_new: float32 [32, 256, 2048], P('tp', ('dp', 'sp'))
- gains_new: float32 [2, 2048], P(None, ('dp', 'sp'))
- qkv_first_new: float32 [8, 2048, 384], P('tp', ('dp', 'sp'))
- proj_first_new: float32 [8, 256, 2048], P('tp', ('dp', 'sp'))
- feed_first_new: float32 [2, 2048, 8192], P(None, ('dp', 'sp'), 'tp')
- down_first_new: float32 [32, 256, 2048], P('tp', ('dp', 'sp'))
- gains_first_new: float32 [2, 2048], P(None, ('dp', 'sp'))
- qkv_second_new: float32 [8, 2048, 384], P('tp', ('dp', 'sp'))
- proj_second_new: float32 [8, 256, 2048], P('tp', ('dp', 'sp'))
- feed_second_new: float32 [2, 2048, 8192], P(None, ('dp', 'sp'), 'tp')
- down_second_new: float32 [32, 256, 2048], P('tp', ('dp', 'sp'))
- gains_second_new: float32 [2, 2048], P(None, ('dp', 'sp'))
All inputs are finite; a program needn't handle non-finite values.
Results may differ from a plain program's by a relative error of at most 0.014.
The roundings to bfloat16 on the way count: a program that leaves them out, or rounds other values in their place, can miss the bound.
Values may be sent and summed in bfloat16 or wider, within the bound.
No kernel may reach another device: no remote copies, remote signals or barrier semaphores. Data moves between devices by JAX's collectives and lax.ppermute only.
A program may use at most 256 MiB of HBM per device.

v0:
```python
import jax
import jax.numpy as jnp
from jax import lax
from jax.sharding import PartitionSpec as P

HD = 64
QPK = 4
STEP = 10


NORM_EPSILON = 1e-05
ROPE_BASE = 500000.0
MASKED = -1e30
BETA_ONE = 0.9
BETA_TWO = 0.95
ADAM_EPSILON = 1e-08
WEIGHT_DECAY = 0.1
QKV_RATE = 0.05
PROJ_RATE = 0.4
FEED_RATE = 0.05
DOWN_RATE = 0.03
GAIN_RATE = 0.5


def rms_forward(activations, gain_row):
    mean_square = jnp.mean(activations * activations, axis=-1, keepdims=True)
    inverse_rms = lax.rsqrt(mean_square + NORM_EPSILON)
    unit_rows = activations * inverse_rms
    return (unit_rows, inverse_rms, (unit_rows * gain_row).astype(jnp.bfloat16))


def rms_backward(grad_normed, unit_rows, inverse_rms, gain_row):
    grad_unit = grad_normed * gain_row
    row_inner = jnp.mean(grad_unit * unit_rows, axis=-1, keepdims=True)
    return (
        inverse_rms * (grad_unit - unit_rows * row_inner),
        jnp.sum(grad_normed * unit_rows, axis=(0, 1)),
    )


def rope_tables(positions, head_size):
    half_width = head_size // 2
    frequency = ROPE_BASE ** (-(jnp.arange(half_width, dtype=jnp.float32) * 2.0 / head_size))
    angles = positions.astype(jnp.float32)[:, None] * frequency[None, :]
    return (jnp.cos(angles), jnp.sin(angles))


def rotate(values, cosine_table, sine_table, direction):
    half_width = values.shape[-1] // 2
    table_shape = (1, values.shape[1]) + (1,) * (values.ndim - 3) + (half_width,)
    cosine_part = cosine_table.reshape(table_shape)
    sine_part = sine_table.reshape(table_shape) * direction
    first_half = values[..., :half_width]
    second_half = values[..., half_width:]
    return jnp.concatenate(
        [
            first_half * cosine_part - second_half * sine_part,
            second_half * cosine_part + first_half * sine_part,
        ],
        axis=-1,
    )


def masked_scores(query_block, keyval_block, allowed):
    scores = jnp.einsum(
        "qgnd,kgd->gqnk", query_block, keyval_block[..., :HD], preferred_element_type=jnp.float32
    ) * HD ** (-0.5)
    return jnp.where(allowed[None, :, None, :], scores, MASKED)


def adamw(param, grad, first, second, rate, decay):
    first_new = BETA_ONE * first + (1.0 - BETA_ONE) * grad
    second_new = BETA_TWO * second + (1.0 - BETA_TWO) * grad * grad
    first_hat = first_new / (1.0 - BETA_ONE**STEP)
    second_hat = second_new / (1.0 - BETA_TWO**STEP)
    param_new = param - rate * (first_hat / (jnp.sqrt(second_hat) + ADAM_EPSILON) + decay * param)
    return (param_new, first_new, second_new)


def local(
    block_in,
    cotangent,
    qkv_weight,
    proj_weight,
    feed_weight,
    down_weight,
    norm_gains,
    qkv_first,
    proj_first,
    feed_first,
    down_first,
    gains_first,
    qkv_second,
    proj_second,
    feed_second,
    down_second,
    gains_second,
):
    qkv_low, proj_low, feed_low, down_low, gains_low = (
        lax.all_gather(qkv_weight.astype(jnp.bfloat16), ("dp", "sp"), axis=1, tiled=True),
        lax.all_gather(proj_weight.astype(jnp.bfloat16), ("dp", "sp"), axis=1, tiled=True),
        lax.all_gather(feed_weight.astype(jnp.bfloat16), ("dp", "sp"), axis=1, tiled=True),
        lax.all_gather(down_weight.astype(jnp.bfloat16), ("dp", "sp"), axis=1, tiled=True),
        lax.all_gather(norm_gains.astype(jnp.bfloat16), ("dp", "sp"), axis=1, tiled=True),
    )
    sequences, local_rows, model_width = block_in.shape
    groups = qkv_low.shape[0]
    columns = qkv_low.shape[2]
    query_width = QPK * HD
    span_rows = local_rows * lax.axis_size("tp")
    length = span_rows * lax.axis_size("sp")
    flat_rows = sequences * span_rows
    gain_values = gains_low.astype(jnp.float32)
    proj_flat = proj_low.reshape(groups * query_width, model_width)
    down_flat = down_low.reshape(-1, model_width)
    inputs = block_in.astype(jnp.float32)
    unit_one, inverse_one, normed_one = rms_forward(inputs, gain_values[0])
    normed_one_all = lax.all_gather(normed_one, "tp", axis=1, tiled=True)
    flat_one = normed_one_all.reshape(flat_rows, model_width)
    projected = jnp.einsum("rd,gdc->rgc", flat_one, qkv_low, preferred_element_type=jnp.float32)
    projected = projected.reshape(sequences, span_rows, groups, columns)
    positions = lax.axis_index("sp") * span_rows + jnp.arange(span_rows)
    cosine_table, sine_table = rope_tables(positions, HD)
    queries = rotate(
        projected[..., :query_width].reshape(sequences, span_rows, groups, QPK, HD),
        cosine_table,
        sine_table,
        1.0,
    ).astype(jnp.bfloat16)
    key_rows = rotate(projected[..., query_width : query_width + HD], cosine_table, sine_table, 1.0)
    keyvals = jnp.concatenate([key_rows, projected[..., query_width + HD :]], axis=-1).astype(
        jnp.bfloat16
    )
    keyvals_all = lax.all_gather(keyvals, "sp", axis=1, tiled=True)
    allowed = jnp.arange(length)[None, :] <= positions[:, None]

    def attend(operands):
        query_block, keyval_block = operands
        scores = masked_scores(query_block, keyval_block, allowed)
        row_peak = jnp.max(scores, axis=-1, keepdims=True)
        weights = jnp.exp(scores - row_peak)
        row_total = jnp.sum(weights, axis=-1, keepdims=True)
        softmax_low = (weights / row_total).astype(jnp.bfloat16)
        context_block = jnp.einsum(
            "gqnk,kgd->qgnd",
            softmax_low,
            keyval_block[..., HD:],
            preferred_element_type=jnp.float32,
        )
        return (context_block.astype(jnp.bfloat16), (row_peak + jnp.log(row_total))[..., 0])

    context, log_total = lax.map(attend, (queries, keyvals_all))
    flat_context = context.reshape(flat_rows, groups * query_width)
    attn_part = jnp.dot(flat_context, proj_flat, preferred_element_type=jnp.float32)
    attn_mine = lax.psum_scatter(
        attn_part.reshape(sequences, span_rows, model_width), "tp", scatter_dimension=1, tiled=True
    )
    hidden_one = inputs + attn_mine
    unit_two, inverse_two, normed_two = rms_forward(hidden_one, gain_values[1])
    normed_two_all = lax.all_gather(normed_two, "tp", axis=1, tiled=True)
    flat_two = normed_two_all.reshape(flat_rows, model_width)
    gate_rows = jnp.dot(flat_two, feed_low[0], preferred_element_type=jnp.float32)
    up_rows = jnp.dot(flat_two, feed_low[1], preferred_element_type=jnp.float32)
    sigmoid = jax.nn.sigmoid(gate_rows)
    activated = gate_rows * sigmoid
    hidden = (activated * up_rows).astype(jnp.bfloat16)
    ffn_part = jnp.dot(hidden, down_flat, preferred_element_type=jnp.float32)
    ffn_mine = lax.psum_scatter(
        ffn_part.reshape(sequences, span_rows, model_width), "tp", scatter_dimension=1, tiled=True
    )
    block_out = hidden_one + ffn_mine
    grad_all = lax.all_gather(cotangent, "tp", axis=1, tiled=True).reshape(flat_rows, model_width)
    down_grad_part = jnp.dot(hidden.T, grad_all, preferred_element_type=jnp.float32).reshape(
        down_low.shape
    )
    grad_hidden = jnp.dot(grad_all, down_flat.T, preferred_element_type=jnp.float32)
    grad_gate = (grad_hidden * up_rows * sigmoid * (1.0 + gate_rows * (1.0 - sigmoid))).astype(
        jnp.bfloat16
    )
    grad_up = (grad_hidden * activated).astype(jnp.bfloat16)
    feed_grad_part = jnp.stack(
        [
            jnp.dot(flat_two.T, grad_gate, preferred_element_type=jnp.float32),
            jnp.dot(flat_two.T, grad_up, preferred_element_type=jnp.float32),
        ]
    )
    grad_normed_two = jnp.dot(
        grad_gate, feed_low[0].T, preferred_element_type=jnp.float32
    ) + jnp.dot(grad_up, feed_low[1].T, preferred_element_type=jnp.float32)
    grad_normed_two = lax.psum_scatter(
        grad_normed_two.reshape(sequences, span_rows, model_width),
        "tp",
        scatter_dimension=1,
        tiled=True,
    )
    back_two, gain_two_part = rms_backward(grad_normed_two, unit_two, inverse_two, gain_values[1])
    grad_hidden_one = cotangent.astype(jnp.float32) + back_two
    grad_rows = lax.all_gather(grad_hidden_one.astype(jnp.bfloat16), "tp", axis=1, tiled=True)
    grad_rows = grad_rows.reshape(flat_rows, model_width)
    proj_grad_part = jnp.dot(flat_context.T, grad_rows, preferred_element_type=jnp.float32).reshape(
        proj_low.shape
    )
    grad_context = jnp.dot(grad_rows, proj_flat.T, preferred_element_type=jnp.float32)
    grad_context = grad_context.reshape(context.shape).astype(jnp.bfloat16)

    def attend_back(operands):
        query_block, keyval_block, log_block, grad_block = operands
        scores = masked_scores(query_block, keyval_block, allowed)
        softmax_rows = jnp.exp(scores - log_block[..., None])
        grad_softmax = jnp.einsum(
            "qgnd,kgd->gqnk", grad_block, keyval_block[..., HD:], preferred_element_type=jnp.float32
        )
        row_inner = jnp.sum(softmax_rows * grad_softmax, axis=-1, keepdims=True)
        grad_scores = (softmax_rows * (grad_softmax - row_inner)).astype(jnp.bfloat16)
        grad_query = jnp.einsum(
            "gqnk,kgd->qgnd",
            grad_scores,
            keyval_block[..., :HD],
            preferred_element_type=jnp.float32,
        ) * HD ** (-0.5)
        grad_key = jnp.einsum(
            "gqnk,qgnd->kgd", grad_scores, query_block, preferred_element_type=jnp.float32
        ) * HD ** (-0.5)
        grad_value = jnp.einsum(
            "gqnk,qgnd->kgd",
            softmax_rows.astype(jnp.bfloat16),
            grad_block,
            preferred_element_type=jnp.float32,
        )
        return (grad_query, jnp.concatenate([grad_key, grad_value], axis=-1))

    grad_queries, grad_keyvals = lax.map(
        attend_back, (queries, keyvals_all, log_total, grad_context)
    )
    grad_keyvals = lax.psum_scatter(grad_keyvals, "sp", scatter_dimension=1, tiled=True)
    grad_keys = rotate(grad_keyvals[..., :HD], cosine_table, sine_table, -1.0).astype(jnp.bfloat16)
    grad_values = grad_keyvals[..., HD:].astype(jnp.bfloat16)
    grad_queries = rotate(grad_queries, cosine_table, sine_table, -1.0).astype(jnp.bfloat16)
    grad_queries = grad_queries.reshape(sequences, span_rows, groups, query_width)
    grad_projected = jnp.concatenate([grad_queries, grad_keys, grad_values], axis=-1)
    grad_projected = grad_projected.reshape(flat_rows, groups, columns)
    qkv_grad_part = jnp.einsum(
        "rd,rgc->gdc", flat_one, grad_projected, preferred_element_type=jnp.float32
    )
    grad_normed_one = jnp.einsum(
        "rgc,gdc->rd", grad_projected, qkv_low, preferred_element_type=jnp.float32
    )
    grad_normed_one = lax.psum_scatter(
        grad_normed_one.reshape(sequences, span_rows, model_width),
        "tp",
        scatter_dimension=1,
        tiled=True,
    )
    back_one, gain_one_part = rms_backward(grad_normed_one, unit_one, inverse_one, gain_values[0])
    input_grad = grad_hidden_one + back_one
    gains_part = jnp.stack([gain_one_part, gain_two_part])
    feed_grad, down_grad, qkv_grad, proj_grad, gains_sum = (
        lax.psum_scatter(feed_grad_part, ("dp", "sp"), scatter_dimension=1, tiled=True),
        lax.psum_scatter(down_grad_part, ("dp", "sp"), scatter_dimension=1, tiled=True),
        lax.psum_scatter(qkv_grad_part, ("dp", "sp"), scatter_dimension=1, tiled=True),
        lax.psum_scatter(proj_grad_part, ("dp", "sp"), scatter_dimension=1, tiled=True),
        lax.psum_scatter(gains_part, ("dp", "sp"), scatter_dimension=1, tiled=True),
    )
    gains_grad = lax.psum(gains_sum, "tp")
    qkv_new, qkv_first_new, qkv_second_new = adamw(
        qkv_weight, qkv_grad, qkv_first, qkv_second, QKV_RATE, WEIGHT_DECAY
    )
    proj_new, proj_first_new, proj_second_new = adamw(
        proj_weight, proj_grad, proj_first, proj_second, PROJ_RATE, WEIGHT_DECAY
    )
    feed_new, feed_first_new, feed_second_new = adamw(
        feed_weight, feed_grad, feed_first, feed_second, FEED_RATE, WEIGHT_DECAY
    )
    down_new, down_first_new, down_second_new = adamw(
        down_weight, down_grad, down_first, down_second, DOWN_RATE, WEIGHT_DECAY
    )
    gains_new, gains_first_new, gains_second_new = adamw(
        norm_gains, gains_grad, gains_first, gains_second, GAIN_RATE, 0.0
    )
    return (
        block_out,
        input_grad,
        qkv_grad,
        proj_grad,
        feed_grad,
        down_grad,
        gains_grad,
        qkv_new,
        proj_new,
        feed_new,
        down_new,
        gains_new,
        qkv_first_new,
        proj_first_new,
        feed_first_new,
        down_first_new,
        gains_first_new,
        qkv_second_new,
        proj_second_new,
        feed_second_new,
        down_second_new,
        gains_second_new,
    )


def solution(mesh):
    placed = (
        P("dp", ("sp", "tp"), None),
        P("dp", ("sp", "tp"), None),
        P("tp", ("dp", "sp"), None),
        P("tp", ("dp", "sp"), None),
        P(None, ("dp", "sp"), "tp"),
        P("tp", ("dp", "sp"), None),
        P(None, ("dp", "sp")),
        P("tp", ("dp", "sp"), None),
        P("tp", ("dp", "sp"), None),
        P(None, ("dp", "sp"), "tp"),
        P("tp", ("dp", "sp"), None),
        P(None, ("dp", "sp")),
        P("tp", ("dp", "sp"), None),
        P("tp", ("dp", "sp"), None),
        P(None, ("dp", "sp"), "tp"),
        P("tp", ("dp", "sp"), None),
        P(None, ("dp", "sp")),
    )
    return jax.shard_map(
        local,
        mesh=mesh,
        in_specs=placed,
        out_specs=(
            P("dp", ("sp", "tp"), None),
            P("dp", ("sp", "tp"), None),
            P("tp", ("dp", "sp"), None),
            P("tp", ("dp", "sp"), None),
            P(None, ("dp", "sp"), "tp"),
            P("tp", ("dp", "sp"), None),
            P(None, ("dp", "sp")),
            P("tp", ("dp", "sp"), None),
            P("tp", ("dp", "sp"), None),
            P(None, ("dp", "sp"), "tp"),
            P("tp", ("dp", "sp"), None),
            P(None, ("dp", "sp")),
            P("tp", ("dp", "sp"), None),
            P("tp", ("dp", "sp"), None),
            P(None, ("dp", "sp"), "tp"),
            P("tp", ("dp", "sp"), None),
            P(None, ("dp", "sp")),
            P("tp", ("dp", "sp"), None),
            P("tp", ("dp", "sp"), None),
            P(None, ("dp", "sp"), "tp"),
            P("tp", ("dp", "sp"), None),
            P(None, ("dp", "sp")),
        ),
        check_vma=False,
    )
```

profile of v0, /device:TPU:0, one launch (start us, length us, event | category | flops | bytes accessed | tf_op | source)
XLA Modules:
  0.0 2342.0 jit_solution(1124611244705418744)
XLA Ops:
  9.9 22.3 all_gather.30
  37.8 36.2 %all-gather.12.cloned.1.call-done = bf16[2,2048,384]{2,1,0:T(8,128)(2,1)} async-done(((bf16[2,256,384]{2,1,0:T(8,128)(2,1)}), bf16[2,2048,384]{2,1,0:T(8,128)(2,1)}) %all-gather.12.cloned.1.call-update) | async-done | bytes 3145744 | tf_op jit(solution)/shard_map/all_gather | solution.py:100
  73.9 35.3 %all-gather.10.cloned.1.call-done = bf16[4,256,2048]{2,1,0:T(8,128)(2,1)} async-done(((bf16[4,64,2048]{2,1,0:T(8,128)(2,1)}), bf16[4,256,2048]{2,1,0:T(8,128)(2,1)}) %all-gather.10.cloned.1.call-update) | async-done | bytes 4194320 | tf_op jit(solution)/shard_map/all_gather | solution.py:118
  136.1 40.0 %all-gather.14.cloned.1.call-done = bf16[4,1024,2,128]{3,1,2,0:T(8,128)(2,1)} async-done(((bf16[4,256,2,128]{3,1,2,0:T(8,128)(2,1)}), bf16[4,1024,2,128]{3,1,2,0:T(8,128)(2,1)}) %all-gather.14.cloned.1.call-update) | async-done | bytes 2097168 | tf_op jit(solution)/shard_map/all_gather | solution.py:134
  179.0 32.1 %while.26 = (s32[]{:T(128)}, bf16[4,256,2,4,64]{1,4,3,2,0:T(8,128)(2,1)}, f32[4,2,256,4]{2,3,1,0:T(4,128)}, bf16[4,1024,2,128]{1,3,2,0:T(8,128)(2,1)S(1)}, bf16[...) while((s32[]{:T(128)}, bf16[4,256,2,4,64]{1,4,3,2,0:T(8,128)(2,1)}, ...), condition=%wide.region_4.5_spmd.clone, body=%wide.region_1.4_spmd.clone.sunk | while | flops 562427904 | bytes 28378212 | solution.py:152
  211.1 15.5 all-gather.16.cloned.1.call-done
  238.3 66.3 %reduce-scatter.13.cloned.1.call-done = f32[4,64,2048]{2,1,0:T(8,128)} async-done(((f32[4,256,2048]{2,1,0:T(8,128)}), f32[4,64,2048]{2,1,0:T(8,128)}) %reduce-scatter.13.cloned.1.call-update) | async-done | bytes 2097168 | tf_op jit(solution)/shard_map/reduce_scatter | solution.py:155
  309.4 225.7 %all-gather.20.cloned.1.call-done = bf16[2,2048,2048]{2,1,0:T(8,128)(2,1)} async-done(((bf16[2,256,2048]{2,1,0:T(8,128)(2,1)}), bf16[2,2048,2048]{2,1,0:T(8,128)(2,1)}) %all-gather.20.cloned.1.call-update) | async-done | bytes 16777232 | tf_op jit(solution)/shard_map/all_gather | solution.py:102
  535.1 34.9 %all-gather.18.cloned.1.call-done = bf16[4,256,2048]{2,1,0:T(8,128)(2,1)} async-done(((bf16[4,64,2048]{2,1,0:T(8,128)(2,1)}), bf16[4,256,2048]{2,1,0:T(8,128)(2,1)}) %all-gather.18.cloned.1.call-update) | async-done | bytes 4194320 | tf_op jit(solution)/shard_map/all_gather | solution.py:160
  570.0 13.5 fusion.50
  583.6 17.7 fusion.44
  607.7 15.1 fusion.104
  622.9 282.1 %reduce-scatter.29.cloned.1.call-done = f32[8,32,2048]{2,1,0:T(8,128)} async-done(((f32[8,256,2048]{2,1,0:T(8,128)}), f32[8,32,2048]{2,1,0:T(8,128)}) %reduce-scatter.29.cloned.1.call-update) | async-done | bytes 2097168 | tf_op jit(solution)/shard_map/reduce_scatter | solution.py:259
  913.6 124.0 %all-gather.22.cloned.1.call-done = bf16[8,256,2048]{2,1,0:T(8,128)(2,1)} async-done(((bf16[8,32,2048]{2,1,0:T(8,128)(2,1)}), bf16[8,256,2048]{2,1,0:T(8,128)(2,1)}) %all-gather.22.cloned.1.call-update) | async-done | bytes 8388624 | tf_op jit(solution)/shard_map/all_gather | solution.py:103
  1037.7 22.0 multiply_convert_fusion.1
  1059.7 12.7 fusion.49
  1072.4 13.5 fusion.53
  1086.2 69.8 %reduce-scatter.17.cloned.1.call-done = f32[4,64,2048]{2,1,0:T(8,128)} async-done(((f32[4,256,2048]{2,1,0:T(8,128)}), f32[4,64,2048]{2,1,0:T(8,128)}) %reduce-scatter.17.cloned.1.call-update) | async-done | bytes 2097168 | tf_op jit(solution)/shard_map/reduce_scatter | solution.py:190
  1160.7 34.6 %all-gather.26.cloned.1.call-done = bf16[4,256,2048]{2,1,0:T(8,128)(2,1)} async-done(((bf16[4,64,2048]{2,1,0:T(8,128)(2,1)}), bf16[4,256,2048]{2,1,0:T(8,128)(2,1)}) %all-gather.26.cloned.1.call-update) | async-done | bytes 4194320 | tf_op jit(solution)/shard_map/all_gather | solution.py:198
  1201.6 57.3 %while.27 = (s32[]{:T(128)}, f32[4,256,2,4,64]{1,4,3,2,0:T(8,128)S(1)}, f32[4,1024,2,128]{1,3,2,0:T(8,128)}, bf16[4,1024,2,128]{1,3,2,0:T(8,128)(2,1)}, bf16[4,2...) while((s32[]{:T(128)}, ...), condition=%wide.region_12.13_spmd.clone, body=%wide.region_10.12_spmd.clone.sunk | while | flops 1374418944 | bytes 74769568 | solution.py:232
  1262.5 73.4 %reduce-scatter.19.cloned.1.call-done = f32[4,256,2,128]{1,3,2,0:T(8,128)} async-done(((f32[4,1024,2,128]{1,3,2,0:T(8,128)}), f32[4,256,2,128]{1,3,2,0:T(8,128)}) %reduce-scatter.19.cloned.1.call-update) | async-done | bytes 1048592 | tf_op jit(solution)/shard_map/reduce_scatter | solution.py:235
  1368.8 14.5 fusion.102
  1383.4 15.6 convolution_bitcast_fusion.1
  1399.0 11.7 convolution_bitcast_fusion.2
  1410.7 11.9 reduce-scatter.21.cloned.1.call-done
  1426.5 23.3 pad_maximum_fusion
  1452.9 62.2 %reduce-scatter.25.cloned.1.call-done = f32[2,32,2048]{2,1,0:T(8,128)} async-done(((f32[2,256,2048]{2,1,0:T(8,128)}), f32[2,32,2048]{2,1,0:T(8,128)}) %reduce-scatter.25.cloned.1.call-update) | async-done | bytes 524304 | tf_op jit(solution)/shard_map/reduce_scatter | solution.py:261
  1518.0 118.7 %reduce-scatter.23.cloned.1.call-done = f32[2,256,384]{1,2,0:T(8,128)} async-done(((f32[2,2048,384]{1,2,0:T(8,128)}), f32[2,256,384]{1,2,0:T(8,128)}) %reduce-scatter.23.cloned.1.call-update) | async-done | bytes 786448 | tf_op jit(solution)/shard_map/reduce_scatter | solution.py:260
  1649.0 61.0 %reduce-scatter.15.cloned.1.call-done = f32[4,64,2048]{2,1,0:T(8,128)} async-done(((f32[4,256,2048]{2,1,0:T(8,128)}), f32[4,64,2048]{2,1,0:T(8,128)}) %reduce-scatter.15.cloned.1.call-update) | async-done | bytes 2097168 | tf_op jit(solution)/shard_map/reduce_scatter | solution.py:168
  1716.3 61.4 %reduce-scatter.31.cloned.1.call-done = f32[256,2]{1,0:T(8,128)} async-done(((f32[2048,2]{1,0:T(8,128)}), f32[256,2]{1,0:T(8,128)}) %reduce-scatter.31.cloned.1.call-update) | async-done | bytes 2064
  1784.9 539.4 %reduce-scatter.27.cloned.1.call-done = f32[2,256,2048]{2,1,0:T(8,128)} async-done(((f32[2,2048,2048]{2,1,0:T(8,128)}), f32[2,256,2048]{2,1,0:T(8,128)}) %reduce-scatter.27.cloned.1.call-update) | async-done | bytes 4194320 | tf_op jit(solution)/shard_map/reduce_scatter | solution.py:258
  2324.3 10.9 multiply_subtract_fusion
  (263 shorter events, 241.8 us)
Async XLA Ops:
  7.2 66.8 %all-gather.12.cloned.1.call-start = ((), (), s32[]{:S(2)}) async-start(), calls=%async_computation.11 | async-start | bytes 3538944 | tf_op jit(solution)/shard_map/all_gather | solution.py:100
  9.2 100.0 %all-gather.10.cloned.1.call-start = ((), (), s32[]{:S(2)}) async-start(), calls=%async_computation.10 | async-start | bytes 5242880 | tf_op jit(solution)/shard_map/all_gather | solution.py:118
  33.8 1125.1 %copy-start.17 = (f32[1,2048]{1,0:T(1,128)}, f32[1,2048]{1,0:T(1,128)S(1)}, u32[]{:S(2)}) copy-start(f32[1,2048]{1,0:T(1,128)S(1)} %get-tuple-element.349) | copy-start | bytes 24580
  36.9 139.2 %all-gather.14.cloned.1.call-start = ((), (), s32[]{:S(2)}) async-start(), calls=%async_computation.12 | async-start | bytes 2621440 | tf_op jit(solution)/shard_map/all_gather | solution.py:134
  37.8 97.8 %copy-start.12 = (f32[256,32]{0,1:T(8,128)}, f32[256,32]{0,1:T(8,128)S(1)}, u32[]{:S(2)}) copy-start(f32[256,32]{0,1:T(8,128)S(1)} %get-tuple-element.353) | copy-start | bytes 98308
  130.0 96.7 %all-gather.16.cloned.1.call-start = ((), (), s32[]{:S(2)}) async-start(), calls=%async_computation.13 | async-start | bytes 2359296 | tf_op jit(solution)/shard_map/all_gather | solution.py:101
  131.8 172.8 %reduce-scatter.13.cloned.1.call-start = ((), (), s32[]{:S(2)}) async-start(), calls=%async_computation.14 | async-start | bytes 10485760 | tf_op jit(solution)/shard_map/reduce_scatter | solution.py:155
  234.3 300.8 %all-gather.20.cloned.1.call-start = ((), (), s32[]{:S(2)}) async-start(), calls=%async_computation.16 | async-start | bytes 18874368 | tf_op jit(solution)/shard_map/all_gather | solution.py:102
  238.3 331.7 %all-gather.18.cloned.1.call-start = ((), (), s32[]{:S(2)}) async-start(), calls=%async_computation.15 | async-start | bytes 5242880 | tf_op jit(solution)/shard_map/all_gather | solution.py:160
  306.6 852.3 %copy-start = (f32[4,64,2048]{2,1,0:T(8,128)}, f32[4,64,2048]{2,1,0:T(8,128)S(1)}, u32[]{:S(2)}) copy-start(f32[4,64,2048]{2,1,0:T(8,128)S(1)} %get-tuple-element.328) | copy-start | bytes 6291460
  306.6 852.3 %copy-start.23 = (f32[4,64]{1,0:T(4,128)}, f32[4,64]{1,0:T(4,128)S(1)}, u32[]{:S(2)}) copy-start(f32[4,64]{1,0:T(4,128)S(1)} %add_rsqrt_fusion) | copy-start | bytes 3076
  308.0 299.6 %all-gather.24.cloned.1.call-start = ((), (), s32[]{:S(2)}) async-start(), calls=%async_computation.19 | async-start | bytes 5242880 | tf_op jit(solution)/shard_map/all_gather | solution.py:172
  308.8 596.2 %reduce-scatter.29.cloned.1.call-start = ((), (), s32[]{:S(2)}) async-start(), calls=%async_computation.27 | async-start | bytes 18874368 | tf_op jit(solution)/shard_map/reduce_scatter | solution.py:259
  622.8 414.9 %all-gather.22.cloned.1.call-start = ((), (), s32[]{:S(2)}) async-start(), calls=%async_computation.17 | async-start | bytes 9437184 | tf_op jit(solution)/shard_map/all_gather | solution.py:103
  913.6 242.4 %reduce-scatter.17.cloned.1.call-start = ((), (), s32[]{:S(2)}) async-start(), calls=%async_computation.20 | async-start | bytes 10485760 | tf_op jit(solution)/shard_map/reduce_scatter | solution.py:190
  1085.9 73.0 %copy-start.8 = (bf16[4,64,2048]{2,1,0:T(8,128)(2,1)S(1)}, bf16[4,64,2048]{2,1,0:T(8,128)(2,1)}, u32[]{:S(2)}) copy-start(bf16[4,64,2048]{2,1,0:T(8,128)(2,1)} %param.22) | copy-start | bytes 3145732
  1085.9 109.4 %all-gather.26.cloned.1.call-start = ((), (), s32[]{:S(2)}) async-start(), calls=%async_computation.21 | async-start | bytes 5242880 | tf_op jit(solution)/shard_map/all_gather | solution.py:198
  1160.7 175.3 %reduce-scatter.19.cloned.1.call-start = ((), (), s32[]{:S(2)}) async-start(), calls=%async_computation.22 | async-start | bytes 5242880 | tf_op jit(solution)/shard_map/reduce_scatter | solution.py:235
  1259.0 163.6 %reduce-scatter.21.cloned.1.call-start = ((), (), s32[]{:S(2)}) async-start(), calls=%async_computation.23 | async-start | bytes 10485760 | tf_op jit(solution)/shard_map/reduce_scatter | solution.py:248
  1350.2 164.9 %reduce-scatter.25.cloned.1.call-start = ((), (), s32[]{:S(2)}) async-start(), calls=%async_computation.25 | async-start | bytes 4718592 | tf_op jit(solution)/shard_map/reduce_scatter | solution.py:261
  1357.9 278.7 %reduce-scatter.23.cloned.1.call-start = ((), (), s32[]{:S(2)}) async-start(), calls=%async_computation.24 | async-start | bytes 7077888 | tf_op jit(solution)/shard_map/reduce_scatter | solution.py:260
  1368.6 341.4 %reduce-scatter.15.cloned.1.call-start = ((), (), s32[]{:S(2)}) async-start(), calls=%async_computation.18 | async-start | bytes 10485760 | tf_op jit(solution)/shard_map/reduce_scatter | solution.py:168
  1383.3 394.4 %reduce-scatter.31.cloned.1.call-start = ((), (), s32[]{:S(2)}) async-start(), calls=%async_computation.28 | async-start | bytes 1179648
  1426.2 898.1 %reduce-scatter.27.cloned.1.call-start = ((), (), s32[]{:S(2)}) async-start(), calls=%async_computation.26 | async-start | bytes 37748736 | tf_op jit(solution)/shard_map/reduce_scatter | solution.py:258
  1639.5 70.4 %copy-start.1 = (f32[4,64,2048]{2,1,0:T(8,128)S(1)}, f32[4,64,2048]{2,1,0:T(8,128)}, u32[]{:S(2)}) copy-start(f32[4,64,2048]{2,1,0:T(8,128)} %copy-done) | copy-start | bytes 6291460
  1639.5 70.4 %copy-start.18 = (f32[1,2048]{1,0:T(1,128)S(1)}, f32[1,2048]{1,0:T(1,128)}, u32[]{:S(2)}) copy-start(f32[1,2048]{1,0:T(1,128)} %copy-done.17) | copy-start | bytes 24580
  1639.5 70.5 %copy-start.24 = (f32[4,64]{1,0:T(4,128)S(1)}, f32[4,64]{1,0:T(4,128)}, u32[]{:S(2)}) copy-start(f32[4,64]{1,0:T(4,128)} %copy-done.23) | copy-start | bytes 3076
  1639.5 70.5 %copy-start.29 = (f32[4,64]{1,0:T(4,128)S(1)}, f32[4,64]{1,0:T(4,128)}, u32[]{:S(2)}) copy-start(f32[4,64]{1,0:T(4,128)} %copy-done.28) | copy-start | bytes 3076
  1649.0 135.3 %copy-start.30 = (f32[2,256]{1,0:T(2,128)S(1)}, f32[2,256]{1,0:T(2,128)}, u32[]{:S(2)}) copy-start(f32[2,256]{1,0:T(2,128)} %param.27) | copy-start | bytes 6148
  1649.0 135.3 %copy-start.32 = (f32[2,256]{1,0:T(2,128)S(1)}, f32[2,256]{1,0:T(2,128)}, u32[]{:S(2)}) copy-start(f32[2,256]{1,0:T(2,128)} %param.32) | copy-start | bytes 6148
  1649.0 135.3 %copy-start.33 = (f32[2,256]{1,0:T(2,128)S(1)}, f32[2,256]{1,0:T(2,128)}, u32[]{:S(2)}) copy-start(f32[2,256]{1,0:T(2,128)} %param.37) | copy-start | bytes 6148
  1784.3 550.9 %copy-start.31 = (f32[2,256]{1,0:T(2,128)}, f32[2,256]{1,0:T(2,128)S(1)}, u32[]{:S(2)}) copy-start(f32[2,256]{1,0:T(2,128)S(1)} %psum.7) | copy-start | bytes 6148
  (30 other events, 389.2 us)
Sparse Core Ops, SparseCore 0:
  10.7 63.1 all-gather.11
  76.1 33.0 all-gather.9
  130.1 45.9 all-gather.13
  178.6 48.0 all-gather.15
  234.4 70.2 reduce-scatter.12
  307.5 227.6 all-gather.19
  537.3 32.6 all-gather.17
  571.7 34.4 all-gather.23
  622.9 282.0 reduce-scatter.28
  913.7 123.9 all-gather.21
  1086.0 69.9 reduce-scatter.16
  1160.8 34.4 all-gather.25
  1259.1 76.7 reduce-scatter.18
  1350.3 72.2 reduce-scatter.20
  1427.1 87.9 reduce-scatter.24
  1518.5 118.0 reduce-scatter.22
  1639.1 70.8 reduce-scatter.14
  1714.2 63.4 reduce-scatter.30
  1782.0 542.2 reduce-scatter.26
where the time goes:
time: 2350 us; the launch traced here: 2340 us
  waiting for transfers between devices  1890 us (80%)
  matrix products  234 us (10%)
  other arithmetic  113 us (5%)
  local copies, waits for them, and re-layouts  56 us (2%)
  blocking collectives  27.9 us (1%)
    reduce_scatter x1, waiting for transfers between devices, local(): lax.psum_scatter(feed_grad_part, ('dp', 'sp'), scatter_dimension=1, tiled...  539 us
    reduce_scatter x1, waiting for transfers between devices, local(): lax.psum_scatter(down_grad_part, ('dp', 'sp'), scatter_dimension=1, tiled...  282 us
    all_gather x1, waiting for transfers between devices, local(): lax.all_gather(feed_weight.astype(jnp.bfloat16), ('dp', 'sp'), axis=1, ti...  226 us
    all_gather x1, waiting for transfers between devices, local(): lax.all_gather(down_weight.astype(jnp.bfloat16), ('dp', 'sp'), axis=1, ti...  124 us
    reduce_scatter x1, waiting for transfers between devices, local(): lax.psum_scatter(qkv_grad_part, ('dp', 'sp'), scatter_dimension=1, tiled=...  119 us
    reduce_scatter x1, waiting for transfers between devices, local(): lax.psum_scatter(grad_keyvals, 'sp', scatter_dimension=1, tiled=True)  73.4 us
    reduce_scatter x1, waiting for transfers between devices, local(): lax.psum_scatter(grad_normed_two.reshape(sequences, span_rows, model_widt...  69.8 us
    reduce_scatter x1, waiting for transfers between devices, local(): lax.psum_scatter(attn_part.reshape(sequences, span_rows, model_width), 't...  66.3 us
  transfers between devices with their start and end apart: 19, of which 18 were waited for; matrix products, arithmetic and copies ran while one was open for 9% of the time, Pallas kernels for 0%

commit v1 on v0

v1 whole, which is shorter than its diff:
```python
import functools

import jax
import jax.numpy as jnp
from jax import lax
from jax.experimental import pallas as pl
from jax.experimental.pallas import tpu as pltpu
from jax.sharding import PartitionSpec as P

HD = 64
QPK = 4
STEP = 10
LANES = 128
VMEM_LIMIT = 56 * 1024 * 1024


NORM_EPSILON = 1e-05
ROPE_BASE = 500000.0
MASKED = -1e30
BETA_ONE = 0.9
BETA_TWO = 0.95
ADAM_EPSILON = 1e-08
WEIGHT_DECAY = 0.1
QKV_RATE = 0.05
PROJ_RATE = 0.4
FEED_RATE = 0.05
DOWN_RATE = 0.03
GAIN_RATE = 0.5

BF = jnp.bfloat16
F32 = jnp.float32


def after(value, *earlier):
    return lax.optimization_barrier((value,) + earlier)[0]


def swap(value, axis, mask):
    return lax.ppermute(value, axis, [(i, i ^ mask) for i in range(lax.axis_size(axis))])


def pick(value, index, axis):
    return lax.dynamic_index_in_dim(value, index, axis, keepdims=False)


def dot(left, right, dims):
    return lax.dot_general(left, right, ((dims[0], dims[1]), ((), ())), preferred_element_type=F32)


def mm(left, right):
    return dot(left, right, ((1,), (0,)))


def mm_nt(left, right):
    return dot(left, right, ((1,), (1,)))


def mm_tn(left, right):
    return dot(left, right, ((0,), (0,)))


def turn(block, cosine, sine):
    lane = lax.broadcasted_iota(jnp.int32, block.shape, 1)
    ahead = pltpu.roll(block, LANES - HD // 2, 1)
    behind = pltpu.roll(block, HD // 2, 1)
    return block * cosine + jnp.where(lane % HD < HD // 2, ahead, behind) * sine

def key_tables(cosine, sine):
    lane = lax.broadcasted_iota(jnp.int32, cosine.shape, 1)
    return jnp.where(lane < HD, cosine, 1.0), jnp.where(lane < HD, sine, 0.0)

def attend_kernel(tile, p_ref, cos_ref, sin_ref, qkv_ref, ctx_ref, log_ref, q_s, k_s, vt_s, c_s):
    length = p_ref.shape[0]
    cosine, sine = cos_ref[...], sin_ref[...]
    for b in range(QPK // 2):
        block = turn(p_ref[:, b * LANES : (b + 1) * LANES], cosine, sine).astype(BF) * BF(HD ** -0.5)
        qkv_ref[:, b * LANES : (b + 1) * LANES] = block
        q_s[2 * b] = block[:, :HD]
        q_s[2 * b + 1] = block[:, HD:]
    k_cos, k_sin = key_tables(cosine, sine)
    block = turn(p_ref[:, QPK * HD :], k_cos, k_sin)
    qkv_ref[:, QPK * HD :] = block.astype(BF)
    k_s[...] = block[:, :HD].astype(BF)
    vt_s[...] = jnp.transpose(block)[HD:].astype(BF)
    keep = lax.broadcasted_iota(jnp.int32, (tile, tile), 0) <= lax.broadcasted_iota(jnp.int32, (tile, tile), 1)

    def head(n, carry):
        for t in range(length // tile):
            before, here = t * tile, slice(t * tile, (t + 1) * tile)
            q = q_s[n, here, :]
            s_here = jnp.where(keep, mm_nt(k_s[here, :], q), MASKED)
            peak = jnp.max(s_here, axis=0, keepdims=True)
            if t:
                s_before = mm_nt(k_s[:before, :], q)
                peak = jnp.maximum(peak, jnp.max(s_before, axis=0, keepdims=True))
            e_here = jnp.exp(s_here - peak)
            total = jnp.sum(e_here, axis=0, keepdims=True)
            if t:
                e_before = jnp.exp(s_before - peak)
                total = total + jnp.sum(e_before, axis=0, keepdims=True)
            scale = 1.0 / total
            out = mm(vt_s[:, here], (e_here * scale).astype(BF))
            if t:
                out = out + mm(vt_s[:, :before], (e_before * scale).astype(BF))
            c_s[pl.ds(pl.multiple_of(n * HD, HD), HD), here] = out
            log_ref[0, pl.ds(n, 1), here] = peak + jnp.log(total)
        return carry

    lax.fori_loop(0, QPK, head, 0)
    ctx_ref[...] = jnp.transpose(c_s[...]).astype(BF)

def attend(projected, cosine, sine, groups, tile=256):
    length, columns = projected.shape[0], projected.shape[1] // groups
    qw = QPK * HD
    table = pl.BlockSpec((length, LANES), lambda g: (0, 0))
    return pl.pallas_call(
        functools.partial(attend_kernel, tile),
        grid=(groups,),
        in_specs=[pl.BlockSpec((length, columns), lambda g: (0, g)), table, table],
        out_specs=[
            pl.BlockSpec((length, columns), lambda g: (0, g)),
            pl.BlockSpec((length, qw), lambda g: (0, g)),
            pl.BlockSpec((1, QPK, length), lambda g: (g, 0, 0)),
        ],
        out_shape=[
            jax.ShapeDtypeStruct((length, groups * columns), BF),
            jax.ShapeDtypeStruct((length, groups * qw), BF),
            jax.ShapeDtypeStruct((groups, QPK, length), F32),
        ],
        scratch_shapes=[
            pltpu.VMEM((QPK, length, HD), BF),
            pltpu.VMEM((length, HD), BF),
            pltpu.VMEM((HD, length), BF),
            pltpu.VMEM((qw, length), F32),
        ],
        compiler_params=pltpu.CompilerParams(vmem_limit_bytes=VMEM_LIMIT),
        cost_estimate=pl.CostEstimate(flops=groups * QPK * length * length * 4 * HD, bytes_accessed=length * columns * groups * 8, transcendentals=0),
        name="attend",
    )(projected, cosine, sine)

def attend_back_kernel(tile, qkv_ref, grad_ref, log_ref, cos_ref, sin_ref, out_ref, q_s, k_s, v_s, kt_s, g_s, dk_s, dv_s, dq_s):
    length = qkv_ref.shape[0]
    for b in range(QPK // 2):
        lanes = slice(b * LANES, (b + 1) * LANES)
        block, grad = qkv_ref[:, lanes], grad_ref[:, lanes]
        q_s[2 * b], q_s[2 * b + 1] = block[:, :HD], block[:, HD:]
        g_s[2 * b], g_s[2 * b + 1] = grad[:, :HD], grad[:, HD:]
    block = qkv_ref[:, QPK * HD :]
    k_s[...] = block[:, :HD]
    v_s[...] = block[:, HD:]
    kt_s[...] = jnp.transpose(block.astype(F32))[:HD].astype(BF)
    dk_s[...] = jnp.zeros_like(dk_s)
    dv_s[...] = jnp.zeros_like(dv_s)
    keep = lax.broadcasted_iota(jnp.int32, (tile, tile), 0) <= lax.broadcasted_iota(jnp.int32, (tile, tile), 1)

    def head(n, carry):
        for t in range(length // tile):
            before, here = t * tile, slice(t * tile, (t + 1) * tile)
            upto = slice(0, (t + 1) * tile)
            q, g = q_s[n, here, :], g_s[n, here, :]
            log = log_ref[0, pl.ds(n, 1), here]
            a_here = jnp.exp(jnp.where(keep, mm_nt(k_s[here, :], q), MASKED) - log)
            d_here = mm_nt(v_s[here, :], g)
            inner = jnp.sum(a_here * d_here, axis=0, keepdims=True)
            if t:
                a_before = jnp.exp(mm_nt(k_s[:before, :], q) - log)
                d_before = mm_nt(v_s[:before, :], g)
                inner = inner + jnp.sum(a_before * d_before, axis=0, keepdims=True)
            s_here = (a_here * (d_here - inner)).astype(BF)
            dq = mm(kt_s[:, here], s_here)
            dk_s[here, :] += mm(s_here, q)
            dv_s[here, :] += mm(a_here.astype(BF), g)
            if t:
                s_before = (a_before * (d_before - inner)).astype(BF)
                dq = dq + mm(kt_s[:, :before], s_before)
                dk_s[:before, :] += mm(s_before, q)
                dv_s[:before, :] += mm(a_before.astype(BF), g)
            dq_s[pl.ds(pl.multiple_of(n * HD, HD), HD), here] = dq * HD ** -0.5
        return carry

    lax.fori_loop(0, QPK, head, 0)
    cosine, sine = cos_ref[...], sin_ref[...]
    grad = jnp.transpose(dq_s[...])
    for b in range(QPK // 2):
        lanes = slice(b * LANES, (b + 1) * LANES)
        out_ref[:, lanes] = turn(grad[:, lanes], cosine, -sine).astype(BF)
    k_cos, k_sin = key_tables(cosine, sine)
    block = jnp.concatenate([dk_s[...], dv_s[...]], axis=1)
    out_ref[:, QPK * HD :] = turn(block, k_cos, -k_sin).astype(BF)

def attend_back(qkv, grad, log, cosine, sine, groups, tile=256):
    length, columns = qkv.shape[0], qkv.shape[1] // groups
    qw = QPK * HD
    table = pl.BlockSpec((length, LANES), lambda g: (0, 0))
    return pl.pallas_call(
        functools.partial(attend_back_kernel, tile),
        grid=(groups,),
        in_specs=[
            pl.BlockSpec((length, columns), lambda g: (0, g)),
            pl.BlockSpec((length, qw), lambda g: (0, g)),
            pl.BlockSpec((1, QPK, length), lambda g: (g, 0, 0)),
            table, table],
        out_specs=pl.BlockSpec((length, columns), lambda g: (0, g)),
        out_shape=jax.ShapeDtypeStruct((length, groups * columns), BF),
        scratch_shapes=[
            pltpu.VMEM((QPK, length, HD), BF),
            pltpu.VMEM((length, HD), BF),
            pltpu.VMEM((length, HD), BF),
            pltpu.VMEM((HD, length), BF),
            pltpu.VMEM((QPK, length, HD), BF),
            pltpu.VMEM((length, HD), F32),
            pltpu.VMEM((length, HD), F32),
            pltpu.VMEM((qw, length), F32),
        ],
        compiler_params=pltpu.CompilerParams(vmem_limit_bytes=VMEM_LIMIT),
        cost_estimate=pl.CostEstimate(flops=groups * QPK * length * length * 10 * HD, bytes_accessed=length * columns * groups * 8, transcendentals=0),
        name="attend_back",
    )(qkv, grad, log, cosine, sine)

def tables(length):
    half = HD // 2
    freq = ROPE_BASE ** (-(jnp.arange(half, dtype=F32) * 2.0 / HD))
    ang = jnp.arange(length).astype(F32)[:, None] * freq[None, :]
    c, s = jnp.cos(ang), jnp.sin(ang)
    return jnp.concatenate([c, c, c, c], 1), jnp.concatenate([-s, s, -s, s], 1)

def gate_kernel(n_ref, g_ref, u_ref, hid_ref, a_ref, b_ref):
    rows = n_ref[...]
    gate = mm(rows, g_ref[...])
    up = mm(rows, u_ref[...])
    s = jax.nn.sigmoid(gate)
    act = gate * s
    hid_ref[...] = (act * up).astype(BF)
    a_ref[...] = act
    b_ref[...] = up * s * (1.0 + gate * (1.0 - s))

def gate_up(rows, gate_w, up_w, tm=512, tf=256):
    m, k = rows.shape; f = gate_w.shape[1]
    o = pl.BlockSpec((tm, tf), lambda i, j: (i, j))
    return pl.pallas_call(gate_kernel, grid=(m // tm, f // tf),
        in_specs=[pl.BlockSpec((tm, k), lambda i, j: (i, 0)), pl.BlockSpec((k, tf), lambda i, j: (0, j)), pl.BlockSpec((k, tf), lambda i, j: (0, j))],
        out_specs=[o, o, o],
        out_shape=[jax.ShapeDtypeStruct((m, f), BF), jax.ShapeDtypeStruct((m, f), F32), jax.ShapeDtypeStruct((m, f), F32)],
        compiler_params=pltpu.CompilerParams(vmem_limit_bytes=VMEM_LIMIT),
        cost_estimate=pl.CostEstimate(flops=4*m*k*f, bytes_accessed=2*m*k+4*k*f+10*m*f, transcendentals=0),
        name="gate_up")(rows, gate_w, up_w)

def ffn_back_kernel(tf, dy_ref, a_ref, b_ref, d_ref, g_ref, u_ref, *refs):
    dg_ref, du_ref, dn_ref = refs[-3:]
    dy = dy_ref[...]
    for j in range(d_ref.shape[0] // tf):
        c = slice(j * tf, (j + 1) * tf)
        dh = mm_nt(dy, d_ref[c, :])
        dg_ref[:, c] = (dh * b_ref[:, c]).astype(BF)
        du_ref[:, c] = (dh * a_ref[:, c]).astype(BF)
    dn_ref[...] = (mm_nt(dg_ref[...], g_ref[...]) + mm_nt(du_ref[...], u_ref[...])).astype(BF)


def ffn_back(dy, a, b, down_w, gate_w, up_w, part, earlier, tm=256, tf=256):
    m, k = dy.shape
    f = gate_w.shape[1]
    steps = m // 2 // tm
    inner = pl.BlockSpec((tm, f), lambda i: (i + part * steps, 0))
    rows = pl.BlockSpec((tm, k), lambda i: (i + part * steps, 0))

    def whole(shape):
        return pl.BlockSpec(shape, lambda i: (0, 0), pipeline_mode=pl.Buffered(1))

    held = () if earlier is None else earlier
    return pl.pallas_call(
        functools.partial(ffn_back_kernel, tf),
        grid=(steps,),
        in_specs=[rows, inner, inner, whole((f, k)), whole((k, f)), whole((k, f))]
        + [pl.BlockSpec(memory_space=pl.ANY)] * len(held),
        out_specs=[inner, inner, pl.BlockSpec((tm, k), lambda i: (i, 0))],
        out_shape=[
            jax.ShapeDtypeStruct((m, f), BF),
            jax.ShapeDtypeStruct((m, f), BF),
            jax.ShapeDtypeStruct((m // 2, k), BF),
        ],
        input_output_aliases={6 + i: i for i in range(len(held))},
        compiler_params=pltpu.CompilerParams(vmem_limit_bytes=VMEM_LIMIT),
        cost_estimate=pl.CostEstimate(
            flops=3 * m * k * f, bytes_accessed=2 * m * k + 6 * k * f + 6 * m * f, transcendentals=0
        ),
        name="ffn_back",
    )(dy, a, b, down_w, gate_w, up_w, *held)


def adamw(param, grad, first, second, rate, decay):
    first_new = BETA_ONE * first + (1.0 - BETA_ONE) * grad
    second_new = BETA_TWO * second + (1.0 - BETA_TWO) * grad * grad
    first_hat = first_new / (1.0 - BETA_ONE**STEP)
    second_hat = second_new / (1.0 - BETA_TWO**STEP)
    param_new = param - rate * (first_hat / (jnp.sqrt(second_hat) + ADAM_EPSILON) + decay * param)
    return (param_new, first_new, second_new)


def line(value, step, direction):
    n = lax.axis_size("sp")
    if direction > 0:
        pairs = [(i, i + 1) for i in range(step - 1, n - 1)]
    else:
        pairs = [(i, i - 1) for i in range(1, n - step + 1)]
    return lax.ppermute(value, "sp", pairs)


def line_gather(value, zi):
    below, above = line(value, 1, 1), line(value, 1, -1)
    below_two, above_two = line(below, 2, 1), line(above, 2, -1)
    below_three, above_three = line(below_two, 3, 1), line(above_two, 3, -1)
    near = jnp.where(zi < 2, above, below)
    mid = jnp.where(
        zi == 0, above_two, jnp.where(zi == 1, below, jnp.where(zi == 2, above, below_two))
    )
    far = jnp.where(
        zi == 0, above_three, jnp.where(zi == 1, above_two, jnp.where(zi == 2, below_two, below_three))
    )
    mid_from = jnp.where(zi == 0, 2, jnp.where(zi == 1, 0, jnp.where(zi == 2, 3, 1)))
    pieces = [
        (value, zi),
        (near, jnp.where(zi < 2, zi + 1, zi - 1)),
        (mid, mid_from),
        (far, jnp.where(zi < 2, 3, 0)),
    ]
    return pieces, (below_two, above_two)


def direct_gather(sends, zi):
    return [(v if k == 0 else swap(v, "sp", k), zi ^ k) for k, v in sends.items()]


def fill_rows(pieces, xi, gates=()):
    nx, nz = lax.axis_size("dp"), lax.axis_size("sp")
    rows, columns = pieces[0][0].shape
    out = jnp.zeros((nx * nz * rows, columns), pieces[0][0].dtype)
    for piece, source in pieces:
        for kx in range(nx):
            got = piece if kx == 0 else swap(after(piece, *gates), "dp", kx)
            out = lax.dynamic_update_slice(out, got, (((xi ^ kx) * nz + source) * rows, 0))
    return out


def fill_units(pieces, xi, gates=()):
    nx, nz = lax.axis_size("dp"), lax.axis_size("sp")
    outer, rows, columns = pieces[0][0].shape
    out = jnp.zeros((outer, nx * nz * rows, columns), pieces[0][0].dtype)
    for piece, source in pieces:
        for kx in range(nx):
            got = piece if kx == 0 else swap(after(piece, *gates), "dp", kx)
            out = lax.dynamic_update_slice(out, got, (0, ((xi ^ kx) * nz + source) * rows, 0))
    return out.reshape(outer * nx * nz * rows, columns)


def reduce_dp(parts, xi):
    total = pick(parts, xi, 0).astype(F32)
    for k in range(1, lax.axis_size("dp")):
        total = total + swap(pick(parts, xi ^ k, 0), "dp", k).astype(F32)
    return total


def reduce_line(parts, xi, zi):
    n = lax.axis_size("sp")
    summed = reduce_dp(parts, xi).astype(BF)
    up = down = None
    for step in range(1, n):
        to_up = pick(summed, jnp.clip(n - step + zi, 0, n - 1), 0)
        to_down = pick(summed, jnp.clip(zi - n + step, 0, n - 1), 0)
        if up is not None:
            to_up = (to_up.astype(F32) + up.astype(F32)).astype(BF)
            to_down = (to_down.astype(F32) + down.astype(F32)).astype(BF)
        up = lax.ppermute(to_up, "sp", [(i, i + 1) for i in range(step)])
        down = lax.ppermute(to_down, "sp", [(i, i - 1) for i in range(n - step, n)])
    return pick(summed, zi, 0).astype(F32) + up.astype(F32) + down.astype(F32)


def reduce_half(parts, xi, zi):
    summed = reduce_dp(parts, xi).astype(BF)
    moved = {k: swap(pick(summed, zi ^ k, 0), "sp", k).astype(F32) for k in (1, 2, 3)}
    return pick(summed, zi, 0).astype(F32) + moved[2], moved[1] + moved[3]


def order_tp(pieces, ti):
    rows = pieces[0]
    out = jnp.zeros((rows.shape[0], 4) + rows.shape[1:], rows.dtype)
    for k, piece in pieces.items():
        out = lax.dynamic_update_slice(out, piece[:, None], (0, ti ^ k, 0, 0))
    return out


def gather_tp(rows, ti):
    from_y = swap(rows, "tp", 2)
    return order_tp({0: rows, 1: swap(rows, "tp", 1), 2: from_y, 3: swap(from_y, "tp", 1)}, ti)


def reduce_tp(parts, ti):
    y, c = ti // 2, ti % 2
    split = parts.reshape((parts.shape[0], 2, 2) + parts.shape[2:])
    got = swap(pick(split, 1 - c, 2), "tp", 1)
    mine = (pick(split, c, 2).astype(F32) + got.astype(F32)).astype(BF)
    return pick(mine, y, 1).astype(F32) + swap(pick(mine, 1 - y, 1), "tp", 2).astype(F32)


def gather_group(rows):
    n = rows.shape[0] // 2
    a, b = rows[:n], rows[n:]
    a_y = swap(a, "tp", 2)
    b_z = swap(b, "sp", 1)
    a_z = swap(a, "sp", 1)
    b_y = swap(b, "tp", 2)
    a_yz = swap(a_y, "sp", 1)
    b_zy = swap(b_z, "tp", 2)
    mine = [a, a_z, a_y, a_yz, b, b_y, b_z, b_zy]
    other = [swap(v, "tp", 1) for v in mine]
    return jnp.concatenate(mine + other, axis=0)


def reduce_group(mine, other):
    total = (mine.astype(F32) + swap(other, "tp", 1).astype(F32)).astype(BF)
    n = mine.shape[0] // 8
    a, b = total[: 4 * n], total[4 * n :]
    a_got = swap(a[2 * n :], "tp", 2)
    b_got = swap(b[2 * n :], "sp", 1)
    a = (a[: 2 * n].astype(F32) + a_got.astype(F32)).astype(BF)
    b = (b[: 2 * n].astype(F32) + b_got.astype(F32)).astype(BF)
    a_got = swap(a[n:], "sp", 1)
    b_got = swap(b[n:], "tp", 2)
    return jnp.concatenate(
        [a[:n].astype(F32) + a_got.astype(F32), b[:n].astype(F32) + b_got.astype(F32)], axis=0
    )


def place(pieces, index):
    out = jnp.zeros((len(pieces),) + pieces[0].shape, pieces[0].dtype)
    for mask, piece in pieces.items():
        out = lax.dynamic_update_index_in_dim(out, piece, index ^ mask, 0)
    return out


def spread(rows, zi, gates=()):
    got = {0: pick(rows, zi, 0)}
    for k in (1, 2, 3):
        got[k] = swap(after(pick(rows, zi ^ k, 0), *gates), "sp", k)
    return got


def local(
    block_in,
    cotangent,
    qkv_weight,
    proj_weight,
    feed_weight,
    down_weight,
    norm_gains,
    qkv_first,
    proj_first,
    feed_first,
    down_first,
    gains_first,
    qkv_second,
    proj_second,
    feed_second,
    down_second,
    gains_second,
):
    xi, zi, ti = lax.axis_index("dp"), lax.axis_index("sp"), lax.axis_index("tp")
    nx, nz = lax.axis_size("dp"), lax.axis_size("sp")
    half = zi % 2
    width = block_in.shape[2]
    span = block_in.shape[1]
    length = span * nz * 4
    groups, row_block, columns = qkv_weight.shape
    proj_rows = proj_weight.shape[1]
    units, unit_rows = down_weight.shape[0], down_weight.shape[1]
    feed_columns = feed_weight.shape[2] // 2

    x_pieces = spread(block_in, zi)
    x_rows = place(x_pieces, zi)
    x_from_y = place({k: swap(v, "tp", 2) for k, v in x_pieces.items()}, zi)
    x_all = order_tp(
        {0: x_rows, 1: swap(x_rows, "tp", 1), 2: x_from_y, 3: swap(x_from_y, "tp", 1)}, ti
    ).reshape(length, width)

    gains_low = norm_gains.astype(BF)
    gain_values = fill_units(
        [(v[:, None], z) for v, z in direct_gather({k: gains_low for k in range(4)}, zi)], xi
    )
    gain_values = gain_values.reshape(2, width).astype(F32)

    qkv_mine = qkv_weight.transpose(1, 0, 2).reshape(row_block, groups * columns).astype(BF)
    qkv_pieces, qkv_late = line_gather(qkv_mine, zi)
    qkv_all = fill_rows(qkv_pieces, xi)
    proj_mine = after(proj_weight.astype(BF), *qkv_late)
    proj_pieces, proj_late = line_gather(proj_mine, zi)
    proj_all = fill_units(proj_pieces, xi)

    dy_pieces = spread(cotangent, zi, qkv_late)
    dy_rows = place(dy_pieces, zi)

    def halves(value, axis, gates):
        size = value.shape[axis] // 2
        same = lax.dynamic_slice_in_dim(value, half * size, size, axis).astype(BF)
        other = lax.dynamic_slice_in_dim(value, (1 - half) * size, size, axis).astype(BF)
        same, other = lax.optimization_barrier((same, other) + tuple(gates))[:2]
        return {0: same, 1: other, 2: same, 3: other}

    gate_pieces = direct_gather(halves(feed_weight[0], 1, qkv_late), zi)
    up_pieces = direct_gather(halves(feed_weight[1], 1, (gate_pieces[2][0], gate_pieces[3][0])), zi)
    down_pieces = direct_gather(halves(down_weight, 0, (up_pieces[2][0], up_pieces[3][0])), zi)

    def norm(rows, gain):
        inverse = lax.rsqrt(jnp.mean(rows * rows, axis=-1, keepdims=True) + NORM_EPSILON)
        unit = rows * inverse
        return unit, inverse, (unit * gain).astype(BF)

    _, _, normed_one = norm(x_all.astype(F32), gain_values[0])
    projected = mm(normed_one, qkv_all)
    cosine, sine = tables(length)
    qkv, context, logs = attend(projected, cosine, sine, groups)
    attn_part = mm(context, proj_all).astype(BF).reshape(nz, 4, span, width)
    attn_mine = reduce_tp(attn_part, ti).reshape(-1, width)
    inputs = x_rows.astype(F32).reshape(-1, width)
    hidden_one = inputs + attn_mine
    unit_two, inverse_two, normed_two = norm(hidden_one, gain_values[1])

    gate_all = fill_rows(gate_pieces, xi, (projected,))
    up_all = fill_rows(up_pieces, xi, (context,))
    down_all = fill_units(down_pieces, xi, (attn_part,))
    dy_all = gather_group(after(dy_rows.reshape(-1, width), projected))

    normed_all = gather_group(normed_two)
    hidden, activated, slope = gate_up(normed_all, gate_all, up_all)
    part_rows = dy_all.shape[0] // 2
    grad_gate, grad_up, grad_other = ffn_back(
        dy_all, activated, slope, down_all, gate_all, up_all, 1, None
    )
    grad_gate, grad_up, grad_mine = ffn_back(
        dy_all, activated, slope, down_all, gate_all, up_all, 0, (grad_gate, grad_up)
    )
    grad_normed_two = reduce_group(grad_mine, grad_other)

    down_part = mm_tn(hidden, dy_all).astype(BF)
    down_part = down_part.reshape(units // 2, nx, nz, unit_rows, width).transpose(1, 2, 0, 3, 4)
    down_same, down_other = reduce_half(down_part, xi, zi)
    gate_part = mm_tn(normed_all, grad_gate).astype(BF)
    gate_part = gate_part.reshape(nx, nz, row_block, feed_columns)
    gate_same, gate_other = reduce_half(gate_part, xi, zi)
    up_part = mm_tn(normed_all, grad_up).astype(BF).reshape(nx, nz, row_block, feed_columns)
    up_same, up_other = reduce_half(up_part, xi, zi)
    out_part = mm(hidden, down_all).astype(BF)
    ffn_mine = reduce_group(out_part[:part_rows], out_part[part_rows:])

    grad_unit = grad_normed_two * gain_values[1]
    row_inner = jnp.mean(grad_unit * unit_two, axis=-1, keepdims=True)
    dy_own = dy_rows.astype(F32).reshape(-1, width)
    back_two = inverse_two * (grad_unit - unit_two * row_inner)
    gain_two_part = jnp.sum(grad_normed_two * unit_two, axis=0)
    grad_hidden_one = dy_own + back_two
    grad_rows = gather_tp(grad_hidden_one.astype(BF).reshape(nz, span, width), ti)
    grad_rows = grad_rows.reshape(length, width)
    grad_context = mm_nt(grad_rows, proj_all).astype(BF)
    proj_part = mm_tn(context, grad_rows).astype(BF).reshape(groups, nx, nz, proj_rows, width)
    proj_grad = reduce_line(proj_part.transpose(1, 2, 0, 3, 4), xi, zi)
    grad_projected = attend_back(qkv, grad_context, logs, cosine, sine, groups)

    grad_normed_one = mm_nt(grad_projected, qkv_all).astype(BF).reshape(nz, 4, span, width)
    grad_normed_one = reduce_tp(grad_normed_one, ti).reshape(-1, width)
    qkv_part = mm_tn(normed_one, grad_projected).astype(BF)
    qkv_part = qkv_part.reshape(nx, nz, row_block, groups * columns)
    qkv_grad = reduce_line(qkv_part, xi, zi)
    qkv_grad = qkv_grad.reshape(row_block, groups, columns).transpose(1, 0, 2)

    inverse_one = lax.rsqrt(jnp.mean(inputs * inputs, axis=-1, keepdims=True) + NORM_EPSILON)
    unit_one = inputs * inverse_one
    grad_unit = grad_normed_one * gain_values[0]
    row_inner = jnp.mean(grad_unit * unit_one, axis=-1, keepdims=True)
    back_one = inverse_one * (grad_unit - unit_one * row_inner)
    gain_one_part = jnp.sum(grad_normed_one * unit_one, axis=0)

    block_delta = (attn_mine + ffn_mine).astype(BF).reshape(nz, span, width)
    input_delta = (back_two + back_one).astype(BF).reshape(nz, span, width)
    block_out = block_in.astype(F32) + place(spread(block_delta, zi), zi).astype(F32)
    input_grad = cotangent.astype(F32) + place(spread(input_delta, zi), zi).astype(F32)

    gains_part = jnp.stack([gain_one_part, gain_two_part])
    gains_part = gains_part + swap(gains_part, "tp", 1)
    gains_part = gains_part + swap(gains_part, "tp", 2)
    gains_part = gains_part.reshape(2, nx, nz, row_block).transpose(1, 2, 0, 3)
    gains_sum = pick(gains_part, xi, 0)
    for k in range(1, nx):
        gains_sum = gains_sum + swap(pick(gains_part, xi ^ k, 0), "dp", k)
    gains_grad = pick(gains_sum, zi, 0)
    for k in (1, 2, 3):
        gains_grad = gains_grad + swap(pick(gains_sum, zi ^ k, 0), "sp", k)

    def join(same, other, axis):
        low = jnp.where(half == 0, same, other)
        high = jnp.where(half == 0, other, same)
        return jnp.concatenate([low, high], axis=axis)

    feed_grad = jnp.stack([join(gate_same, gate_other, 1), join(up_same, up_other, 1)])
    down_grad = join(down_same, down_other, 0)

    qkv_new, qkv_first_new, qkv_second_new = adamw(
        qkv_weight, qkv_grad, qkv_first, qkv_second, QKV_RATE, WEIGHT_DECAY
    )
    proj_new, proj_first_new, proj_second_new = adamw(
        proj_weight, proj_grad, proj_first, proj_second, PROJ_RATE, WEIGHT_DECAY
    )
    feed_new, feed_first_new, feed_second_new = adamw(
        feed_weight, feed_grad, feed_first, feed_second, FEED_RATE, WEIGHT_DECAY
    )
    down_new, down_first_new, down_second_new = adamw(
        down_weight, down_grad, down_first, down_second, DOWN_RATE, WEIGHT_DECAY
    )
    gains_new, gains_first_new, gains_second_new = adamw(
        norm_gains, gains_grad, gains_first, gains_second, GAIN_RATE, 0.0
    )
    return (
        block_out,
        input_grad,
        qkv_grad,
        proj_grad,
        feed_grad,
        down_grad,
        gains_grad,
        qkv_new,
        proj_new,
        feed_new,
        down_new,
        gains_new,
        qkv_first_new,
        proj_first_new,
        feed_first_new,
        down_first_new,
        gains_first_new,
        qkv_second_new,
        proj_second_new,
        feed_second_new,
        down_second_new,
        gains_second_new,
    )


def solution(mesh):
    rows = P("dp", ("sp", "tp"), None)
    heads = P("tp", ("dp", "sp"), None)
    feed = P(None, ("dp", "sp"), "tp")
    gains = P(None, ("dp", "sp"))
    params = (heads, heads, feed, heads, gains)
    return jax.shard_map(
        local,
        mesh=mesh,
        in_specs=(rows, rows) + params * 3,
        out_specs=(rows, rows) + params * 4,
        check_vma=False,
    )
```

time: 2350 us -> 1060 us (0.45)
  waiting for transfers between devices: 1890 us -> 435 us
  starting transfers between devices: 2.6 us -> 224 us
  matrix products: 234 us -> 76.5 us
  Pallas kernels: 0 us -> 125 us
  local copies, waits for them, and re-layouts: 56 us -> 104 us
  other arithmetic: 113 us -> 81.4 us
  blocking collectives: 27.9 us -> 0 us
    reduce_scatter x9 -> x0, waiting for transfers between devices: 1280 us -> none  [the longest x1 539 us: local(): lax.psum_scatter(feed_grad_part, ('dp', 'sp'), scatter_dimension=1, tiled...]
    all_gather x9 -> x0, waiting for transfers between devices: 546 us -> none  [the longest x1 226 us: local(): lax.all_gather(feed_weight.astype(jnp.bfloat16), ('dp', 'sp'), axis=1, ti...]
    ppermute x0 -> x143, waiting for transfers between devices: none -> 435 us  [the longest x119 416 us: swap(): lax.ppermute(value, axis, [(i, i ^ mask) for i in range(lax.axis_size(axi...]
    ppermute x0 -> x143, starting transfers between devices: none -> 224 us  [the longest x119 166 us: swap(): lax.ppermute(value, axis, [(i, i ^ mask) for i in range(lax.axis_size(axi...]
    dot_general x43 -> x10, matrix products: 234 us -> 76.5 us  [dot(): lax.dot_general(left, right, ((dims[0], dims[1]), ((), ())), preferred_el...]
    pallas_call x0 -> x5, Pallas kernels: none -> 125 us  [the longest x2 41.9 us: ffn_back(): pl.pallas_call(functools.partial(ffn_back_kernel, tf), grid=(steps,), in_...]
    unnamed x20 -> x0, waiting for transfers between devices: 62.4 us -> none
    another operation x4 -> x2, other arithmetic: 26.5 us -> 0.28 us  [local(): jnp.stack([join(gate_same, gate_other, 1), join(up_same, up_other, 1)])]
  transfers between devices with their start and end apart: 19 -> 143, of which waited for: 18 -> 52; matrix products, arithmetic and copies ran while one was open for 9% -> 22% of each run, Pallas kernels for 0% -> 9%
where the time goes in v1:
time: 1060 us; the launch traced here: 1050 us
  waiting for transfers between devices  435 us (41%)
  starting transfers between devices  224 us (21%)
  Pallas kernels  125 us (12%)
  local copies, waits for them, and re-layouts  104 us (10%)
  other arithmetic  81.4 us (8%)
  matrix products  76.5 us (7%)
    ppermute x119, waiting for transfers between devices, swap(): lax.ppermute(value, axis, [(i, i ^ mask) for i in range(lax.axis_size(axi...  416 us
    ppermute x119, starting transfers between devices, swap(): lax.ppermute(value, axis, [(i, i ^ mask) for i in range(lax.axis_size(axi...  166 us
    dot_general x10, matrix products, dot(): lax.dot_general(left, right, ((dims[0], dims[1]), ((), ())), preferred_el...  76.5 us
    unnamed x192, local copies, waits for them, and re-layouts  46.9 us
    pallas_call x2, Pallas kernels, ffn_back(): pl.pallas_call(functools.partial(ffn_back_kernel, tf), grid=(steps,), in_...  41.9 us
    pallas_call x1, Pallas kernels, gate_up(): pl.pallas_call(gate_kernel, grid=(m // tm, f // tf), in_specs=[pl.BlockSp...  33 us
    ppermute x6, starting transfers between devices, reduce_line(): up = lax.ppermute(to_up, 'sp', [(i, i + 1) for i in range(step)])  29.7 us
    pallas_call x1, Pallas kernels, attend_back(): pl.pallas_call(functools.partial(attend_back_kernel, tile), grid=(groups,...  28.9 us
  transfers between devices with their start and end apart: 143, of which 52 were waited for; matrix products, arithmetic and copies ran while one was open for 22% of the time, Pallas kernels for 9%

profile of v1, /device:TPU:0, one launch (start us, length us, event | category | flops | bytes accessed | tf_op | source)
XLA Modules:
  0.0 1049.6 jit_solution(9520941643838337077)
XLA Ops:
  62.4 13.5 %collective-permute-done.1 = bf16[64,2048]{1,0:T(8,128)(2,1)S(1)} collective-permute-done((bf16[64,2048]{1,0:T(8,128)(2,1)}, bf16[64,2048]{1,0:T(8,128)(2,1)S(1)}, u32[]{:S(2)}, u32[]{:S(2)}) %collective-permute-start.1) | collective-permute-done | bytes 262176 | tf_op jit(solution)/shard_map/ppermute | solution.py:39
  133.6 29.2 %collective-permute-done.82 = bf16[64,2048]{1,0:T(8,128)(2,1)S(1)} collective-permute-done((bf16[64,2048]{1,0:T(8,128)(2,1)S(1)}, bf16[64,2048]{1,0:T(8,128)(2,1)S(1)}, u32[]{:S(2)}, u32[]{:S(2)}) %collective-permute-start.82) | collective-permute-done | bytes 262176 | tf_op jit(solution)/shard_map/ppermute | solution.py:39
  185.4 10.9 %collective-permute-start.62 = (bf16[256,1024]{1,0:T(8,128)(2,1)S(1)}, bf16[256,1024]{1,0:T(8,128)(2,1)}, u32[]{:S(2)}, u32[]{:S(2)}) collective-permute-start(bf16[256,1024]{1,0:T(8,128)(2,1)S(1)} %copy-done.47), channel_id=1, source_target_pairs={{0,8},{4,12},{8,0},{12,4},{1,9},{5,13},{9,1},{13,5},{2,10},{6,14},... | collective-permute-start | bytes 1572872 | tf_op jit(solution)/shard_map/ppermute | solution.py:39
  225.2 21.4 %attend.1 = (bf16[1024,768]{1,0:T(8,128)(2,1)}, bf16[1024,512]{1,0:T(8,128)(2,1)}, f32[2,4,1024]{2,1,0:T(4,128)}) custom-call(f32[1024,768]{1,0:T(8,128)} %fusion.72.p_ref, f32[1024,128]{1,0:T(8,128)} %get-tuple-element.258.cos_ref, f32[1024,128]{1,0:T(8,128)} %get-tuple-element.259.sin_ref), custom_call_target="tpu_custom_call" | custom-call | flops 2147483648 | bytes 6291456 | tf_op jit(solution)/shard_map/attend/pallas_call | solution.py:116
  262.9 10.1 collective-permute-done.52
  273.0 10.6 %collective-permute-start.69 = (bf16[4,32,2048]{2,1,0:T(8,128)(2,1)S(1)}, bf16[4,32,2048]{2,1,0:T(8,128)(2,1)S(1)}, u32[]{:S(2)}, u32[]{:S(2)}) collective-permute-start(bf16[4,32,2048]{2,1,0:T(8,128)(2,1)S(1)} %copy-done.48), channel_id=1, source_target_pairs={{0,8},{4,12},{8,0},{12,4},{1,9},{5,13},{9,1},{13,5},{2,10},{6,14},... | collective-permute-start | bytes 1572872 | tf_op jit(solution)/shard_map/ppermute | solution.py:39
  286.9 8.6 collective-permute-done.56
  306.8 11.2 %collective-permute-done.61 = bf16[256,1024]{1,0:T(8,128)(2,1)S(1)} collective-permute-done((bf16[256,1024]{1,0:T(8,128)(2,1)}, bf16[256,1024]{1,0:T(8,128)(2,1)S(1)}, u32[]{:S(2)}, u32[]{:S(2)}) %collective-permute-start.61) | collective-permute-done | bytes 524320 | tf_op jit(solution)/shard_map/ppermute | solution.py:39
  317.9 10.1 collective-permute-start.71
  367.5 12.2 %collective-permute-done.68 = bf16[4,32,2048]{2,1,0:T(8,128)(2,1)S(1)} collective-permute-done((bf16[4,32,2048]{2,1,0:T(8,128)(2,1)S(1)}, bf16[4,32,2048]{2,1,0:T(8,128)(2,1)S(1)}, u32[]{:S(2)}, u32[]{:S(2)}) %collective-permute-start.68) | collective-permute-done | bytes 524320 | tf_op jit(solution)/shard_map/ppermute | solution.py:39
  382.5 8.4 collective-permute-done.70
  392.6 9.2 collective-permute-done.72
  402.5 12.8 %collective-permute-done.37 = bf16[4,64,2048]{2,1,0:T(8,128)(2,1)S(1)} collective-permute-done((bf16[4,64,2048]{2,1,0:T(8,128)(2,1)S(1)}, bf16[4,64,2048]{2,1,0:T(8,128)(2,1)S(1)}, u32[]{:S(2)}, u32[]{:S(2)}) %collective-permute-start.37) | collective-permute-done | bytes 1048608 | tf_op jit(solution)/shard_map/ppermute | solution.py:39
  437.7 9.5 collective-permute-done.42
  475.4 33.0 %gate_up.1 = (bf16[2048,1024]{1,0:T(8,128)(2,1)}, f32[2048,1024]{1,0:T(8,128)}, f32[2048,1024]{1,0:T(8,128)}) custom-call(bf16[2048,2048]{1,0:T(8,128)(2,1)} %constant_dynamic-update-slice_fusion.n_ref, bf16[2048,1024]{1,0:T(8,128)(2,1)} %copy-done.29, bf16[2048,1024]{1,0:T(8,128)(2,1)} %copy-done.24), custom_call_target="tpu_custom_call" | custom-call | flops 17179869184 | bytes 37748736 | tf_op jit(solution)/shard_map/gate_up/pallas_call | solution.py:240
  508.3 12.8 %convolution_convert_fusion.1 = bf16[1024,2048]{1,0:T(8,128)(2,1)S(1)} fusion(bf16[2048,1024]{1,0:T(8,128)(2,1)} %get-tuple-element.71, bf16[2048,2048]{1,0:T(8,128)(2,1)} %constant_dynamic-update-slice_fusion.16.dy_ref), kind=kOutput, calls=%fused_computation.22 | convolution fusion | flops 8592031744 | bytes 16777216 | tf_op jit(solution)/shard_map/dot_general | solution.py:47
  524.5 20.8 %ffn_back.2 = (bf16[2048,1024]{1,0:T(8,128)(2,1)}, bf16[2048,1024]{1,0:T(8,128)(2,1)}, bf16[1024,2048]{1,0:T(8,128)(2,1)}) custom-call(bf16[2048,2048]{1,0:T(8,128)(2,1)} %constant_dynamic-update-slice_fusion.16.dy_ref, f32[2048,1024]{1,0:T(8,128)} %get-tuple-element.82.a_ref, f32[2048,1024]{1,0:T(8,128)} %get-tuple-element.83.b_ref, ...), custom_call_target="tpu_custom_call" | custom-call | flops 12884901888 | bytes 33554432 | tf_op jit(solution)/shard_map/ffn_back/pallas_call | solution.py:270
  545.3 21.0 %ffn_back.3 = (bf16[2048,1024]{1,0:T(8,128)(2,1)}, bf16[2048,1024]{1,0:T(8,128)(2,1)}, bf16[1024,2048]{1,0:T(8,128)(2,1)}) custom-call(bf16[2048,2048]{1,0:T(8,128)(2,1)} %constant_dynamic-update-slice_fusion.16.dy_ref, f32[2048,1024]{1,0:T(8,128)} %get-tuple-element.82.a_ref, ...), custom_call_target="tpu_custom_call", output_to_operand_aliasing={{0}: (6, {}), {1}: (7, {})} | custom-call | flops 12884901888 | bytes 33554432 | tf_op jit(solution)/shard_map/ffn_back/pallas_call | solution.py:270
  566.3 12.9 %convolution_convert_fusion.5 = bf16[2048,1024]{1,0:T(8,128)(2,1)S(1)} fusion(bf16[2048,2048]{1,0:T(8,128)(2,1)} %constant_dynamic-update-slice_fusion.n_ref, bf16[2048,1024]{1,0:T(8,128)(2,1)} %get-tuple-element.90), kind=kOutput, calls=%fused_computation.26 | convolution fusion | flops 8592031744 | bytes 16777216 | tf_op jit(solution)/shard_map/dot_general | solution.py:47
  581.4 11.5 %convolution_convert_fusion.4 = bf16[2048,1024]{1,0:T(8,128)(2,1)S(1)} fusion(bf16[2048,2048]{1,0:T(8,128)(2,1)} %constant_dynamic-update-slice_fusion.n_ref, bf16[2048,1024]{1,0:T(8,128)(2,1)S(1)} %copy-done.73), kind=kOutput, calls=%fused_computation.25 | convolution fusion | flops 8592031744 | bytes 16777216 | tf_op jit(solution)/shard_map/dot_general | solution.py:47
  595.9 11.0 %convolution_convert_fusion = bf16[2048,2048]{1,0:T(8,128)(2,1)S(1)} fusion(bf16[2048,1024]{1,0:T(8,128)(2,1)} %get-tuple-element.71, bf16[1024,2048]{1,0:T(8,128)(2,1)S(1)} %bitcast.348), kind=kOutput, calls=%fused_computation.6 | convolution fusion | flops 8594128896 | bytes 16777216 | tf_op jit(solution)/shard_map/dot_general | solution.py:47
  611.4 16.7 %collective-permute-done.125 = bf16[4,256,1024]{2,1,0:T(8,128)(2,1)} collective-permute-done((bf16[4,256,1024]{2,1,0:T(8,128)(2,1)S(1)}, bf16[4,256,1024]{2,1,0:T(8,128)(2,1)}, u32[]{:S(2)}, u32[]{:S(2)}) %collective-permute-start.125) | collective-permute-done | bytes 2097184 | tf_op jit(solution)/shard_map/ppermute | solution.py:39
  634.5 37.2 %collective-permute-done.129 = bf16[4,256,1024]{2,1,0:T(8,128)(2,1)} collective-permute-done((bf16[4,256,1024]{2,1,0:T(8,128)(2,1)}, bf16[4,256,1024]{2,1,0:T(8,128)(2,1)}, u32[]{:S(2)}, u32[]{:S(2)}) %collective-permute-start.129) | collective-permute-done | bytes 2097184 | tf_op jit(solution)/shard_map/ppermute | solution.py:39
  680.0 8.6 collective-permute-done.128
  689.8 50.2 %collective-permute-done.130 = bf16[256,1024]{1,0:T(8,128)(2,1)S(1)} collective-permute-done((bf16[256,1024]{1,0:T(8,128)(2,1)S(1)}, bf16[256,1024]{1,0:T(8,128)(2,1)S(1)}, u32[]{:S(2)}, u32[]{:S(2)}) %collective-permute-start.130) | collective-permute-done | bytes 524320 | tf_op jit(solution)/shard_map/ppermute | solution.py:39
  745.0 10.2 multiply_subtract_fusion
  760.9 22.9 %collective-permute-start.101 = (bf16[256,2048]{1,0:T(8,128)(2,1)S(1)}, bf16[256,2048]{1,0:T(8,128)(2,1)S(1)}, u32[]{:S(2)}, u32[]{:S(2)}) collective-permute-start(bf16[256,2048]{1,0:T(8,128)(2,1)S(1)} %get-tuple-element.184), channel_id=1, source_target_pairs={{0,4},{4,0},{8,12},{12,8},{1,5},{5,1},{9,13},{13,9},{2,6},{6,2},{1... | collective-permute-start | bytes 3145736 | tf_op jit(solution)/shard_map/ppermute | solution.py:39
  792.0 15.9 %collective-permute-done.101 = bf16[256,2048]{1,0:T(8,128)(2,1)S(1)} collective-permute-done((bf16[256,2048]{1,0:T(8,128)(2,1)S(1)}, bf16[256,2048]{1,0:T(8,128)(2,1)S(1)}, u32[]{:S(2)}, u32[]{:S(2)}) %collective-permute-start.101) | collective-permute-done | bytes 1048608 | tf_op jit(solution)/shard_map/ppermute | solution.py:39
  813.3 19.0 %collective-permute-done.74 = bf16[256,2048]{1,0:T(8,128)(2,1)S(1)} collective-permute-done((bf16[256,2048]{1,0:T(8,128)(2,1)S(1)}, bf16[256,2048]{1,0:T(8,128)(2,1)S(1)}, u32[]{:S(2)}, u32[]{:S(2)}) %collective-permute-start.74) | collective-permute-done | bytes 1048608 | tf_op jit(solution)/shard_map/ppermute | solution.py:39
  864.7 17.9 %collective-permute-done.79 = bf16[64,2048]{1,0:T(8,128)(2,1)S(1)} collective-permute-done((bf16[64,2048]{1,0:T(8,128)(2,1)S(1)}, bf16[64,2048]{1,0:T(8,128)(2,1)S(1)}, u32[]{:S(2)}, u32[]{:S(2)}) %collective-permute-start.79) | collective-permute-done | bytes 262176 | tf_op jit(solution)/shard_map/ppermute | solution.py:39
  893.6 28.9 %attend_back.1 = bf16[1024,768]{1,0:T(8,128)(2,1)} custom-call(bf16[1024,768]{1,0:T(8,128)(2,1)} %get-tuple-element.88.qkv_ref, bf16[1024,512]{1,0:T(8,128)(2,1)} %convolution_convert_fusion.8.grad_ref, f32[2,4,1024]{2,1,0:T(4,128)} %get-tuple-element.89.log_ref, f32[1024,128]{1,0:T(8,128)} %get-tuple-element.258.cos_ref, f32[1024,128]{1,0:T(8,128)} %get-tuple-element.259.sin_ref), custom_call_target="tpu_custom_call" | custom-call | flops 5368709120 | bytes 6291456 | tf_op jit(solution)/shard_map/attend_back/pallas_call | solution.py:195
  1005.6 9.8 collective-permute-done.107
  (647 shorter events, 508.2 us)
Async XLA Ops:
  2.3 86.2 %collective-permute-start.17 = (bf16[256,768]{0,1:T(8,128)(2,1)S(1)}, bf16[256,768]{0,1:T(8,128)(2,1)}, u32[]{:S(2)}, u32[]{:S(2)}) collective-permute-start(bf16[256,768]{0,1:T(8,128)(2,1)S(1)} %bitcast.355), channel_id=1, source_target_pairs={{4,0},{8,4},{12,8},{5,1},{9,5},{13,9},{6,2},{10,6},{14,10},{7,3},{... | collective-permute-start | bytes 1179656 | tf_op jit(solution)/shard_map/ppermute | solution.py:305
  3.6 84.9 %collective-permute-start.18 = (bf16[256,768]{0,1:T(8,128)(2,1)S(1)}, bf16[256,768]{0,1:T(8,128)(2,1)}, u32[]{:S(2)}, u32[]{:S(2)}) collective-permute-start(bf16[256,768]{0,1:T(8,128)(2,1)S(1)} %bitcast.356), channel_id=1, source_target_pairs={{0,4},{4,8},{8,12},{1,5},{5,9},{9,13},{2,6},{6,10},{10,14},{3,7},{... | collective-permute-start | bytes 1179656 | tf_op jit(solution)/shard_map/ppermute | solution.py:305
  45.2 41.8 %collective-permute-start.16 = (bf16[256,768]{0,1:T(8,128)(2,1)S(1)}, bf16[256,768]{0,1:T(8,128)(2,1)S(1)}, u32[]{:S(2)}, u32[]{:S(2)}) collective-permute-start(bf16[256,768]{0,1:T(8,128)(2,1)S(1)} %bitcast.358), channel_id=1, source_target_pairs={{0,16},{16,0},{1,17},{17,1},{2,18},{18,2},{3,19},{19,3},{4,20},{20... | collective-permute-start | bytes 1179656 | tf_op jit(solution)/shard_map/ppermute | solution.py:39
  109.6 55.3 %collective-permute-start.22 = (bf16[256,768]{0,1:T(8,128)(2,1)S(1)}, bf16[256,768]{0,1:T(8,128)(2,1)S(1)}, u32[]{:S(2)}, u32[]{:S(2)}) collective-permute-start(bf16[256,768]{0,1:T(8,128)(2,1)S(1)} %get-tuple-element.172), channel_id=1, source_target_pairs={{0,16},{16,0},{1,17},{17,1},{2,18},{18,2},{3,19},{19,3},{4,20},{20... | collective-permute-start | bytes 1179656 | tf_op jit(solution)/shard_map/ppermute | solution.py:39
  111.6 65.0 %collective-permute-start.55 = (bf16[256,1024]{1,0:T(8,128)(2,1)S(1)}, bf16[256,1024]{1,0:T(8,128)(2,1)S(1)}, u32[]{:S(2)}, u32[]{:S(2)}) collective-permute-start(bf16[256,1024]{1,0:T(8,128)(2,1)S(1)} %copy-done.46), channel_id=1, source_target_pairs={{0,8},{4,12},{8,0},{12,4},{1,9},{5,13},{9,1},{13,5},{2,10},{6,14},... | collective-permute-start | bytes 1572872 | tf_op jit(solution)/shard_map/ppermute | solution.py:39
  125.5 38.7 %collective-permute-start.83 = (bf16[64,2048]{1,0:T(8,128)(2,1)S(1)}, bf16[64,2048]{1,0:T(8,128)(2,1)S(1)}, u32[]{:S(2)}, u32[]{:S(2)}) collective-permute-start(bf16[64,2048]{1,0:T(8,128)(2,1)S(1)} %copy-done.59), channel_id=1, source_target_pairs={{0,12},{4,8},{8,4},{12,0},{1,13},{5,9},{9,5},{13,1},{2,14},{6,10},... | collective-permute-start | bytes 786440 | tf_op jit(solution)/shard_map/ppermute | solution.py:39
  131.9 46.5 %collective-permute-start.57 = (bf16[256,1024]{1,0:T(8,128)(2,1)}, bf16[256,1024]{1,0:T(8,128)(2,1)}, u32[]{:S(2)}, u32[]{:S(2)}) collective-permute-start(bf16[256,1024]{1,0:T(8,128)(2,1)} %get-tuple-element.61), channel_id=1, source_target_pairs={{0,12},{4,8},{8,4},{12,0},{1,13},{5,9},{9,5},{13,1},{2,14},{6,10},... | collective-permute-start | bytes 1572872 | tf_op jit(solution)/shard_map/ppermute | solution.py:39
  179.8 66.9 %collective-permute-start.53 = (bf16[256,1024]{1,0:T(8,128)(2,1)}, bf16[256,1024]{1,0:T(8,128)(2,1)}, u32[]{:S(2)}, u32[]{:S(2)}) collective-permute-start(bf16[256,1024]{1,0:T(8,128)(2,1)} %get-tuple-element.61), channel_id=1, source_target_pairs={{0,4},{4,0},{8,12},{12,8},{1,5},{5,1},{9,13},{13,9},{2,6},{6,2},{1... | collective-permute-start | bytes 1572872 | tf_op jit(solution)/shard_map/ppermute | solution.py:39
  185.4 67.0 %collective-permute-start.62 = (bf16[256,1024]{1,0:T(8,128)(2,1)S(1)}, bf16[256,1024]{1,0:T(8,128)(2,1)}, u32[]{:S(2)}, u32[]{:S(2)}) collective-permute-start(bf16[256,1024]{1,0:T(8,128)(2,1)S(1)} %copy-done.47), channel_id=1, source_target_pairs={{0,8},{4,12},{8,0},{12,4},{1,9},{5,13},{9,1},{13,5},{2,10},{6,14},... | collective-permute-start | bytes 1572872 | tf_op jit(solution)/shard_map/ppermute | solution.py:39
  252.3 44.3 %collective-permute-start.85 = (bf16[128,2048]{1,0:T(8,128)(2,1)S(1)}, bf16[128,2048]{1,0:T(8,128)(2,1)S(1)}, u32[]{:S(2)}, u32[]{:S(2)}) collective-permute-start(bf16[128,2048]{1,0:T(8,128)(2,1)S(1)} %get-tuple-element.229), channel_id=1, source_target_pairs={{0,2},{1,3},{2,0},{3,1},{4,6},{5,7},{6,4},{7,5},{8,10},{9,11},{10,... | collective-permute-start | bytes 1572872 | tf_op jit(solution)/shard_map/ppermute | solution.py:39
  261.8 44.9 %collective-permute-start.58 = (bf16[256,1024]{1,0:T(8,128)(2,1)}, bf16[256,1024]{1,0:T(8,128)(2,1)S(1)}, u32[]{:S(2)}, u32[]{:S(2)}) collective-permute-start(bf16[256,1024]{1,0:T(8,128)(2,1)} %collective-permute-done.57), channel_id=1, source_target_pairs={{0,16},{16,0},{1,17},{17,1},{2,18},{18,2},{3,19},{19,3},{4,20},{20... | collective-permute-start | bytes 1572872 | tf_op jit(solution)/shard_map/ppermute | solution.py:39
  273.0 69.1 %collective-permute-start.69 = (bf16[4,32,2048]{2,1,0:T(8,128)(2,1)S(1)}, bf16[4,32,2048]{2,1,0:T(8,128)(2,1)S(1)}, u32[]{:S(2)}, u32[]{:S(2)}) collective-permute-start(bf16[4,32,2048]{2,1,0:T(8,128)(2,1)S(1)} %copy-done.48), channel_id=1, source_target_pairs={{0,8},{4,12},{8,0},{12,4},{1,9},{5,13},{9,1},{13,5},{2,10},{6,14},... | collective-permute-start | bytes 1572872 | tf_op jit(solution)/shard_map/ppermute | solution.py:39
  347.1 55.4 %collective-permute-start.94 = (bf16[128,2048]{1,0:T(8,128)(2,1)S(1)}, bf16[128,2048]{1,0:T(8,128)(2,1)S(1)}, u32[]{:S(2)}, u32[]{:S(2)}) collective-permute-start(bf16[128,2048]{1,0:T(8,128)(2,1)S(1)} %get-tuple-element.227), channel_id=1, source_target_pairs={{0,1},{1,0},{2,3},{3,2},{4,5},{5,4},{6,7},{7,6},{8,9},{9,8},{10,11... | collective-permute-start | bytes 1572872 | tf_op jit(solution)/shard_map/ppermute | solution.py:39
  366.7 52.5 %collective-permute-start.95 = (bf16[128,2048]{1,0:T(8,128)(2,1)}, bf16[128,2048]{1,0:T(8,128)(2,1)}, u32[]{:S(2)}, u32[]{:S(2)}) collective-permute-start(bf16[128,2048]{1,0:T(8,128)(2,1)} %collective-permute-done.87), channel_id=1, source_target_pairs={{0,1},{1,0},{2,3},{3,2},{4,5},{5,4},{6,7},{7,6},{8,9},{9,8},{10,11... | collective-permute-start | bytes 1572872 | tf_op jit(solution)/shard_map/ppermute | solution.py:39
  427.4 40.0 %collective-permute-start.44 = (bf16[128,2048]{1,0:T(8,128)(2,1)S(1)}, bf16[128,2048]{1,0:T(8,128)(2,1)S(1)}, u32[]{:S(2)}, u32[]{:S(2)}) collective-permute-start(bf16[128,2048]{1,0:T(8,128)(2,1)S(1)} %get-tuple-element.244), channel_id=1, source_target_pairs={{0,1},{1,0},{2,3},{3,2},{4,5},{5,4},{6,7},{7,6},{8,9},{9,8},{10,11... | collective-permute-start | bytes 1572872 | tf_op jit(solution)/shard_map/ppermute | solution.py:39
  523.3 107.6 %collective-permute-start.133 = (bf16[4,4,32,2048]{3,2,1,0:T(8,128)(2,1)}, bf16[4,4,32,2048]{3,2,1,0:T(8,128)(2,1)}, u32[]{:S(2)}, u32[]{:S(2)}) collective-permute-start(bf16[4,4,32,2048]{3,2,1,0:T(8,128)(2,1)} %bitcast.325), channel_id=1, source_target_pairs={{0,16},{16,0},{1,17},{17,1},{2,18},{18,2},{3,19},{19,3},{4,20},{20... | collective-permute-start | bytes 6291464 | tf_op jit(solution)/shard_map/ppermute | solution.py:39
  579.4 48.7 %collective-permute-start.125 = (bf16[4,256,1024]{2,1,0:T(8,128)(2,1)S(1)}, bf16[4,256,1024]{2,1,0:T(8,128)(2,1)}, u32[]{:S(2)}, u32[]{:S(2)}) collective-permute-start(bf16[4,256,1024]{2,1,0:T(8,128)(2,1)S(1)} %dynamic-slice_bitcast_fusion.1), channel_id=1, source_target_pairs={{0,16},{16,0},{1,17},{17,1},{2,18},{18,2},{3,19},{19,3},{4,20},{20... | collective-permute-start | bytes 6291464 | tf_op jit(solution)/shard_map/ppermute | solution.py:39
  594.5 77.3 %collective-permute-start.129 = (bf16[4,256,1024]{2,1,0:T(8,128)(2,1)}, bf16[4,256,1024]{2,1,0:T(8,128)(2,1)}, u32[]{:S(2)}, u32[]{:S(2)}) collective-permute-start(bf16[4,256,1024]{2,1,0:T(8,128)(2,1)} %dynamic-slice_bitcast_fusion), channel_id=1, source_target_pairs={{0,16},{16,0},{1,17},{17,1},{2,18},{18,2},{3,19},{19,3},{4,20},{20... | collective-permute-start | bytes 6291464 | tf_op jit(solution)/shard_map/ppermute | solution.py:39
  606.9 148.3 %collective-permute-start.98 = (bf16[1024,2048]{1,0:T(8,128)(2,1)}, bf16[1024,2048]{1,0:T(8,128)(2,1)}, u32[]{:S(2)}, u32[]{:S(2)}) collective-permute-start(bf16[1024,2048]{1,0:T(8,128)(2,1)} %get-tuple-element.87), channel_id=1, source_target_pairs={{0,1},{1,0},{2,3},{3,2},{4,5},{5,4},{6,7},{7,6},{8,9},{9,8},{10,11... | collective-permute-start | bytes 12582920 | tf_op jit(solution)/shard_map/ppermute | solution.py:39
  611.4 172.4 %collective-permute-start.73 = (bf16[1024,2048]{1,0:T(8,128)(2,1)}, bf16[1024,2048]{1,0:T(8,128)(2,1)}, u32[]{:S(2)}, u32[]{:S(2)}) collective-permute-start(bf16[1024,2048]{1,0:T(8,128)(2,1)} %slice.125), channel_id=1, source_target_pairs={{0,1},{1,0},{2,3},{3,2},{4,5},{5,4},{6,7},{7,6},{8,9},{9,8},{10,11... | collective-permute-start | bytes 12582920 | tf_op jit(solution)/shard_map/ppermute | solution.py:39
  630.8 45.5 %collective-permute-start.126 = (bf16[256,1024]{1,0:T(8,128)(2,1)S(1)}, bf16[256,1024]{1,0:T(8,128)(2,1)S(1)}, u32[]{:S(2)}, u32[]{:S(2)}) collective-permute-start(bf16[256,1024]{1,0:T(8,128)(2,1)S(1)} %get-tuple-element.204), channel_id=1, source_target_pairs={{0,8},{4,12},{8,0},{12,4},{1,9},{5,13},{9,1},{13,5},{2,10},{6,14},... | collective-permute-start | bytes 1572872 | tf_op jit(solution)/shard_map/ppermute | solution.py:39
  630.9 46.8 %collective-permute-start.127 = (bf16[256,1024]{1,0:T(8,128)(2,1)S(1)}, bf16[256,1024]{1,0:T(8,128)(2,1)S(1)}, u32[]{:S(2)}, u32[]{:S(2)}) collective-permute-start(bf16[256,1024]{1,0:T(8,128)(2,1)S(1)} %get-tuple-element.206), channel_id=1, source_target_pairs={{0,4},{4,0},{8,12},{12,8},{1,5},{5,1},{9,13},{13,9},{2,6},{6,2},{1... | collective-permute-start | bytes 1572872 | tf_op jit(solution)/shard_map/ppermute | solution.py:39
  676.3 63.8 %collective-permute-start.130 = (bf16[256,1024]{1,0:T(8,128)(2,1)S(1)}, bf16[256,1024]{1,0:T(8,128)(2,1)S(1)}, u32[]{:S(2)}, u32[]{:S(2)}) collective-permute-start(bf16[256,1024]{1,0:T(8,128)(2,1)S(1)} %get-tuple-element.207), channel_id=1, source_target_pairs={{0,8},{4,12},{8,0},{12,4},{1,9},{5,13},{9,1},{13,5},{2,10},{6,14},... | collective-permute-start | bytes 1572872 | tf_op jit(solution)/shard_map/ppermute | solution.py:39
  677.7 62.4 %collective-permute-start.131 = (bf16[256,1024]{1,0:T(8,128)(2,1)S(1)}, bf16[256,1024]{1,0:T(8,128)(2,1)S(1)}, u32[]{:S(2)}, u32[]{:S(2)}) collective-permute-start(bf16[256,1024]{1,0:T(8,128)(2,1)S(1)} %get-tuple-element.209), channel_id=1, source_target_pairs={{0,4},{4,0},{8,12},{12,8},{1,5},{5,1},{9,13},{13,9},{2,6},{6,2},{1... | collective-permute-start | bytes 1572872 | tf_op jit(solution)/shard_map/ppermute | solution.py:39
  688.5 51.5 %collective-permute-start.132 = (bf16[256,1024]{1,0:T(8,128)(2,1)S(1)}, bf16[256,1024]{1,0:T(8,128)(2,1)S(1)}, u32[]{:S(2)}, u32[]{:S(2)}) collective-permute-start(bf16[256,1024]{1,0:T(8,128)(2,1)S(1)} %get-tuple-element.208), channel_id=1, source_target_pairs={{0,12},{4,8},{8,4},{12,0},{1,13},{5,9},{9,5},{13,1},{2,14},{6,10},... | collective-permute-start | bytes 1572872 | tf_op jit(solution)/shard_map/ppermute | solution.py:39
  740.1 49.0 %collective-permute-start.134 = (bf16[4,32,2048]{2,1,0:T(8,128)(2,1)}, bf16[4,32,2048]{2,1,0:T(8,128)(2,1)}, u32[]{:S(2)}, u32[]{:S(2)}) collective-permute-start(bf16[4,32,2048]{2,1,0:T(8,128)(2,1)} %get-tuple-element.201), channel_id=1, source_target_pairs={{0,8},{4,12},{8,0},{12,4},{1,9},{5,13},{9,1},{13,5},{2,10},{6,14},... | collective-permute-start | bytes 1572872 | tf_op jit(solution)/shard_map/ppermute | solution.py:39
  740.1 50.1 %collective-permute-start.135 = (bf16[4,32,2048]{2,1,0:T(8,128)(2,1)}, bf16[4,32,2048]{2,1,0:T(8,128)(2,1)}, u32[]{:S(2)}, u32[]{:S(2)}) collective-permute-start(bf16[4,32,2048]{2,1,0:T(8,128)(2,1)} %get-tuple-element.203), channel_id=1, source_target_pairs={{0,4},{4,0},{8,12},{12,8},{1,5},{5,1},{9,13},{13,9},{2,6},{6,2},{1... | collective-permute-start | bytes 1572872 | tf_op jit(solution)/shard_map/ppermute | solution.py:39
  740.1 50.2 %collective-permute-start.136 = (bf16[4,32,2048]{2,1,0:T(8,128)(2,1)S(1)}, bf16[4,32,2048]{2,1,0:T(8,128)(2,1)}, u32[]{:S(2)}, u32[]{:S(2)}) collective-permute-start(bf16[4,32,2048]{2,1,0:T(8,128)(2,1)S(1)} %get-tuple-element.202), channel_id=1, source_target_pairs={{0,12},{4,8},{8,4},{12,0},{1,13},{5,9},{9,5},{13,1},{2,14},{6,10},... | collective-permute-start | bytes 1572872 | tf_op jit(solution)/shard_map/ppermute | solution.py:39
  760.9 46.9 %collective-permute-start.101 = (bf16[256,2048]{1,0:T(8,128)(2,1)S(1)}, bf16[256,2048]{1,0:T(8,128)(2,1)S(1)}, u32[]{:S(2)}, u32[]{:S(2)}) collective-permute-start(bf16[256,2048]{1,0:T(8,128)(2,1)S(1)} %get-tuple-element.184), channel_id=1, source_target_pairs={{0,4},{4,0},{8,12},{12,8},{1,5},{5,1},{9,13},{13,9},{2,6},{6,2},{1... | collective-permute-start | bytes 3145736 | tf_op jit(solution)/shard_map/ppermute | solution.py:39
  789.1 43.3 %collective-permute-start.74 = (bf16[256,2048]{1,0:T(8,128)(2,1)S(1)}, bf16[256,2048]{1,0:T(8,128)(2,1)S(1)}, u32[]{:S(2)}, u32[]{:S(2)}) collective-permute-start(bf16[256,2048]{1,0:T(8,128)(2,1)S(1)} %get-tuple-element.187), channel_id=1, source_target_pairs={{0,2},{1,3},{2,0},{3,1},{4,6},{5,7},{6,4},{7,5},{8,10},{9,11},{10,... | collective-permute-start | bytes 3145736 | tf_op jit(solution)/shard_map/ppermute | solution.py:39
  790.2 42.2 %collective-permute-start.76 = (bf16[256,2048]{1,0:T(8,128)(2,1)S(1)}, bf16[256,2048]{1,0:T(8,128)(2,1)S(1)}, u32[]{:S(2)}, u32[]{:S(2)}) collective-permute-start(bf16[256,2048]{1,0:T(8,128)(2,1)S(1)} %get-tuple-element.188), channel_id=1, source_target_pairs={{0,4},{4,0},{8,12},{12,8},{1,5},{5,1},{9,13},{13,9},{2,6},{6,2},{1... | collective-permute-start | bytes 3145736 | tf_op jit(solution)/shard_map/ppermute | solution.py:39
  893.6 46.9 %collective-permute-start.118 = (bf16[4,2,32,2048]{3,2,1,0:T(8,128)(2,1)}, bf16[4,2,32,2048]{3,2,1,0:T(8,128)(2,1)}, u32[]{:S(2)}, u32[]{:S(2)}) collective-permute-start(bf16[4,2,32,2048]{3,2,1,0:T(8,128)(2,1)} %bitcast.328), channel_id=1, source_target_pairs={{0,16},{16,0},{1,17},{17,1},{2,18},{18,2},{3,19},{19,3},{4,20},{20... | collective-permute-start | bytes 3145736 | tf_op jit(solution)/shard_map/ppermute | solution.py:39
  (188 other events, 4121.0 us)

commit v2 on v1

v2 whole, which is shorter than its diff:
```python
import functools

import jax
import jax.numpy as jnp
from jax import lax
from jax.experimental import pallas as pl
from jax.experimental.pallas import tpu as pltpu
from jax.sharding import Mesh, PartitionSpec as P

HD = 64
QPK = 4
STEP = 10
LANES = 128
VMEM_LIMIT = 56 * 1024 * 1024
SP = ("sp_pair", "sp_in_pair")


NORM_EPSILON = 1e-05
ROPE_BASE = 500000.0
MASKED = -1e30
BETA_ONE = 0.9
BETA_TWO = 0.95
ADAM_EPSILON = 1e-08
WEIGHT_DECAY = 0.1
QKV_RATE = 0.05
PROJ_RATE = 0.4
FEED_RATE = 0.05
DOWN_RATE = 0.03
GAIN_RATE = 0.5

BF = jnp.bfloat16
F32 = jnp.float32
HEAVY = pl.CostEstimate(flops=1 << 36, bytes_accessed=1 << 20, transcendentals=0)
LIGHT = pl.CostEstimate(flops=1 << 32, bytes_accessed=1 << 20, transcendentals=0)


def after(value, *earlier):
    return lax.optimization_barrier((value,) + earlier)[0]


def swap(value, axis, mask):
    return lax.ppermute(value, axis, [(i, i ^ mask) for i in range(lax.axis_size(axis))])


def pick(value, index, axis):
    return lax.dynamic_index_in_dim(value, index, axis, keepdims=False)


def dot(left, right, dims):
    return lax.dot_general(left, right, ((dims[0], dims[1]), ((), ())), preferred_element_type=F32)


def mm(left, right):
    return dot(left, right, ((1,), (0,)))


def mm_nt(left, right):
    return dot(left, right, ((1,), (1,)))


def mm_tn(left, right):
    return dot(left, right, ((0,), (0,)))


def turn(block, cosine, sine):
    lane = lax.broadcasted_iota(jnp.int32, block.shape, 1)
    ahead = pltpu.roll(block, LANES - HD // 2, 1)
    behind = pltpu.roll(block, HD // 2, 1)
    return block * cosine + jnp.where(lane % HD < HD // 2, ahead, behind) * sine

def key_tables(cosine, sine):
    lane = lax.broadcasted_iota(jnp.int32, cosine.shape, 1)
    return jnp.where(lane < HD, cosine, 1.0), jnp.where(lane < HD, sine, 0.0)

def attend_kernel(tile, p_ref, cos_ref, sin_ref, qkv_ref, ctx_ref, log_ref, q_s, k_s, vt_s, c_s):
    length = p_ref.shape[0]
    cosine, sine = cos_ref[...], sin_ref[...]
    for b in range(QPK // 2):
        block = turn(p_ref[:, b * LANES : (b + 1) * LANES], cosine, sine).astype(BF) * BF(HD ** -0.5)
        qkv_ref[:, b * LANES : (b + 1) * LANES] = block
        q_s[2 * b] = block[:, :HD]
        q_s[2 * b + 1] = block[:, HD:]
    k_cos, k_sin = key_tables(cosine, sine)
    block = turn(p_ref[:, QPK * HD :], k_cos, k_sin)
    qkv_ref[:, QPK * HD :] = block.astype(BF)
    k_s[...] = block[:, :HD].astype(BF)
    vt_s[...] = jnp.transpose(block)[HD:].astype(BF)
    keep = lax.broadcasted_iota(jnp.int32, (tile, tile), 0) <= lax.broadcasted_iota(jnp.int32, (tile, tile), 1)

    def head(n, carry):
        for t in range(length // tile):
            before, here = t * tile, slice(t * tile, (t + 1) * tile)
            q = q_s[n, here, :]
            s_here = jnp.where(keep, mm_nt(k_s[here, :], q), MASKED)
            peak = jnp.max(s_here, axis=0, keepdims=True)
            if t:
                s_before = mm_nt(k_s[:before, :], q)
                peak = jnp.maximum(peak, jnp.max(s_before, axis=0, keepdims=True))
            e_here = jnp.exp(s_here - peak)
            total = jnp.sum(e_here, axis=0, keepdims=True)
            if t:
                e_before = jnp.exp(s_before - peak)
                total = total + jnp.sum(e_before, axis=0, keepdims=True)
            scale = 1.0 / total
            out = mm(vt_s[:, here], (e_here * scale).astype(BF))
            if t:
                out = out + mm(vt_s[:, :before], (e_before * scale).astype(BF))
            c_s[pl.ds(pl.multiple_of(n * HD, HD), HD), here] = out
            log_ref[0, pl.ds(n, 1), here] = peak + jnp.log(total)
        return carry

    lax.fori_loop(0, QPK, head, 0)
    ctx_ref[...] = jnp.transpose(c_s[...]).astype(BF)

def attend(projected, cosine, sine, groups, tile=256):
    length, columns = projected.shape[0], projected.shape[1] // groups
    qw = QPK * HD
    table = pl.BlockSpec((length, LANES), lambda g: (0, 0))
    return pl.pallas_call(
        functools.partial(attend_kernel, tile),
        grid=(groups,),
        in_specs=[pl.BlockSpec((length, columns), lambda g: (0, g)), table, table],
        out_specs=[
            pl.BlockSpec((length, columns), lambda g: (0, g)),
            pl.BlockSpec((length, qw), lambda g: (0, g)),
            pl.BlockSpec((1, QPK, length), lambda g: (g, 0, 0)),
        ],
        out_shape=[
            jax.ShapeDtypeStruct((length, groups * columns), BF),
            jax.ShapeDtypeStruct((length, groups * qw), BF),
            jax.ShapeDtypeStruct((groups, QPK, length), F32),
        ],
        scratch_shapes=[
            pltpu.VMEM((QPK, length, HD), BF),
            pltpu.VMEM((length, HD), BF),
            pltpu.VMEM((HD, length), BF),
            pltpu.VMEM((qw, length), F32),
        ],
        compiler_params=pltpu.CompilerParams(vmem_limit_bytes=VMEM_LIMIT),
        cost_estimate=HEAVY,
        name="attend",
    )(projected, cosine, sine)

def attend_back_kernel(tile, qkv_ref, grad_ref, log_ref, cos_ref, sin_ref, out_ref, q_s, k_s, v_s, kt_s, g_s, dk_s, dv_s, dq_s):
    length = qkv_ref.shape[0]
    for b in range(QPK // 2):
        lanes = slice(b * LANES, (b + 1) * LANES)
        block, grad = qkv_ref[:, lanes], grad_ref[:, lanes]
        q_s[2 * b], q_s[2 * b + 1] = block[:, :HD], block[:, HD:]
        g_s[2 * b], g_s[2 * b + 1] = grad[:, :HD], grad[:, HD:]
    block = qkv_ref[:, QPK * HD :]
    k_s[...] = block[:, :HD]
    v_s[...] = block[:, HD:]
    kt_s[...] = jnp.transpose(block.astype(F32))[:HD].astype(BF)
    dk_s[...] = jnp.zeros_like(dk_s)
    dv_s[...] = jnp.zeros_like(dv_s)
    keep = lax.broadcasted_iota(jnp.int32, (tile, tile), 0) <= lax.broadcasted_iota(jnp.int32, (tile, tile), 1)

    def head(n, carry):
        for t in range(length // tile):
            before, here = t * tile, slice(t * tile, (t + 1) * tile)
            upto = slice(0, (t + 1) * tile)
            q, g = q_s[n, here, :], g_s[n, here, :]
            log = log_ref[0, pl.ds(n, 1), here]
            a_here = jnp.exp(jnp.where(keep, mm_nt(k_s[here, :], q), MASKED) - log)
            d_here = mm_nt(v_s[here, :], g)
            inner = jnp.sum(a_here * d_here, axis=0, keepdims=True)
            if t:
                a_before = jnp.exp(mm_nt(k_s[:before, :], q) - log)
                d_before = mm_nt(v_s[:before, :], g)
                inner = inner + jnp.sum(a_before * d_before, axis=0, keepdims=True)
            s_here = (a_here * (d_here - inner)).astype(BF)
            dq = mm(kt_s[:, here], s_here)
            dk_s[here, :] += mm(s_here, q)
            dv_s[here, :] += mm(a_here.astype(BF), g)
            if t:
                s_before = (a_before * (d_before - inner)).astype(BF)
                dq = dq + mm(kt_s[:, :before], s_before)
                dk_s[:before, :] += mm(s_before, q)
                dv_s[:before, :] += mm(a_before.astype(BF), g)
            dq_s[pl.ds(pl.multiple_of(n * HD, HD), HD), here] = dq * HD ** -0.5
        return carry

    lax.fori_loop(0, QPK, head, 0)
    cosine, sine = cos_ref[...], sin_ref[...]
    grad = jnp.transpose(dq_s[...])
    for b in range(QPK // 2):
        lanes = slice(b * LANES, (b + 1) * LANES)
        out_ref[:, lanes] = turn(grad[:, lanes], cosine, -sine).astype(BF)
    k_cos, k_sin = key_tables(cosine, sine)
    block = jnp.concatenate([dk_s[...], dv_s[...]], axis=1)
    out_ref[:, QPK * HD :] = turn(block, k_cos, -k_sin).astype(BF)

def attend_back(qkv, grad, log, cosine, sine, groups, tile=256):
    length, columns = qkv.shape[0], qkv.shape[1] // groups
    qw = QPK * HD
    table = pl.BlockSpec((length, LANES), lambda g: (0, 0))
    return pl.pallas_call(
        functools.partial(attend_back_kernel, tile),
        grid=(groups,),
        in_specs=[
            pl.BlockSpec((length, columns), lambda g: (0, g)),
            pl.BlockSpec((length, qw), lambda g: (0, g)),
            pl.BlockSpec((1, QPK, length), lambda g: (g, 0, 0)),
            table, table],
        out_specs=pl.BlockSpec((length, columns), lambda g: (0, g)),
        out_shape=jax.ShapeDtypeStruct((length, groups * columns), BF),
        scratch_shapes=[
            pltpu.VMEM((QPK, length, HD), BF),
            pltpu.VMEM((length, HD), BF),
            pltpu.VMEM((length, HD), BF),
            pltpu.VMEM((HD, length), BF),
            pltpu.VMEM((QPK, length, HD), BF),
            pltpu.VMEM((length, HD), F32),
            pltpu.VMEM((length, HD), F32),
            pltpu.VMEM((qw, length), F32),
        ],
        compiler_params=pltpu.CompilerParams(vmem_limit_bytes=VMEM_LIMIT),
        cost_estimate=HEAVY,
        name="attend_back",
    )(qkv, grad, log, cosine, sine)

def tables(length):
    half = HD // 2
    freq = ROPE_BASE ** (-(jnp.arange(half, dtype=F32) * 2.0 / HD))
    ang = jnp.arange(length).astype(F32)[:, None] * freq[None, :]
    c, s = jnp.cos(ang), jnp.sin(ang)
    return jnp.concatenate([c, c, c, c], 1), jnp.concatenate([-s, s, -s, s], 1)

def by_parts(at_ref, rows_ref, weights):
    depth = weights[0].shape[0]
    total = None
    for k, weight in enumerate(weights):
        rows = rows_ref[:, pl.ds(pl.multiple_of(at_ref[k] * depth, depth), depth)]
        part = mm(rows, weight[...])
        total = part if total is None else total + part
    return total


def gate_kernel(blocks, at_ref, *refs):
    rows_refs, weights, (gate_ref, rows_ref) = refs[:blocks], refs[blocks:-2], refs[-2:]

    @pl.when(pl.program_id(1) == 0)
    def _():
        for t in range(blocks):

            @pl.when(pl.program_id(0) == t)
            def _():
                rows_ref[...] = rows_refs[t][...]

    gate_ref[...] = by_parts(at_ref, rows_ref, weights)


def gate_rows(at, rows, gates, tf=512):
    tm, k = rows[0].shape
    f = gates[0].shape[1]
    parts, blocks = len(gates), len(rows)
    return pl.pallas_call(
        functools.partial(gate_kernel, blocks),
        grid=(blocks, f // tf),
        in_specs=[pl.BlockSpec(memory_space=pltpu.SMEM)]
        + [pl.BlockSpec((tm, k), lambda i, j: (0, 0), pipeline_mode=pl.Buffered(1))] * blocks
        + [pl.BlockSpec((k // parts, tf), lambda i, j: (0, j))] * parts,
        out_specs=[
            pl.BlockSpec((tm, tf), lambda i, j: (i, j)),
            pl.BlockSpec((tm, k), lambda i, j: (i, 0)),
        ],
        out_shape=[
            jax.ShapeDtypeStruct((tm * blocks, f), F32),
            jax.ShapeDtypeStruct((tm * blocks, k), BF),
        ],
        compiler_params=pltpu.CompilerParams(vmem_limit_bytes=VMEM_LIMIT),
        cost_estimate=HEAVY,
        name="gate_rows",
    )(at, *rows, *gates)


def up_kernel(at_ref, rows_ref, gate_ref, *refs):
    weights, (hid_ref, a_ref, b_ref) = refs[:-3], refs[-3:]
    up = by_parts(at_ref, rows_ref, weights)
    gate = gate_ref[...]
    s = jax.nn.sigmoid(gate)
    act = gate * s
    hid_ref[...] = (act * up).astype(BF)
    a_ref[...] = act
    b_ref[...] = up * s * (1.0 + gate * (1.0 - s))


def up_rows(at, rows, gate, ups, tm=512, tf=512):
    m, k = rows.shape
    f = gate.shape[1]
    parts = len(ups)
    o = pl.BlockSpec((tm, tf), lambda i, j: (i, j))
    return pl.pallas_call(
        up_kernel,
        grid=(m // tm, f // tf),
        in_specs=[
            pl.BlockSpec(memory_space=pltpu.SMEM),
            pl.BlockSpec((tm, k), lambda i, j: (i, 0)),
            o,
        ]
        + [pl.BlockSpec((k // parts, tf), lambda i, j: (0, j))] * parts,
        out_specs=[o, o, o],
        out_shape=[
            jax.ShapeDtypeStruct((m, f), BF),
            jax.ShapeDtypeStruct((m, f), F32),
            jax.ShapeDtypeStruct((m, f), F32),
        ],
        compiler_params=pltpu.CompilerParams(vmem_limit_bytes=VMEM_LIMIT),
        cost_estimate=HEAVY,
        name="up_rows",
    )(at, rows, gate, *ups)


def ffn_back_kernel(tf, parts, at_ref, dy_ref, a_ref, b_ref, d_ref, *refs):
    weights, (dg_ref, du_ref, dn_ref) = refs[: 2 * parts], refs[-3:]
    dy = dy_ref[...]
    for j in range(d_ref.shape[0] // tf):
        c = slice(j * tf, (j + 1) * tf)
        dh = mm_nt(dy, d_ref[c, :])
        dg_ref[:, c] = (dh * b_ref[:, c]).astype(BF)
        du_ref[:, c] = (dh * a_ref[:, c]).astype(BF)
    depth = weights[0].shape[0]
    for k in range(parts):
        part = mm_nt(dg_ref[...], weights[k][...]) + mm_nt(du_ref[...], weights[parts + k][...])
        dn_ref[:, pl.ds(pl.multiple_of(at_ref[k] * depth, depth), depth)] = part.astype(BF)


def ffn_back(at, dy, a, b, down_w, gates, ups, part, earlier, tm=256, tf=256):
    m, k = dy.shape
    f = gates[0].shape[1]
    parts = len(gates)
    steps = m // 2 // tm
    inner = pl.BlockSpec((tm, f), lambda i: (i + part * steps, 0))
    rows = pl.BlockSpec((tm, k), lambda i: (i + part * steps, 0))

    def whole(shape):
        return pl.BlockSpec(shape, lambda i: (0, 0), pipeline_mode=pl.Buffered(1))

    held = () if earlier is None else earlier
    return pl.pallas_call(
        functools.partial(ffn_back_kernel, tf, parts),
        grid=(steps,),
        in_specs=[pl.BlockSpec(memory_space=pltpu.SMEM), rows, inner, inner, whole((f, k))]
        + [whole((k // parts, f))] * (2 * parts)
        + [pl.BlockSpec(memory_space=pl.ANY)] * len(held),
        out_specs=[inner, inner, pl.BlockSpec((tm, k), lambda i: (i, 0))],
        out_shape=[
            jax.ShapeDtypeStruct((m, f), BF),
            jax.ShapeDtypeStruct((m, f), BF),
            jax.ShapeDtypeStruct((m // 2, k), BF),
        ],
        input_output_aliases={5 + 2 * parts + i: i for i in range(len(held))},
        compiler_params=pltpu.CompilerParams(vmem_limit_bytes=VMEM_LIMIT),
        cost_estimate=HEAVY,
        name="ffn_back",
    )(at, dy, a, b, down_w, *gates, *ups, *held)


def project_kernel(pieces, at_ref, *refs):
    piece_refs, (gain_ref, w_ref, n_ref, p_ref, x_s) = refs[:pieces], refs[pieces:]
    rows = piece_refs[0].shape[1]
    for k in range(pieces):
        x_s[pl.ds(pl.multiple_of(at_ref[k] * rows, rows), rows), :] = piece_refs[k][0]
    x = x_s[...].astype(F32)
    inverse = lax.rsqrt(jnp.mean(x * x, axis=-1, keepdims=True) + NORM_EPSILON)
    n_ref[...] = (x * inverse * gain_ref[...]).astype(BF)
    p_ref[...] = mm(n_ref[...], w_ref[...])


def project(at, pieces, gain, weights):
    b, r, d = pieces[0].shape
    c = weights.shape[1]
    rows = r * len(pieces)
    return pl.pallas_call(
        functools.partial(project_kernel, len(pieces)),
        grid=(b,),
        in_specs=[pl.BlockSpec(memory_space=pltpu.SMEM)]
        + [pl.BlockSpec((1, r, d), lambda i: (i, 0, 0))] * len(pieces)
        + [
            pl.BlockSpec((1, d), lambda i: (0, 0)),
            pl.BlockSpec((d, c), lambda i: (0, 0), pipeline_mode=pl.Buffered(1)),
        ],
        out_specs=[pl.BlockSpec((rows, d), lambda i: (i, 0)), pl.BlockSpec((rows, c), lambda i: (i, 0))],
        out_shape=[jax.ShapeDtypeStruct((b * rows, d), BF), jax.ShapeDtypeStruct((b * rows, c), F32)],
        scratch_shapes=[pltpu.VMEM((rows, d), BF)],
        compiler_params=pltpu.CompilerParams(vmem_limit_bytes=VMEM_LIMIT),
        cost_estimate=LIGHT,
        name="project",
    )(at, *pieces, gain, weights)


def context_kernel(pieces, at_ref, *refs):
    piece_refs, (w_ref, rows_ref, c_ref) = refs[:pieces], refs[pieces:]
    rows = piece_refs[0].shape[1]
    for k in range(pieces):
        rows_ref[pl.ds(pl.multiple_of(at_ref[k] * rows, rows), rows), :] = piece_refs[k][0]
    c_ref[...] = mm_nt(rows_ref[...], w_ref[...]).astype(BF)


def context_grad(at, pieces, weights):
    b, r, d = pieces[0].shape
    c = weights.shape[0]
    rows = r * len(pieces)
    return pl.pallas_call(
        functools.partial(context_kernel, len(pieces)),
        grid=(b,),
        in_specs=[pl.BlockSpec(memory_space=pltpu.SMEM)]
        + [pl.BlockSpec((1, r, d), lambda i: (i, 0, 0))] * len(pieces)
        + [pl.BlockSpec((c, d), lambda i: (0, 0), pipeline_mode=pl.Buffered(1))],
        out_specs=[pl.BlockSpec((rows, d), lambda i: (i, 0)), pl.BlockSpec((rows, c), lambda i: (i, 0))],
        out_shape=[jax.ShapeDtypeStruct((b * rows, d), BF), jax.ShapeDtypeStruct((b * rows, c), BF)],
        compiler_params=pltpu.CompilerParams(vmem_limit_bytes=VMEM_LIMIT),
        cost_estimate=LIGHT,
        name="context_grad",
    )(at, *pieces, weights)


def collect_kernel(put, parts, at_ref, *refs):
    for k in range(parts):
        put(refs[k], refs[parts], at_ref[k])


def collect(at, pieces, shape, put):
    return pl.pallas_call(
        functools.partial(collect_kernel, put, len(pieces)),
        in_specs=[pl.BlockSpec(memory_space=pltpu.SMEM)]
        + [pl.BlockSpec(memory_space=pltpu.VMEM)] * len(pieces),
        out_specs=pl.BlockSpec(memory_space=pltpu.VMEM),
        out_shape=jax.ShapeDtypeStruct(shape, pieces[0].dtype),
        compiler_params=pltpu.CompilerParams(vmem_limit_bytes=VMEM_LIMIT),
        name="collect",
    )(at, *pieces)


def fence_kernel(x_ref, o_ref):
    o_ref[...] = x_ref[...]


def fence_call(value):
    return pl.pallas_call(
        fence_kernel,
        out_shape=jax.ShapeDtypeStruct(value.shape, value.dtype),
        cost_estimate=HEAVY,
        name="fence",
    )(value)


def adamw(param, grad, first, second, rate, decay):
    first_new = BETA_ONE * first + (1.0 - BETA_ONE) * grad
    second_new = BETA_TWO * second + (1.0 - BETA_TWO) * grad * grad
    first_hat = first_new / (1.0 - BETA_ONE**STEP)
    second_hat = second_new / (1.0 - BETA_TWO**STEP)
    param_new = param - rate * (first_hat / (jnp.sqrt(second_hat) + ADAM_EPSILON) + decay * param)
    return (param_new, first_new, second_new)


class Chain:
    def __init__(self):
        self.token = None
        self.begun = []

    def now(self, value):
        return value if self.token is None else after(value, self.token)

    def take(self, value):
        value = self.now(value)
        self.begun.append(value)
        return value

    def start(self, value, axis, mask, name):
        value = self.take(value)
        with jax.named_scope(name):
            return swap(value, axis, mask)

    def start_dp(self, value, name):
        return [self.start(value, "dp", k, name) for k in range(1, lax.axis_size("dp"))]

    def start_all(self, blocks, name):
        blocks = self.take(blocks)
        with jax.named_scope(name):
            return lax.all_to_all(blocks, SP, 0, 0, tiled=True)

    def fence(self, *values):
        seed = self.token
        if seed is None or seed.shape != (8, LANES):
            seed = jnp.zeros((8, LANES), F32) if seed is None else after(jnp.zeros((8, LANES), F32), seed)
        self.passed(fence_call(after(seed, *self.begun, *values)))

    def passed(self, token):
        self.token = token
        self.begun = []

    def gate(self, value):
        return after(value, *self.begun) if self.begun else value


def order_units(pieces, at, sp):
    _, outer, rows, width = pieces[0].shape
    if rows % 16:
        out = jnp.zeros((outer, len(pieces), sp * rows, width), BF)
        for k, piece in enumerate(pieces):
            piece = piece.transpose(1, 0, 2, 3).reshape(outer, 1, sp * rows, width)
            out = lax.dynamic_update_slice(out, piece, (0, at[k], 0, 0))
        return out.reshape(-1, width)

    def put(piece, out, x):
        for z in range(sp):
            out[:, x, z * rows : (z + 1) * rows] = piece[z]

    return collect(at, pieces, (outer, len(pieces), sp * rows, width), put).reshape(-1, width)


def place(pieces, index):
    out = jnp.zeros((len(pieces),) + pieces[0].shape, pieces[0].dtype)
    for mask, piece in pieces.items():
        out = lax.dynamic_update_index_in_dim(out, piece, index ^ mask, 0)
    return out


class Gather:
    def __init__(self, chain, rows, name):
        self.chain = chain
        self.name = name
        n = rows.shape[0] // 2
        self.a, self.b, self.n = rows[:n], rows[n:], n
        self.a_y = chain.start(self.a, "tp", 2, name)
        self.b_z = chain.start(self.b, SP, 1, name)

    def second(self):
        now, n = self.chain.now, self.n
        self.near = jnp.concatenate([self.a, now(self.a_y), self.b, now(self.b_z)], axis=0)
        self.far_z = self.chain.start(self.near[: 2 * n], SP, 1, self.name)
        self.far_y = self.chain.start(self.near[2 * n :], "tp", 2, self.name)

    def near_core(self):
        self.near_other = self.chain.start(self.near, "tp", 1, self.name)

    def far_core(self):
        now = self.chain.now
        self.far = jnp.concatenate([now(self.far_z), now(self.far_y)], axis=0)
        self.far_other = self.chain.start(self.far, "tp", 1, self.name)

    def result(self):
        now = self.chain.now
        return [self.near, self.far, now(self.near_other), now(self.far_other)]


class Reduce:
    def __init__(self, chain, other, name):
        self.chain = chain
        self.name = name
        self.got = chain.start(other, "tp", 1, name)

    def first(self, mine):
        total = (mine.astype(F32) + self.chain.now(self.got).astype(F32)).astype(BF)
        total = total.reshape(2, 2, 2, -1, total.shape[-1])
        self.a, self.b = (total[0, 0, 0], total[1, 0, 0]), (total[0, 1, 0], total[1, 1, 0])
        self.a_y = self.chain.start(total[:, 0, 1], "tp", 2, self.name)
        self.b_z = self.chain.start(total[:, 1, 1], SP, 1, self.name)

    def second(self):
        a_y, b_z = self.chain.now(self.a_y).astype(F32), self.chain.now(self.b_z).astype(F32)
        self.a_sum = self.a[0].astype(F32) + a_y[0]
        self.b_sum = self.b[0].astype(F32) + b_z[0]
        self.a_z = self.chain.start((self.a[1].astype(F32) + a_y[1]).astype(BF), SP, 1, self.name)
        self.b_y = self.chain.start((self.b[1].astype(F32) + b_z[1]).astype(BF), "tp", 2, self.name)

    def result(self):
        a = self.a_sum + self.chain.now(self.a_z).astype(F32)
        b = self.b_sum + self.chain.now(self.b_y).astype(F32)
        return jnp.concatenate([a, b], axis=0)


def local(
    block_in,
    cotangent,
    qkv_weight,
    proj_weight,
    feed_weight,
    down_weight,
    norm_gains,
    qkv_first,
    proj_first,
    feed_first,
    down_first,
    gains_first,
    qkv_second,
    proj_second,
    feed_second,
    down_second,
    gains_second,
):
    xi, zi, ti = lax.axis_index("dp"), lax.axis_index(SP), lax.axis_index("tp")
    nx, nz = lax.axis_size("dp"), lax.axis_size(SP)
    width = block_in.shape[2]
    span = block_in.shape[1]
    length = span * nz * 4
    groups, row_block, columns = qkv_weight.shape
    proj_rows = proj_weight.shape[1]
    units, unit_rows = down_weight.shape[0], down_weight.shape[1]
    feed_columns = feed_weight.shape[2] // 2

    y, c = ti // 2, ti % 2
    chain = Chain()
    now, start, fence = chain.now, chain.start, chain.fence

    at = jnp.stack([xi ^ k for k in range(nx)])

    at_tp = jnp.stack([ti ^ k for k in range(4)])

    x_rows = chain.start_all(block_in, "x_sp")
    qkv_mine = qkv_weight.transpose(1, 0, 2).reshape(row_block, groups * columns).astype(BF)
    qkv_all = lax.all_gather(qkv_mine, ("dp",) + SP, tiled=True)
    fence(qkv_mine)

    gains_low = now(norm_gains).astype(BF)
    gains_sent = {k: start(gains_low, SP, k, "gains_sp") for k in (1, 2, 3)}
    proj_blocks = now(proj_weight).astype(BF)
    proj_blocks = jnp.tile(proj_blocks[None], (nz, 1, 1, 1))
    fence(proj_blocks)

    gate_blocks = now(feed_weight[0]).astype(BF).reshape(row_block, 2, feed_columns)
    gate_blocks = jnp.tile(gate_blocks.transpose(1, 0, 2), (nz // 2, 1, 1))
    up_blocks = now(feed_weight[1]).astype(BF).reshape(row_block, 2, feed_columns)
    up_blocks = jnp.tile(up_blocks.transpose(1, 0, 2), (nz // 2, 1, 1))
    down_blocks = now(down_weight).astype(BF).reshape(2, units // 2, unit_rows, width)
    down_blocks = jnp.tile(down_blocks, (nz // 2, 1, 1, 1))

    x_rows = now(x_rows)
    x_y, x_c = start(x_rows, "tp", 2, "x_y"), start(x_rows, "tp", 1, "x_c")
    gains_sp = place({0: gains_low, **{k: now(v) for k, v in gains_sent.items()}}, zi)
    gains_dp = chain.start_dp(gains_sp, "gains_dp")
    fence()
    proj_own = chain.start_all(proj_blocks, "proj_sp")
    fence()
    x_y = now(x_y)
    x_yc = start(x_y, "tp", 1, "x_yc")
    fence(gate_blocks, up_blocks, down_blocks)

    gains_all = place({0: gains_sp, **{k + 1: now(v) for k, v in enumerate(gains_dp)}}, xi)
    gain_values = gains_all.transpose(2, 0, 1, 3).reshape(2, width).astype(F32)
    x_yc = now(x_yc)
    proj_own = now(proj_own)
    proj_got = chain.start_dp(proj_own, "proj_dp")
    gate_own = chain.start_all(after(gate_blocks, proj_own), "gate_sp")
    fence(x_yc, gain_values)

    def norm(rows, gain):
        inverse = lax.rsqrt(jnp.mean(rows * rows, axis=-1, keepdims=True) + NORM_EPSILON)
        unit = rows * inverse
        return unit, inverse, (unit * gain).astype(BF)

    normed_one, projected = project(at_tp, [x_rows, now(x_c), x_y, x_yc], gain_values[:1], qkv_all)
    cosine, sine = tables(length)
    qkv, context, logs = attend(chain.gate(projected), cosine, sine, groups)
    chain.passed(context)

    proj_all = order_units([proj_own] + [now(v) for v in proj_got], at, nz)
    attn_part = mm(context, proj_all).astype(BF).reshape(nz, 2, 2, span, width)
    attn_core = start(pick(attn_part, 1 - c, 2), "tp", 1, "attn_c")
    fence()
    attn_sum = (pick(attn_part, c, 2).astype(F32) + now(attn_core).astype(F32)).astype(BF)
    attn_y = start(pick(attn_sum, 1 - y, 1), "tp", 2, "attn_y")
    fence()
    gate_own = now(gate_own)
    gate_got = chain.start_dp(gate_own, "gate_dp")
    up_own = chain.start_all(after(up_blocks, gate_own), "up_sp")
    fence()

    attn_mine = (pick(attn_sum, y, 1).astype(F32) + now(attn_y).astype(F32)).reshape(-1, width)
    inputs = x_rows.astype(F32).reshape(-1, width)
    hidden_one = inputs + attn_mine
    unit_two, inverse_two, normed_two = norm(hidden_one, gain_values[1])
    gather = Gather(chain, normed_two, "normed")
    fence()
    gather.second()
    gather.near_core()
    fence()
    up_own = now(up_own)
    up_got = chain.start_dp(up_own, "up_dp")
    dy_rows = chain.start_all(after(cotangent, up_own), "dy_sp")
    fence()
    gather.far_core()
    gate_got = [chain.take(v) for v in gate_got]
    fence()

    def flat(arrays):
        return [v.reshape(-1, v.shape[-1]) for v in arrays]

    dy_rows = now(dy_rows)
    dy_gather = Gather(chain, dy_rows.reshape(-1, width), "dy")
    down_own = chain.start_all(after(down_blocks, dy_rows), "down_sp")
    gates = flat([gate_own] + gate_got)
    first, *others = gather.result()
    gate, normed_all = gate_rows(at, [chain.gate(first)] + others, gates)
    chain.passed(gate)

    dy_gather.second()
    ups = flat([up_own] + [chain.take(v) for v in up_got])
    hidden, activated, slope = up_rows(at, chain.gate(normed_all), gate, ups)
    chain.passed(hidden)

    dy_gather.near_core()
    dy_gather.far_core()
    fence()
    down_own = now(down_own)
    down_got = chain.start_dp(down_own, "down_dp")
    fence()
    dy_all = jnp.concatenate(dy_gather.result(), axis=0)
    down_part = mm_tn(hidden, dy_all).astype(BF)
    down_part = down_part.reshape(units // 2, nx, nz, unit_rows, width).transpose(1, 2, 0, 3, 4)

    def to_dp(parts, name):
        return [start(pick(parts, xi ^ k, 0), "dp", k, name) for k in range(1, nx)]

    def sum_dp(parts, got):
        total = pick(parts, xi, 0).astype(F32)
        for block in got:
            total = total + now(block).astype(F32)
        return total.astype(BF)

    down_dp = to_dp(down_part, "down_grad_dp")
    fence()

    down_all = order_units([down_own] + [now(v) for v in down_got], at, nz)
    grad_gate, grad_up, grad_other = ffn_back(
        at, dy_all, activated, slope, down_all, gates, ups, 1, None
    )
    chain.passed(grad_other)
    reduce = Reduce(chain, grad_other, "normed_grad")
    grad_gate, grad_up, grad_mine = ffn_back(
        at, chain.gate(dy_all), activated, slope, down_all, gates, ups, 0, (grad_gate, grad_up)
    )
    chain.passed(grad_mine)

    reduce.first(grad_mine)
    fence()

    gate_part = mm_tn(now(normed_all), grad_gate).astype(BF)
    gate_part = gate_part.reshape(nx, nz, row_block, feed_columns)
    gate_dp = to_dp(gate_part, "gate_grad_dp")
    fence()

    reduce.second()
    fence()
    down_moved = chain.start_all(sum_dp(down_part, down_dp), "down_grad_sp")
    fence()
    up_part = mm_tn(now(normed_all), grad_up).astype(BF).reshape(nx, nz, row_block, feed_columns)
    up_dp = to_dp(up_part, "up_grad_dp")
    fence()

    grad_normed_two = reduce.result()
    grad_unit = grad_normed_two * gain_values[1]
    row_inner = jnp.mean(grad_unit * unit_two, axis=-1, keepdims=True)
    dy_own = dy_rows.astype(F32).reshape(-1, width)
    back_two = inverse_two * (grad_unit - unit_two * row_inner)
    gain_two_part = jnp.sum(grad_normed_two * unit_two, axis=0)
    grad_hidden_one = dy_own + back_two
    rows_mine = grad_hidden_one.astype(BF).reshape(nz, span, width)
    rows_y, rows_c = start(rows_mine, "tp", 2, "rows_y"), start(rows_mine, "tp", 1, "rows_c")
    fence()
    down_moved = chain.take(down_moved)
    gate_sum = sum_dp(gate_part, gate_dp)
    gate_moved = chain.start_all(after(gate_sum, down_moved), "gate_grad_sp")
    fence()
    out_part = mm(now(hidden), down_all).astype(BF)
    out_rows = out_part.shape[0] // 2
    out_reduce = Reduce(chain, out_part[out_rows:], "out")
    fence()
    rows_y = now(rows_y)
    rows_yc = start(rows_y, "tp", 1, "rows_yc")
    fence()

    grad_rows, grad_context = context_grad(
        at_tp, [rows_mine, now(rows_c), rows_y, now(rows_yc)], proj_all
    )
    out_reduce.first(out_part[:out_rows])
    grad_projected = attend_back(qkv, chain.gate(grad_context), logs, cosine, sine, groups)
    chain.passed(grad_projected)

    gate_moved = chain.take(gate_moved)
    up_sum = sum_dp(up_part, up_dp)
    up_moved = chain.start_all(after(up_sum, gate_moved), "up_grad_sp")
    dn_part = mm_nt(grad_projected, qkv_all).astype(BF).reshape(nz, 2, 2, span, width)
    dn_core = start(pick(dn_part, 1 - c, 2), "tp", 1, "dn_c")
    fence()
    dn_sum = (pick(dn_part, c, 2).astype(F32) + now(dn_core).astype(F32)).astype(BF)
    dn_y = start(pick(dn_sum, 1 - y, 1), "tp", 2, "dn_y")
    fence()
    qkv_part = mm_tn(now(normed_one), grad_projected).astype(BF)
    qkv_grad = lax.psum_scatter(qkv_part, ("dp",) + SP, tiled=True)
    out_reduce.second()
    fence(qkv_part)
    proj_part = mm_tn(context, now(grad_rows)).astype(BF)
    proj_part = proj_part.reshape(groups, nx, nz, proj_rows, width).transpose(1, 2, 0, 3, 4)
    proj_dp = to_dp(proj_part, "proj_grad_dp")
    fence()

    grad_normed_one = (pick(dn_sum, y, 1).astype(F32) + now(dn_y).astype(F32)).reshape(-1, width)
    inverse_one = lax.rsqrt(jnp.mean(inputs * inputs, axis=-1, keepdims=True) + NORM_EPSILON)
    unit_one = inputs * inverse_one
    grad_unit = grad_normed_one * gain_values[0]
    row_inner = jnp.mean(grad_unit * unit_one, axis=-1, keepdims=True)
    back_one = inverse_one * (grad_unit - unit_one * row_inner)
    gain_one_part = jnp.sum(grad_normed_one * unit_one, axis=0)
    input_delta = (back_two + back_one).astype(BF).reshape(nz, span, width)
    gains_part = jnp.stack([gain_one_part, gain_two_part])
    gains_c = start(gains_part, "tp", 1, "gains_c")
    up_moved = chain.take(up_moved)
    input_moved = chain.start_all(after(input_delta, up_moved), "input_sp")
    fence()

    def halves(blocks, axis):
        blocks = [blocks[i].astype(F32) for i in range(nz)]
        parity = [sum(blocks[i] for i in range(p, nz, 2)) for p in range(2)]
        return jnp.concatenate(parity, axis=axis)

    gains_part = gains_part + now(gains_c)
    gains_y = start(gains_part, "tp", 2, "gains_y")
    block_delta = (attn_mine + out_reduce.result()).astype(BF).reshape(nz, span, width)
    down_grad = halves(now(down_moved), 0)
    down_new, down_first_new, down_second_new = adamw(
        down_weight, down_grad, down_first, down_second, DOWN_RATE, WEIGHT_DECAY
    )
    proj_sum = sum_dp(proj_part, proj_dp)
    fence(block_delta, down_new, proj_sum)

    gains_part = (gains_part + now(gains_y)).reshape(2, nx, nz, row_block).transpose(1, 2, 0, 3)
    gains_dp = to_dp(gains_part, "gains_dp")
    feed_grad = jnp.stack([halves(gate_moved, 1), halves(up_moved, 1)])
    feed_new, feed_first_new, feed_second_new = adamw(
        now(feed_weight), feed_grad, feed_first, feed_second, FEED_RATE, WEIGHT_DECAY
    )
    input_moved = chain.take(input_moved)
    proj_moved = chain.start_all(after(proj_sum, input_moved), "proj_grad_sp")
    fence(feed_new)

    gains_sum = pick(gains_part, xi, 0)
    for block in gains_dp:
        gains_sum = gains_sum + now(block)
    gains_moved = {k: start(pick(gains_sum, zi ^ k, 0), SP, k, "gains_sp") for k in (1, 2, 3)}
    input_grad = cotangent.astype(F32) + input_moved.astype(F32)
    proj_moved = chain.take(proj_moved).astype(F32)
    proj_grad = proj_moved[0] + proj_moved[1] + proj_moved[2] + proj_moved[3]
    block_moved = chain.start_all(after(block_delta, proj_moved), "block_sp")
    fence(input_grad)
    qkv_grad = now(qkv_grad).reshape(row_block, groups, columns).transpose(1, 0, 2)
    qkv_grad = after(qkv_grad).astype(F32)
    gains_grad = pick(gains_sum, zi, 0)
    for block in gains_moved.values():
        gains_grad = gains_grad + now(block)
    block_out = block_in.astype(F32) + now(block_moved).astype(F32)

    qkv_new, qkv_first_new, qkv_second_new = adamw(
        qkv_weight, qkv_grad, qkv_first, qkv_second, QKV_RATE, WEIGHT_DECAY
    )
    proj_new, proj_first_new, proj_second_new = adamw(
        proj_weight, proj_grad, proj_first, proj_second, PROJ_RATE, WEIGHT_DECAY
    )
    gains_new, gains_first_new, gains_second_new = adamw(
        norm_gains, gains_grad, gains_first, gains_second, GAIN_RATE, 0.0
    )
    return (
        block_out,
        input_grad,
        qkv_grad,
        proj_grad,
        feed_grad,
        down_grad,
        gains_grad,
        qkv_new,
        proj_new,
        feed_new,
        down_new,
        gains_new,
        qkv_first_new,
        proj_first_new,
        feed_first_new,
        down_first_new,
        gains_first_new,
        qkv_second_new,
        proj_second_new,
        feed_second_new,
        down_second_new,
        gains_second_new,
    )


def solution(mesh):
    sizes = mesh.shape
    mesh = Mesh(
        mesh.devices.reshape(sizes["dp"], sizes["sp"] // 2, 2, sizes["tp"]), ("dp",) + SP + ("tp",)
    )
    rows = P("dp", SP + ("tp",), None)
    heads = P("tp", ("dp",) + SP, None)
    feed = P(None, ("dp",) + SP, "tp")
    gains = P(None, ("dp",) + SP)
    params = (heads, heads, feed, heads, gains)
    return jax.shard_map(
        local,
        mesh=mesh,
        in_specs=(rows, rows) + params * 3,
        out_specs=(rows, rows) + params * 4,
        check_vma=False,
    )
```

time: 1060 us -> 800 us (0.75)
  waiting for transfers between devices: 435 us -> 267 us
  starting transfers between devices: 224 us -> 103 us
  Pallas kernels: 125 us -> 159 us
  local copies, waits for them, and re-layouts: 104 us -> 76.9 us
  other arithmetic: 81.4 us -> 105 us
  between operations: 3.33 us -> 15.4 us
  matrix products: 76.5 us -> 65.3 us
    ppermute x119 -> x50, waiting for transfers between devices: 416 us -> 152 us  [swap(): lax.ppermute(value, axis, [(i, i ^ mask) for i in range(lax.axis_size(axi...]
    ppermute x119 -> x50, starting transfers between devices: 166 us -> 46.5 us  [swap(): lax.ppermute(value, axis, [(i, i ^ mask) for i in range(lax.axis_size(axi...]
    all_to_all x0 -> x12, waiting for transfers between devices: none -> 114 us  [start_all(): return lax.all_to_all(blocks, SP, 0, 0, tiled=True)]
    ppermute x24 -> x0, starting transfers between devices: 57.8 us -> none  [the longest x6 29.7 us: reduce_line(): up = lax.ppermute(to_up, 'sp', [(i, i + 1) for i in range(step)])]
    all_to_all x0 -> x12, starting transfers between devices: none -> 56.2 us  [start_all(): return lax.all_to_all(blocks, SP, 0, 0, tiled=True)]
    pallas_call x3 -> x8, Pallas kernels: 74.8 us -> 109 us  [the longest x2 42.3 us: ffn_back(): pl.pallas_call(functools.partial(ffn_back_kernel, tf, parts), grid=(steps...]
    ppermute x24 -> x0, waiting for transfers between devices: 19.1 us -> none  [the longest x12 10 us: line(): return lax.ppermute(value, 'sp', pairs)]
    dynamic_update_slice x48 -> x0, local copies, waits for them, and re-layouts: 16.6 us -> none  [the longest x21 10.3 us: fill_rows(): lax.dynamic_update_slice(out, got, (((xi ^ kx) * nz + source) * rows, 0))]
  transfers between devices with their start and end apart: 143 -> 64, of which waited for: 52 -> 20; matrix products, arithmetic and copies ran while one was open for 22% -> 28% of each run, Pallas kernels for 9% -> 20%
where the time goes in v2:
time: 800 us; the launch traced here: 792 us
  waiting for transfers between devices  267 us (33%)
  Pallas kernels  159 us (20%)
  other arithmetic  105 us (13%)
  starting transfers between devices  103 us (13%)
  local copies, waits for them, and re-layouts  76.9 us (10%)
  matrix products  65.3 us (8%)
  between operations  15.4 us (2%)
    ppermute x50, waiting for transfers between devices, swap(): lax.ppermute(value, axis, [(i, i ^ mask) for i in range(lax.axis_size(axi...  152 us
    all_to_all x12, waiting for transfers between devices, start_all(): return lax.all_to_all(blocks, SP, 0, 0, tiled=True)  114 us
    dot_general x8, matrix products, dot(): lax.dot_general(left, right, ((dims[0], dims[1]), ((), ())), preferred_el...  65.3 us
    all_to_all x12, starting transfers between devices, start_all(): return lax.all_to_all(blocks, SP, 0, 0, tiled=True)  56.2 us
    ppermute x50, starting transfers between devices, swap(): lax.ppermute(value, axis, [(i, i ^ mask) for i in range(lax.axis_size(axi...  46.5 us
    pallas_call x2, Pallas kernels, ffn_back(): pl.pallas_call(functools.partial(ffn_back_kernel, tf, parts), grid=(steps...  42.3 us
    unnamed x133, local copies, waits for them, and re-layouts  37.8 us
    pallas_call x1, Pallas kernels, attend_back(): pl.pallas_call(functools.partial(attend_back_kernel, tile), grid=(groups,...  28.8 us
  transfers between devices with their start and end apart: 64, of which 20 were waited for; matrix products, arithmetic and copies ran while one was open for 28% of the time, Pallas kernels for 20%

profile of v2, /device:TPU:0, one launch (start us, length us, event | category | flops | bytes accessed | tf_op | source)
XLA Modules:
  0.0 791.8 jit_solution(680860898682926327)
XLA Ops:
  7.2 6.5 all-to-all-start
  33.3 18.1 %collective-permute-done.3 = bf16[2,256]{1,0:T(2,128)(2,1)S(1)} collective-permute-done((bf16[2,256]{1,0:T(2,128)(2,1)S(1)}, bf16[2,256]{1,0:T(2,128)(2,1)S(1)}, u32[]{:S(2)}, u32[]{:S(2)}) %collective-permute-start.3) | collective-permute-done | bytes 1056 | tf_op jit(solution)/shard_map/gains_sp/ppermute | solution.py:42
  59.1 19.8 %collective-permute-done.1.refs_2_ = bf16[4,64,2048]{2,1,0:T(8,128)(2,1)} collective-permute-done((bf16[4,64,2048]{2,1,0:T(8,128)(2,1)S(1)}, bf16[4,64,2048]{2,1,0:T(8,128)(2,1)}, u32[]{:S(2)}, u32[]{:S(2)}) %collective-permute-start.1) | collective-permute-done | bytes 1048608 | tf_op jit(solution)/shard_map/x_y/ppermute | solution.py:42
  84.9 23.0 %all-to-all-done.1.refs_0_ = bf16[4,2,32,2048]{3,2,1,0:T(8,128)(2,1)} async-done(((bf16[4,2,32,2048]{3,2,1,0:T(8,128)(2,1)}), bf16[4,2,32,2048]{3,2,1,0:T(8,128)(2,1)}, u32[]{:S(2)}, u32[]{:S(2)}) %all-to-all-start.1) | async-done | bytes 1048608 | tf_op jit(solution)/shard_map/proj_sp/all_to_all | solution.py:482
  113.9 8.7 %project.1 = (bf16[1024,2048]{1,0:T(8,128)(2,1)}, f32[1024,768]{1,0:T(8,128)}) custom-call(s32[4]{0:T(128)} %pad_add_fusion.at_ref, bf16[4,64,2048]{2,1,0:T(8,128)(2,1)} %copy-done.5, bf16[4,64,2048]{2,1,0:T(8,128)(2,1)} %collective-permute-done.refs_1_, bf16[4,64,2048]{2,1,0:T(8,128)(2,1)} %collective-permute-done.1.refs_2_, ...), custom_call_target="tpu_custom_call" | custom-call | flops 4294967296 | bytes 1048576 | tf_op jit(solution)/shard_map/project/pallas_call | solution.py:375
  122.6 20.9 %attend.1 = (bf16[1024,768]{1,0:T(8,128)(2,1)}, bf16[1024,512]{1,0:T(8,128)(2,1)}, f32[2,4,1024]{2,1,0:T(4,128)}) custom-call(f32[1024,768]{1,0:T(8,128)} %get-tuple-element.239.p_ref, f32[1024,128]{1,0:T(8,128)} %get-tuple-element.480.cos_ref, f32[1024,128]{1,0:T(8,128)} %get-tuple-element.481.sin_ref), custom_call_target="tpu_custom_call" | custom-call | flops 68719476736 | bytes 1048576 | tf_op jit(solution)/shard_map/attend/pallas_call | solution.py:119
  167.6 16.5 %collective-permute-done.9 = bf16[4,64,2048]{2,1,0:T(8,128)(2,1)} collective-permute-done((bf16[4,64,2048]{2,1,0:T(8,128)(2,1)S(1)}, bf16[4,64,2048]{2,1,0:T(8,128)(2,1)}, u32[]{:S(2)}, u32[]{:S(2)}) %collective-permute-start.9) | collective-permute-done | bytes 1048608 | tf_op jit(solution)/shard_map/attn_y/ppermute | solution.py:42
  191.1 19.9 %collective-permute-done.11 = bf16[128,2048]{1,0:T(8,128)(2,1)S(1)} collective-permute-done((bf16[128,2048]{1,0:T(8,128)(2,1)S(1)}, bf16[128,2048]{1,0:T(8,128)(2,1)S(1)}, u32[]{:S(2)}, u32[]{:S(2)}) %collective-permute-start.11) | collective-permute-done | bytes 524320 | tf_op jit(solution)/shard_map/normed/ppermute | solution.py:42
  217.0 4.9 all-to-all-start.4
  222.8 28.7 %collective-permute-done.12 = bf16[256,2048]{1,0:T(8,128)(2,1)} collective-permute-done((bf16[256,2048]{1,0:T(8,128)(2,1)}, bf16[256,2048]{1,0:T(8,128)(2,1)}, u32[]{:S(2)}, u32[]{:S(2)}) %collective-permute-start.12) | collective-permute-done | bytes 1048608 | tf_op jit(solution)/shard_map/normed/ppermute | solution.py:42
  266.4 19.3 %gate_rows.1 = (f32[2048,1024]{1,0:T(8,128)}, bf16[2048,2048]{1,0:T(8,128)(2,1)}) custom-call(s32[2]{0:T(128)} %pad_add_fusion.1.at_ref, bf16[512,2048]{1,0:T(8,128)(2,1)} %copy-done.36, bf16[512,2048]{1,0:T(8,128)(2,1)} %constant_dynamic-update-slice_fusion.refs_1_, bf16[512,2048]{1,0:T(8,128)(2,1)} %collective-permute-done.15.refs_2_, ...), custom_call_target="tpu_custom_call" | custom-call | flops 68719476736 | bytes 1048576 | tf_op jit(solution)/shard_map/gate_rows/pallas_call | solution.py:258
  291.2 24.4 %up_rows.1 = (bf16[2048,1024]{1,0:T(8,128)(2,1)}, f32[2048,1024]{1,0:T(8,128)}, f32[2048,1024]{1,0:T(8,128)}) custom-call(s32[2]{0:T(128)} %pad_add_fusion.1.at_ref, bf16[2048,2048]{1,0:T(8,128)(2,1)} %get-tuple-element.330.rows_ref, f32[2048,1024]{1,0:T(8,128)} %get-tuple-element.286.gate_ref, bf16[1024,1024]{1,0:T(8,128)(2,1)} %bitcast.34.refs_0_.refs_2_, ...), custom_call_target="tpu_custom_call" | custom-call | flops 68719476736 | bytes 1048576 | tf_op jit(solution)/shard_map/up_rows/pallas_call | solution.py:294
  340.0 11.7 %convolution_convert_fusion.1 = bf16[1024,2048]{1,0:T(8,128)(2,1)S(1)} fusion(bf16[2048,1024]{1,0:T(8,128)(2,1)S(1)} %copy-done.56, bf16[2048,2048]{1,0:T(8,128)(2,1)} %constant_dynamic-update-slice_fusion.2.dy_ref), kind=kOutput, calls=%fused_computation.18 | convolution fusion | flops 8592031744 | bytes 16777216 | tf_op jit(solution)/shard_map/dot_general | solution.py:50
  356.3 24.8 %collective-permute-done.24.refs_1_ = bf16[4,4,32,2048]{3,2,1,0:T(8,128)(2,1)S(1)} collective-permute-done((bf16[4,4,32,2048]{3,2,1,0:T(8,128)(2,1)S(1)}, bf16[4,4,32,2048]{3,2,1,0:T(8,128)(2,1)S(1)}, u32[]{:S(2)}, u32[]{:S(2)}) %collective-permute-start.24) | collective-permute-done | bytes 2097184 | tf_op jit(solution)/shard_map/down_dp/ppermute | solution.py:42
  386.9 21.4 %ffn_back.2 = (bf16[2048,1024]{1,0:T(8,128)(2,1)}, bf16[2048,1024]{1,0:T(8,128)(2,1)}, bf16[1024,2048]{1,0:T(8,128)(2,1)}) custom-call(s32[2]{0:T(128)} %pad_add_fusion.1.at_ref, bf16[2048,2048]{1,0:T(8,128)(2,1)} %constant_dynamic-update-slice_fusion.2.dy_ref, f32[2048,1024]{1,0:T(8,128)} %get-tuple-element.305.a_ref, ...), custom_call_target="tpu_custom_call" | custom-call | flops 68719476736 | bytes 1048576 | tf_op jit(solution)/shard_map/ffn_back/pallas_call | solution.py:341
  408.4 20.9 %ffn_back.3 = (bf16[2048,1024]{1,0:T(8,128)(2,1)}, bf16[2048,1024]{1,0:T(8,128)(2,1)}, bf16[1024,2048]{1,0:T(8,128)(2,1)}) custom-call(s32[2]{0:T(128)} %pad_add_fusion.1.at_ref, bf16[2048,2048]{1,0:T(8,128)(2,1)} %constant_dynamic-update-slice_fusion.2.dy_ref, ...), custom_call_target="tpu_custom_call", output_to_operand_aliasing={{0}: (9, {}), {1}: (10, {})} | custom-call | flops 68719476736 | bytes 1048576 | tf_op jit(solution)/shard_map/ffn_back/pallas_call | solution.py:341
  437.1 11.6 %convolution_convert_fusion.5 = bf16[2048,1024]{1,0:T(8,128)(2,1)S(1)} fusion(bf16[2048,2048]{1,0:T(8,128)(2,1)} %get-tuple-element.330.rows_ref, bf16[2048,1024]{1,0:T(8,128)(2,1)S(1)} %copy-done.59), kind=kOutput, calls=%fused_computation.22 | convolution fusion | flops 8592031744 | bytes 16777216 | tf_op jit(solution)/shard_map/dot_general | solution.py:50
  452.3 7.0 collective-permute-done.27
  472.1 12.7 %convolution_convert_fusion.4 = bf16[2048,1024]{1,0:T(8,128)(2,1)S(1)} fusion(bf16[2048,2048]{1,0:T(8,128)(2,1)} %get-tuple-element.330.rows_ref, bf16[2048,1024]{1,0:T(8,128)(2,1)} %get-tuple-element.331), kind=kOutput, calls=%fused_computation.21 | convolution fusion | flops 8592031744 | bytes 16777216 | tf_op jit(solution)/shard_map/dot_general | solution.py:50
  504.1 15.6 %all-to-all-done.6 = bf16[4,4,32,2048]{3,2,1,0:T(8,128)(2,1)} async-done(((bf16[4,4,32,2048]{3,2,1,0:T(8,128)(2,1)}), bf16[4,4,32,2048]{3,2,1,0:T(8,128)(2,1)}, u32[]{:S(2)}, u32[]{:S(2)}) %all-to-all-start.6) | async-done | bytes 2097184 | tf_op jit(solution)/shard_map/down_grad_sp/all_to_all | solution.py:482
  519.7 11.9 %convolution_convert_fusion = bf16[2048,2048]{1,0:T(8,128)(2,1)S(1)} fusion(bf16[2048,1024]{1,0:T(8,128)(2,1)} %get-tuple-element.343, bf16[1024,2048]{1,0:T(8,128)(2,1)} %bitcast.311), kind=kOutput, calls=%fused_computation.2 | convolution fusion | flops 8594128896 | bytes 16777216 | tf_op jit(solution)/shard_map/dot_general | solution.py:50
  545.2 6.8 context_grad.1
  552.0 5.4 add_convert_fusion
  561.2 28.8 %attend_back.1 = bf16[1024,768]{1,0:T(8,128)(2,1)} custom-call(bf16[1024,768]{1,0:T(8,128)(2,1)} %get-tuple-element.351.qkv_ref, bf16[1024,512]{1,0:T(8,128)(2,1)} %get-tuple-element.356.grad_ref, f32[2,4,1024]{2,1,0:T(4,128)} %get-tuple-element.357.log_ref, f32[1024,128]{1,0:T(8,128)} %get-tuple-element.480.cos_ref, f32[1024,128]{1,0:T(8,128)} %get-tuple-element.481.sin_ref), custom_call_target="tpu_custom_call" | custom-call | flops 68719476736 | bytes 1048576 | tf_op jit(solution)/shard_map/attend_back/pallas_call | solution.py:198
  624.8 4.9 convolution_convert_fusion.6
  630.6 4.9 convolution_convert_fusion.7
  643.6 22.1 %all-to-all-done.8 = bf16[4,256,1024]{2,1,0:T(8,128)(2,1)} async-done(((bf16[4,256,1024]{2,1,0:T(8,128)(2,1)}), bf16[4,256,1024]{2,1,0:T(8,128)(2,1)}, u32[]{:S(2)}, u32[]{:S(2)}) %all-to-all-start.8) | async-done | bytes 2097184 | tf_op jit(solution)/shard_map/up_grad_sp/all_to_all | solution.py:482
  687.0 6.5 multiply_subtract_fusion.1
  696.1 7.5 multiply_subtract_fusion
  705.3 5.1 all-to-all-start.10
  718.2 29.0 %all-to-all-done.10 = bf16[4,2,32,2048]{3,2,1,0:T(8,128)(2,1)S(1)} async-done(((bf16[4,2,32,2048]{3,2,1,0:T(8,128)(2,1)}), bf16[4,2,32,2048]{3,2,1,0:T(8,128)(2,1)S(1)}, u32[]{:S(2)}, u32[]{:S(2)}) %all-to-all-start.10) | async-done | bytes 1048608 | tf_op jit(solution)/shard_map/proj_grad_sp/all_to_all | solution.py:482
  755.4 22.5 %all-to-all-done.11 = bf16[4,64,2048]{2,1,0:T(8,128)(2,1)} async-done(((bf16[4,64,2048]{2,1,0:T(8,128)(2,1)}), bf16[4,64,2048]{2,1,0:T(8,128)(2,1)}, u32[]{:S(2)}, u32[]{:S(2)}) %all-to-all-start.11) | async-done | bytes 1048608 | tf_op jit(solution)/shard_map/block_sp/all_to_all | solution.py:482
  (358 shorter events, 284.8 us)
Async XLA Ops:
  7.2 45.8 %all-to-all-start = ((bf16[4,64,2048]{2,1,0:T(8,128)(2,1)}), bf16[4,64,2048]{2,1,0:T(8,128)(2,1)S(1)}, u32[]{:S(2)}, u32[]{:S(2)}) async-start(bf16[4,64,2048]{2,1,0:T(8,128)(2,1)} %param.17), calls=%async_computation | async-start | bytes 2097152 | tf_op jit(solution)/shard_map/x_sp/all_to_all | solution.py:482
  13.7 100.2 %all-gather.2.cloned.1.call-start = ((), (), s32[]{:S(2)}) async-start(), calls=%async_computation.13 | async-start | bytes 3538944 | tf_op jit(solution)/shard_map/all_gather | solution.py:614
  54.7 53.2 %all-to-all-start.1 = ((bf16[4,2,32,2048]{3,2,1,0:T(8,128)(2,1)}), bf16[4,2,32,2048]{3,2,1,0:T(8,128)(2,1)}, u32[]{:S(2)}, u32[]{:S(2)}) async-start(bf16[4,2,32,2048]{3,2,1,0:T(8,128)(2,1)} %tile.16), calls=%async_computation.1 | async-start | bytes 2097152 | tf_op jit(solution)/shard_map/proj_sp/all_to_all | solution.py:482
  109.2 52.6 %all-to-all-start.2 = ((bf16[4,256,1024]{2,1,0:T(8,128)(2,1)}), bf16[4,256,1024]{2,1,0:T(8,128)(2,1)}, u32[]{:S(2)}, u32[]{:S(2)}) async-start(bf16[4,256,1024]{2,1,0:T(8,128)(2,1)} %bitcast.11), calls=%async_computation.2 | async-start | bytes 4194304 | tf_op jit(solution)/shard_map/gate_sp/all_to_all | solution.py:482
  161.9 55.2 %all-to-all-start.3 = ((bf16[4,256,1024]{2,1,0:T(8,128)(2,1)}), bf16[4,256,1024]{2,1,0:T(8,128)(2,1)}, u32[]{:S(2)}, u32[]{:S(2)}) async-start(bf16[4,256,1024]{2,1,0:T(8,128)(2,1)} %bitcast.14), calls=%async_computation.3 | async-start | bytes 4194304 | tf_op jit(solution)/shard_map/up_sp/all_to_all | solution.py:482
  166.4 89.7 %collective-permute-start.14 = (bf16[4,256,1024]{2,1,0:T(8,128)(2,1)}, bf16[4,256,1024]{2,1,0:T(8,128)(2,1)}, u32[]{:S(2)}, u32[]{:S(2)}) collective-permute-start(bf16[4,256,1024]{2,1,0:T(8,128)(2,1)} %all-to-all-done.2), channel_id=1, source_target_pairs={{0,16},{16,0},{1,17},{17,1},{2,18},{18,2},{3,19},{19,3},{4,20},{20... | collective-permute-start | bytes 6291464 | tf_op jit(solution)/shard_map/gate_dp/ppermute | solution.py:42
  213.4 38.1 %collective-permute-start.12 = (bf16[256,2048]{1,0:T(8,128)(2,1)}, bf16[256,2048]{1,0:T(8,128)(2,1)}, u32[]{:S(2)}, u32[]{:S(2)}) collective-permute-start(bf16[256,2048]{1,0:T(8,128)(2,1)} %pad_maximum_fusion.7), channel_id=1, source_target_pairs={{0,4},{4,0},{8,12},{12,8},{1,5},{5,1},{9,13},{13,9},{2,6},{6,2},{1... | collective-permute-start | bytes 3145736 | tf_op jit(solution)/shard_map/normed/ppermute | solution.py:42
  217.0 39.1 %collective-permute-start.15 = (bf16[512,2048]{1,0:T(8,128)(2,1)S(1)}, bf16[512,2048]{1,0:T(8,128)(2,1)}, u32[]{:S(2)}, u32[]{:S(2)}) collective-permute-start(bf16[512,2048]{1,0:T(8,128)(2,1)S(1)} %pad_maximum_fusion.1.refs_0_), channel_id=1, source_target_pairs={{0,1},{1,0},{2,3},{3,2},{4,5},{5,4},{6,7},{7,6},{8,9},{9,8},{10,11... | collective-permute-start | bytes 6291464 | tf_op jit(solution)/shard_map/normed/ppermute | solution.py:42
  217.0 39.1 %all-to-all-start.4 = ((bf16[4,64,2048]{2,1,0:T(8,128)(2,1)}), bf16[4,64,2048]{2,1,0:T(8,128)(2,1)S(1)}, u32[]{:S(2)}, u32[]{:S(2)}) async-start(bf16[4,64,2048]{2,1,0:T(8,128)(2,1)} %param.18), calls=%async_computation.4 | async-start | bytes 2097152 | tf_op jit(solution)/shard_map/dy_sp/all_to_all | solution.py:482
  221.9 66.4 %collective-permute-start.19 = (bf16[4,256,1024]{2,1,0:T(8,128)(2,1)}, bf16[4,256,1024]{2,1,0:T(8,128)(2,1)}, u32[]{:S(2)}, u32[]{:S(2)}) collective-permute-start(bf16[4,256,1024]{2,1,0:T(8,128)(2,1)} %all-to-all-done.3), channel_id=1, source_target_pairs={{0,16},{16,0},{1,17},{17,1},{2,18},{18,2},{3,19},{19,3},{4,20},{20... | collective-permute-start | bytes 6291464 | tf_op jit(solution)/shard_map/up_dp/ppermute | solution.py:42
  260.7 72.0 %all-to-all-start.5 = ((bf16[4,4,32,2048]{3,2,1,0:T(8,128)(2,1)}), bf16[4,4,32,2048]{3,2,1,0:T(8,128)(2,1)S(1)}, u32[]{:S(2)}, u32[]{:S(2)}) async-start(bf16[4,4,32,2048]{3,2,1,0:T(8,128)(2,1)} %bitcast.16), calls=%async_computation.5 | async-start | bytes 4194304 | tf_op jit(solution)/shard_map/down_sp/all_to_all | solution.py:482
  288.3 40.5 %collective-permute-start.20 = (bf16[256,2048]{1,0:T(8,128)(2,1)S(1)}, bf16[256,2048]{1,0:T(8,128)(2,1)S(1)}, u32[]{:S(2)}, u32[]{:S(2)}) collective-permute-start(bf16[256,2048]{1,0:T(8,128)(2,1)S(1)} %pad_maximum_fusion.9), channel_id=1, source_target_pairs={{0,4},{4,0},{8,12},{12,8},{1,5},{5,1},{9,13},{13,9},{2,6},{6,2},{1... | collective-permute-start | bytes 3145736 | tf_op jit(solution)/shard_map/dy/ppermute | solution.py:42
  290.4 38.5 %collective-permute-start.21 = (bf16[256,2048]{1,0:T(8,128)(2,1)S(1)}, bf16[256,2048]{1,0:T(8,128)(2,1)S(1)}, u32[]{:S(2)}, u32[]{:S(2)}) collective-permute-start(bf16[256,2048]{1,0:T(8,128)(2,1)S(1)} %pad_maximum_fusion.10), channel_id=1, source_target_pairs={{0,2},{1,3},{2,0},{3,1},{4,6},{5,7},{6,4},{7,5},{8,10},{9,11},{10,... | collective-permute-start | bytes 3145736 | tf_op jit(solution)/shard_map/dy/ppermute | solution.py:42
  332.7 48.4 %collective-permute-start.24 = (bf16[4,4,32,2048]{3,2,1,0:T(8,128)(2,1)S(1)}, bf16[4,4,32,2048]{3,2,1,0:T(8,128)(2,1)S(1)}, u32[]{:S(2)}, u32[]{:S(2)}) collective-permute-start(bf16[4,4,32,2048]{3,2,1,0:T(8,128)(2,1)S(1)} %all-to-all-done.5.refs_0_), channel_id=1, source_target_pairs={{0,16},{16,0},{1,17},{17,1},{2,18},{18,2},{3,19},{19,3},{4,20},{20... | collective-permute-start | bytes 6291464 | tf_op jit(solution)/shard_map/down_dp/ppermute | solution.py:42
  355.1 108.5 %collective-permute-start.28 = (bf16[4,4,32,2048]{3,2,1,0:T(8,128)(2,1)}, bf16[4,4,32,2048]{3,2,1,0:T(8,128)(2,1)}, u32[]{:S(2)}, u32[]{:S(2)}) collective-permute-start(bf16[4,4,32,2048]{3,2,1,0:T(8,128)(2,1)} %bitcast.290), channel_id=1, source_target_pairs={{0,16},{16,0},{1,17},{17,1},{2,18},{18,2},{3,19},{19,3},{4,20},{20... | collective-permute-start | bytes 6291464 | tf_op jit(solution)/shard_map/down_grad_dp/ppermute | solution.py:42
  451.4 48.7 %collective-permute-start.31 = (bf16[4,256,1024]{2,1,0:T(8,128)(2,1)}, bf16[4,256,1024]{2,1,0:T(8,128)(2,1)}, u32[]{:S(2)}, u32[]{:S(2)}) collective-permute-start(bf16[4,256,1024]{2,1,0:T(8,128)(2,1)} %dynamic-slice_bitcast_fusion.1), channel_id=1, source_target_pairs={{0,16},{16,0},{1,17},{17,1},{2,18},{18,2},{3,19},{19,3},{4,20},{20... | collective-permute-start | bytes 6291464 | tf_op jit(solution)/shard_map/gate_grad_dp/ppermute | solution.py:42
  467.4 52.3 %all-to-all-start.6 = ((bf16[4,4,32,2048]{3,2,1,0:T(8,128)(2,1)}), bf16[4,4,32,2048]{3,2,1,0:T(8,128)(2,1)}, u32[]{:S(2)}, u32[]{:S(2)}) async-start(bf16[4,4,32,2048]{3,2,1,0:T(8,128)(2,1)} %fusion.4), calls=%async_computation.6 | async-start | bytes 4194304 | tf_op jit(solution)/shard_map/down_grad_sp/all_to_all | solution.py:482
  487.6 102.6 %collective-permute-start.37 = (bf16[4,256,1024]{2,1,0:T(8,128)(2,1)}, bf16[4,256,1024]{2,1,0:T(8,128)(2,1)}, u32[]{:S(2)}, u32[]{:S(2)}) collective-permute-start(bf16[4,256,1024]{2,1,0:T(8,128)(2,1)} %dynamic-slice_bitcast_fusion), channel_id=1, source_target_pairs={{0,16},{16,0},{1,17},{17,1},{2,18},{18,2},{3,19},{19,3},{4,20},{20... | collective-permute-start | bytes 6291464 | tf_op jit(solution)/shard_map/up_grad_dp/ppermute | solution.py:42
  496.4 39.9 %collective-permute-start.33 = (bf16[4,64,2048]{2,1,0:T(8,128)(2,1)}, bf16[4,64,2048]{2,1,0:T(8,128)(2,1)}, u32[]{:S(2)}, u32[]{:S(2)}) collective-permute-start(bf16[4,64,2048]{2,1,0:T(8,128)(2,1)} %add_convert_fusion.3.refs_0_), channel_id=1, source_target_pairs={{0,2},{1,3},{2,0},{3,1},{4,6},{5,7},{6,4},{7,5},{8,10},{9,11},{10,... | collective-permute-start | bytes 3145736 | tf_op jit(solution)/shard_map/rows_y/ppermute | solution.py:42
  497.2 44.2 %collective-permute-start.35 = (bf16[4,64,2048]{2,1,0:T(8,128)(2,1)}, bf16[4,64,2048]{2,1,0:T(8,128)(2,1)}, u32[]{:S(2)}, u32[]{:S(2)}) collective-permute-start(bf16[4,64,2048]{2,1,0:T(8,128)(2,1)} %add_convert_fusion.3.refs_0_), channel_id=1, source_target_pairs={{0,1},{1,0},{2,3},{3,2},{4,5},{5,4},{6,7},{7,6},{8,9},{9,8},{10,11... | collective-permute-start | bytes 3145736 | tf_op jit(solution)/shard_map/rows_c/ppermute | solution.py:42
  536.7 53.5 %all-to-all-start.7 = ((bf16[4,256,1024]{2,1,0:T(8,128)(2,1)}), bf16[4,256,1024]{2,1,0:T(8,128)(2,1)}, u32[]{:S(2)}, u32[]{:S(2)}) async-start(bf16[4,256,1024]{2,1,0:T(8,128)(2,1)} %fusion.3), calls=%async_computation.7 | async-start | bytes 4194304 | tf_op jit(solution)/shard_map/gate_grad_sp/all_to_all | solution.py:482
  560.1 55.7 %collective-permute-start.34 = (bf16[2,128,2048]{2,1,0:T(8,128)(2,1)}, bf16[2,128,2048]{2,1,0:T(8,128)(2,1)}, u32[]{:S(2)}, u32[]{:S(2)}) collective-permute-start(bf16[2,128,2048]{2,1,0:T(8,128)(2,1)} %get-tuple-element.350), channel_id=1, source_target_pairs={{0,2},{1,3},{2,0},{3,1},{4,6},{5,7},{6,4},{7,5},{8,10},{9,11},{10,... | collective-permute-start | bytes 3145736 | tf_op jit(solution)/shard_map/out/ppermute | solution.py:42
  561.2 56.0 %collective-permute-start.40 = (bf16[2,128,2048]{2,1,0:T(8,128)(2,1)}, bf16[2,128,2048]{2,1,0:T(8,128)(2,1)}, u32[]{:S(2)}, u32[]{:S(2)}) collective-permute-start(bf16[2,128,2048]{2,1,0:T(8,128)(2,1)} %get-tuple-element.355), channel_id=1, source_target_pairs={{0,4},{4,0},{8,12},{12,8},{1,5},{5,1},{9,13},{13,9},{2,6},{6,2},{1... | collective-permute-start | bytes 3145736 | tf_op jit(solution)/shard_map/out/ppermute | solution.py:42
  601.9 63.7 %all-to-all-start.8 = ((bf16[4,256,1024]{2,1,0:T(8,128)(2,1)}), bf16[4,256,1024]{2,1,0:T(8,128)(2,1)}, u32[]{:S(2)}, u32[]{:S(2)}) async-start(bf16[4,256,1024]{2,1,0:T(8,128)(2,1)} %fusion.2), calls=%async_computation.8 | async-start | bytes 4194304 | tf_op jit(solution)/shard_map/up_grad_sp/all_to_all | solution.py:482
  606.4 174.4 %reduce-scatter.2.cloned.1.call-start = ((), (), s32[]{:S(2)}) async-start(), calls=%async_computation.14 | async-start | bytes 3538944 | tf_op jit(solution)/shard_map/reduce_scatter | solution.py:792
  622.8 51.7 %collective-permute-start.39 = (bf16[128,2048]{1,0:T(8,128)(2,1)}, bf16[128,2048]{1,0:T(8,128)(2,1)}, u32[]{:S(2)}, u32[]{:S(2)}) collective-permute-start(bf16[128,2048]{1,0:T(8,128)(2,1)} %get-tuple-element.369), channel_id=1, source_target_pairs={{0,4},{4,0},{8,12},{12,8},{1,5},{5,1},{9,13},{13,9},{2,6},{6,2},{1... | collective-permute-start | bytes 1572872 | tf_op jit(solution)/shard_map/out/ppermute | solution.py:42
  629.7 44.9 %collective-permute-start.42 = (bf16[128,2048]{1,0:T(8,128)(2,1)}, bf16[128,2048]{1,0:T(8,128)(2,1)}, u32[]{:S(2)}, u32[]{:S(2)}) collective-permute-start(bf16[128,2048]{1,0:T(8,128)(2,1)} %get-tuple-element.371), channel_id=1, source_target_pairs={{0,2},{1,3},{2,0},{3,1},{4,6},{5,7},{6,4},{7,5},{8,10},{9,11},{10,... | collective-permute-start | bytes 1572872 | tf_op jit(solution)/shard_map/out/ppermute | solution.py:42
  637.7 44.5 %collective-permute-start.43 = (bf16[4,2,32,2048]{3,2,1,0:T(8,128)(2,1)}, bf16[4,2,32,2048]{3,2,1,0:T(8,128)(2,1)}, u32[]{:S(2)}, u32[]{:S(2)}) collective-permute-start(bf16[4,2,32,2048]{3,2,1,0:T(8,128)(2,1)} %bitcast.293), channel_id=1, source_target_pairs={{0,16},{16,0},{1,17},{17,1},{2,18},{18,2},{3,19},{19,3},{4,20},{20... | collective-permute-start | bytes 3145736 | tf_op jit(solution)/shard_map/proj_grad_dp/ppermute | solution.py:42
  705.3 41.9 %all-to-all-start.10 = ((bf16[4,2,32,2048]{3,2,1,0:T(8,128)(2,1)}), bf16[4,2,32,2048]{3,2,1,0:T(8,128)(2,1)S(1)}, u32[]{:S(2)}, u32[]{:S(2)}) async-start(bf16[4,2,32,2048]{3,2,1,0:T(8,128)(2,1)} %fusion.17), calls=%async_computation.10 | async-start | bytes 2097152 | tf_op jit(solution)/shard_map/proj_grad_sp/all_to_all | solution.py:482
  710.4 41.3 %collective-permute-start.49 = (f32[2,256]{1,0:T(2,128)S(1)}, f32[2,256]{1,0:T(2,128)S(1)}, u32[]{:S(2)}, u32[]{:S(2)}) collective-permute-start(f32[2,256]{1,0:T(2,128)S(1)} %get-tuple-element.405), channel_id=1, source_target_pairs={{0,12},{4,8},{8,4},{12,0},{1,13},{5,9},{9,5},{13,1},{2,14},{6,10},... | collective-permute-start | bytes 6152 | tf_op jit(solution)/shard_map/gains_sp/ppermute | solution.py:42
  714.3 37.4 %collective-permute-start.48 = (f32[2,256]{1,0:T(2,128)S(1)}, f32[2,256]{1,0:T(2,128)S(1)}, u32[]{:S(2)}, u32[]{:S(2)}) collective-permute-start(f32[2,256]{1,0:T(2,128)S(1)} %get-tuple-element.404), channel_id=1, source_target_pairs={{0,8},{4,12},{8,0},{12,4},{1,9},{5,13},{9,1},{13,5},{2,10},{6,14},... | collective-permute-start | bytes 6152 | tf_op jit(solution)/shard_map/gains_sp/ppermute | solution.py:42
  714.3 37.4 %collective-permute-start.47 = (f32[2,256]{1,0:T(2,128)S(1)}, f32[2,256]{1,0:T(2,128)S(1)}, u32[]{:S(2)}, u32[]{:S(2)}) collective-permute-start(f32[2,256]{1,0:T(2,128)S(1)} %get-tuple-element.403), channel_id=1, source_target_pairs={{0,4},{4,0},{8,12},{12,8},{1,5},{5,1},{9,13},{13,9},{2,6},{6,2},{1... | collective-permute-start | bytes 6152 | tf_op jit(solution)/shard_map/gains_sp/ppermute | solution.py:42
  (92 other events, 1297.6 us)
Sparse Core Ops, SparseCore 0:
  19.1 88.8 all-gather.1
  639.0 97.1 reduce-scatter.1

commit v3 on v2

--- a/solution.py
+++ b/solution.py
@@ -141,7 +141,8 @@
         name="attend",
     )(projected, cosine, sine)
 
-def attend_back_kernel(tile, qkv_ref, grad_ref, log_ref, cos_ref, sin_ref, out_ref, q_s, k_s, v_s, kt_s, g_s, dk_s, dv_s, dq_s):
+def attend_back_kernel(tile, qkv_ref, grad_ref, log_ref, cos_ref, sin_ref, *refs):
+    out_ref, q_s, k_s, v_s, kt_s, g_s, dk_s, dv_s, dq_s = refs[-9:]
     length = qkv_ref.shape[0]
     for b in range(QPK // 2):
         lanes = slice(b * LANES, (b + 1) * LANES)
@@ -191,19 +192,23 @@
     block = jnp.concatenate([dk_s[...], dv_s[...]], axis=1)
     out_ref[:, QPK * HD :] = turn(block, k_cos, -k_sin).astype(BF)
 
-def attend_back(qkv, grad, log, cosine, sine, groups, tile=256):
+def attend_back(qkv, grad, log, cosine, sine, groups, group, earlier, tile=256):
     length, columns = qkv.shape[0], qkv.shape[1] // groups
     qw = QPK * HD
     table = pl.BlockSpec((length, LANES), lambda g: (0, 0))
+    held = () if earlier is None else (earlier,)
     return pl.pallas_call(
         functools.partial(attend_back_kernel, tile),
-        grid=(groups,),
+        grid=(1,),
         in_specs=[
-            pl.BlockSpec((length, columns), lambda g: (0, g)),
-            pl.BlockSpec((length, qw), lambda g: (0, g)),
-            pl.BlockSpec((1, QPK, length), lambda g: (g, 0, 0)),
-            table, table],
-        out_specs=pl.BlockSpec((length, columns), lambda g: (0, g)),
+            pl.BlockSpec((length, columns), lambda g: (0, group)),
+            pl.BlockSpec((length, qw), lambda g: (0, group)),
+            pl.BlockSpec((1, QPK, length), lambda g: (group, 0, 0)),
+            table,
+            table,
+        ]
+        + [pl.BlockSpec(memory_space=pl.ANY)] * len(held),
+        out_specs=pl.BlockSpec((length, columns), lambda g: (0, group)),
         out_shape=jax.ShapeDtypeStruct((length, groups * columns), BF),
         scratch_shapes=[
             pltpu.VMEM((QPK, length, HD), BF),
@@ -215,10 +220,12 @@
             pltpu.VMEM((length, HD), F32),
             pltpu.VMEM((qw, length), F32),
         ],
+        input_output_aliases={5: 0} if held else {},
         compiler_params=pltpu.CompilerParams(vmem_limit_bytes=VMEM_LIMIT),
         cost_estimate=HEAVY,
         name="attend_back",
-    )(qkv, grad, log, cosine, sine)
+    )(qkv, grad, log, cosine, sine, *held)
+
 
 def tables(length):
     half = HD // 2
@@ -312,12 +319,14 @@
     )(at, rows, gate, *ups)
 
 
-def ffn_back_kernel(tf, parts, at_ref, dy_ref, a_ref, b_ref, d_ref, *refs):
-    weights, (dg_ref, du_ref, dn_ref) = refs[: 2 * parts], refs[-3:]
+def ffn_back_kernel(tf, downs, parts, at_ref, dy_ref, a_ref, b_ref, *refs):
+    d_refs, weights, (dg_ref, du_ref, dn_ref) = refs[:downs], refs[downs : downs + 2 * parts], refs[-3:]
     dy = dy_ref[...]
-    for j in range(d_ref.shape[0] // tf):
+    each = d_refs[0].shape[0]
+    for j in range(downs * each // tf):
         c = slice(j * tf, (j + 1) * tf)
-        dh = mm_nt(dy, d_ref[c, :])
+        row = j * tf % each
+        dh = mm_nt(dy, d_refs[j * tf // each][row : row + tf, :])
         dg_ref[:, c] = (dh * b_ref[:, c]).astype(BF)
         du_ref[:, c] = (dh * a_ref[:, c]).astype(BF)
     depth = weights[0].shape[0]
@@ -326,7 +335,7 @@
         dn_ref[:, pl.ds(pl.multiple_of(at_ref[k] * depth, depth), depth)] = part.astype(BF)
 
 
-def ffn_back(at, dy, a, b, down_w, gates, ups, part, earlier, tm=256, tf=256):
+def ffn_back(at, dy, a, b, downs, gates, ups, part, earlier, tm=256, tf=256):
     m, k = dy.shape
     f = gates[0].shape[1]
     parts = len(gates)
@@ -339,9 +348,10 @@
 
     held = () if earlier is None else earlier
     return pl.pallas_call(
-        functools.partial(ffn_back_kernel, tf, parts),
+        functools.partial(ffn_back_kernel, tf, len(downs), parts),
         grid=(steps,),
-        in_specs=[pl.BlockSpec(memory_space=pltpu.SMEM), rows, inner, inner, whole((f, k))]
+        in_specs=[pl.BlockSpec(memory_space=pltpu.SMEM), rows, inner, inner]
+        + [whole((f // len(downs), k))] * len(downs)
         + [whole((k // parts, f))] * (2 * parts)
         + [pl.BlockSpec(memory_space=pl.ANY)] * len(held),
         out_specs=[inner, inner, pl.BlockSpec((tm, k), lambda i: (i, 0))],
@@ -350,11 +360,11 @@
             jax.ShapeDtypeStruct((m, f), BF),
             jax.ShapeDtypeStruct((m // 2, k), BF),
         ],
-        input_output_aliases={5 + 2 * parts + i: i for i in range(len(held))},
+        input_output_aliases={4 + len(downs) + 2 * parts + i: i for i in range(len(held))},
         compiler_params=pltpu.CompilerParams(vmem_limit_bytes=VMEM_LIMIT),
         cost_estimate=HEAVY,
         name="ffn_back",
-    )(at, dy, a, b, down_w, *gates, *ups, *held)
+    )(at, dy, a, b, *downs, *gates, *ups, *held)
 
 
 def project_kernel(pieces, at_ref, *refs):
@@ -416,6 +426,53 @@
     )(at, *pieces, weights)
 
 
+def out_kernel(hid_ref, *refs):
+    weights, out_ref = refs[:-1], refs[-1]
+    each = weights[0].shape[0]
+    total = None
+    for k, weight in enumerate(weights):
+        part = mm(hid_ref[:, k * each : (k + 1) * each], weight[...])
+        total = part if total is None else total + part
+    out_ref[...] = total.astype(BF)
+
+
+def out_rows(hidden, weights, tm=256):
+    m, f = hidden.shape
+    each, d = weights[0].shape
+    return pl.pallas_call(
+        out_kernel,
+        grid=(m // tm,),
+        in_specs=[pl.BlockSpec((tm, f), lambda i: (i, 0))]
+        + [pl.BlockSpec((each, d), lambda i: (0, 0), pipeline_mode=pl.Buffered(1))] * len(weights),
+        out_specs=pl.BlockSpec((tm, d), lambda i: (i, 0)),
+        out_shape=jax.ShapeDtypeStruct((m, d), BF),
+        compiler_params=pltpu.CompilerParams(vmem_limit_bytes=VMEM_LIMIT),
+        cost_estimate=LIGHT,
+        name="out_rows",
+    )(hidden, *weights)
+
+
+def join_kernel(count, *refs):
+    rows = refs[0].shape[0]
+    for k in range(count):
+        refs[count][k * rows : (k + 1) * rows] = refs[k][...]
+
+
+def join(pieces):
+    rows, width = pieces[0].shape
+    count = len(pieces)
+    tile = width // 4
+    return pl.pallas_call(
+        functools.partial(join_kernel, count),
+        grid=(width // tile,),
+        in_specs=[pl.BlockSpec((rows, tile), lambda i: (0, i))] * count,
+        out_specs=pl.BlockSpec((rows * count, tile), lambda i: (0, i)),
+        out_shape=jax.ShapeDtypeStruct((rows * count, width), pieces[0].dtype),
+        compiler_params=pltpu.CompilerParams(vmem_limit_bytes=VMEM_LIMIT),
+        name="join",
+    )(*pieces)
+
+
 def collect_kernel(put, parts, at_ref, *refs):
     for k in range(parts):
         put(refs[k], refs[parts], at_ref[k])
@@ -458,6 +515,7 @@
 class Chain:
     def __init__(self):
         self.token = None
+        self.fences = []
         self.begun = []
 
     def now(self, value):
@@ -482,17 +540,16 @@
             return lax.all_to_all(blocks, SP, 0, 0, tiled=True)
 
     def fence(self, *values):
-        seed = self.token
-        if seed is None or seed.shape != (8, LANES):
-            seed = jnp.zeros((8, LANES), F32) if seed is None else after(jnp.zeros((8, LANES), F32), seed)
-        self.passed(fence_call(after(seed, *self.begun, *values)))
+        self.passed(fence_call(after(jnp.zeros((8, LANES), F32), self.token, *self.fences, *self.begun, *values)
+            if self.token is not None else after(jnp.zeros((8, LANES), F32), *self.begun, *values)))
+        self.fences = [self.token]
 
     def passed(self, token):
         self.token = token
         self.begun = []
 
     def gate(self, value):
-        return after(value, *self.begun) if self.begun else value
+        return after(value, self.token, *self.begun)
 
 
 def order_units(pieces, at, sp):
@@ -690,24 +747,28 @@
 
     dy_rows = now(dy_rows)
     dy_gather = Gather(chain, dy_rows.reshape(-1, width), "dy")
-    down_own = chain.start_all(after(down_blocks, dy_rows), "down_sp")
+    fence()
+    cut = units // 4
+    down_own = [chain.start_all(after(down_blocks[:, :cut], dy_rows), "down_sp")]
     gates = flat([gate_own] + gate_got)
     first, *others = gather.result()
     gate, normed_all = gate_rows(at, [chain.gate(first)] + others, gates)
     chain.passed(gate)
 
+    ups = flat([up_own] + [chain.take(v) for v in up_got])
+    down_own[0] = now(down_own[0])
+    down_got = [chain.start_dp(down_own[0], "down_dp")]
+    down_own.append(chain.start_all(after(down_blocks[:, cut:], down_own[0]), "down_sp"))
     dy_gather.second()
-    ups = flat([up_own] + [chain.take(v) for v in up_got])
+    dy_gather.near_core()
     hidden, activated, slope = up_rows(at, chain.gate(normed_all), gate, ups)
     chain.passed(hidden)
 
-    dy_gather.near_core()
+    down_own[1] = now(down_own[1])
+    down_got.append(chain.start_dp(down_own[1], "down_dp"))
     dy_gather.far_core()
     fence()
-    down_own = now(down_own)
-    down_got = chain.start_dp(down_own, "down_dp")
-    fence()
-    dy_all = jnp.concatenate(dy_gather.result(), axis=0)
+    dy_all = join(dy_gather.result())
     down_part = mm_tn(hidden, dy_all).astype(BF)
     down_part = down_part.reshape(units // 2, nx, nz, unit_rows, width).transpose(1, 2, 0, 3, 4)
 
@@ -722,26 +783,26 @@
 
     down_dp = to_dp(down_part, "down_grad_dp")
     fence()
-
-    down_all = order_units([down_own] + [now(v) for v in down_got], at, nz)
+    downs = [
+        order_units([own] + [now(v) for v in got], at, nz) for own, got in zip(down_own, down_got)
+    ]
+
     grad_gate, grad_up, grad_other = ffn_back(
-        at, dy_all, activated, slope, down_all, gates, ups, 1, None
+        at, chain.gate(dy_all), activated, slope, downs, gates, ups, 1, None
     )
     chain.passed(grad_other)
     reduce = Reduce(chain, grad_other, "normed_grad")
     grad_gate, grad_up, grad_mine = ffn_back(
-        at, chain.gate(dy_all), activated, slope, down_all, gates, ups, 0, (grad_gate, grad_up)
+        at, chain.gate(dy_all), activated, slope, downs, gates, ups, 0, (grad_gate, grad_up)
     )
     chain.passed(grad_mine)
 
     reduce.first(grad_mine)
     fence()
-
     gate_part = mm_tn(now(normed_all), grad_gate).astype(BF)
     gate_part = gate_part.reshape(nx, nz, row_block, feed_columns)
     gate_dp = to_dp(gate_part, "gate_grad_dp")
     fence()
-
     reduce.second()
     fence()
     down_moved = chain.start_all(sum_dp(down_part, down_dp), "down_grad_sp")
@@ -764,10 +825,8 @@
     gate_sum = sum_dp(gate_part, gate_dp)
     gate_moved = chain.start_all(after(gate_sum, down_moved), "gate_grad_sp")
     fence()
-    out_part = mm(now(hidden), down_all).astype(BF)
-    out_rows = out_part.shape[0] // 2
-    out_reduce = Reduce(chain, out_part[out_rows:], "out")
-    fence()
+    out_part = out_rows(now(hidden), downs)
+    fence(out_part)
     rows_y = now(rows_y)
     rows_yc = start(rows_y, "tp", 1, "rows_yc")
     fence()
@@ -775,23 +834,31 @@
     grad_rows, grad_context = context_grad(
         at_tp, [rows_mine, now(rows_c), rows_y, now(rows_yc)], proj_all
     )
-    out_reduce.first(out_part[:out_rows])
-    grad_projected = attend_back(qkv, chain.gate(grad_context), logs, cosine, sine, groups)
-    chain.passed(grad_projected)
-
-    gate_moved = chain.take(gate_moved)
-    up_sum = sum_dp(up_part, up_dp)
-    up_moved = chain.start_all(after(up_sum, gate_moved), "up_grad_sp")
-    dn_part = mm_nt(grad_projected, qkv_all).astype(BF).reshape(nz, 2, 2, span, width)
-    dn_core = start(pick(dn_part, 1 - c, 2), "tp", 1, "dn_c")
-    fence()
-    dn_sum = (pick(dn_part, c, 2).astype(F32) + now(dn_core).astype(F32)).astype(BF)
-    dn_y = start(pick(dn_sum, 1 - y, 1), "tp", 2, "dn_y")
-    fence()
-    qkv_part = mm_tn(now(normed_one), grad_projected).astype(BF)
+    rows_half = out_part.shape[0] // 2
+    out_reduce = Reduce(chain, out_part[rows_half:], "out")
+    fence(grad_context)
+    out_reduce.first(out_part[:rows_half])
+    grad_projected = None
+    for group in range(groups):
+        grad_projected = attend_back(
+            qkv, chain.gate(grad_context), logs, cosine, sine, groups, group, grad_projected
+        )
+        chain.passed(grad_projected)
+        if group == 0:
+            gate_moved = chain.take(gate_moved)
+            up_sum = sum_dp(up_part, up_dp)
+            up_moved = chain.start_all(after(up_sum, gate_moved), "up_grad_sp")
+
+    qkv_part = mm_tn(normed_one, now(grad_projected)).astype(BF)
     qkv_grad = lax.psum_scatter(qkv_part, ("dp",) + SP, tiled=True)
     out_reduce.second()
     fence(qkv_part)
+    dn_part = mm_nt(now(grad_projected), qkv_all).astype(BF).reshape(nz, 2, 2, span, width)
+    dn_core = start(pick(dn_part, 1 - c, 2), "tp", 1, "dn_c")
+    fence()
+    dn_sum = (pick(dn_part, c, 2).astype(F32) + now(dn_core).astype(F32)).astype(BF)
+    dn_y = start(pick(dn_sum, 1 - y, 1), "tp", 2, "dn_y")
+    fence()
     proj_part = mm_tn(context, now(grad_rows)).astype(BF)
     proj_part = proj_part.reshape(groups, nx, nz, proj_rows, width).transpose(1, 2, 0, 3, 4)
     proj_dp = to_dp(proj_part, "proj_grad_dp")
@@ -807,6 +874,7 @@
     input_delta = (back_two + back_one).astype(BF).reshape(nz, span, width)
     gains_part = jnp.stack([gain_one_part, gain_two_part])
     gains_c = start(gains_part, "tp", 1, "gains_c")
+    fence(input_delta)
     up_moved = chain.take(up_moved)
     input_moved = chain.start_all(after(input_delta, up_moved), "input_sp")
     fence()
@@ -816,35 +884,38 @@
         parity = [sum(blocks[i] for i in range(p, nz, 2)) for p in range(2)]
         return jnp.concatenate(parity, axis=axis)
 
+    block_delta = (attn_mine + out_reduce.result()).astype(BF).reshape(nz, span, width)
+    proj_sum = sum_dp(proj_part, proj_dp)
     gains_part = gains_part + now(gains_c)
     gains_y = start(gains_part, "tp", 2, "gains_y")
-    block_delta = (attn_mine + out_reduce.result()).astype(BF).reshape(nz, span, width)
     down_grad = halves(now(down_moved), 0)
     down_new, down_first_new, down_second_new = adamw(
-        down_weight, down_grad, down_first, down_second, DOWN_RATE, WEIGHT_DECAY
-    )
-    proj_sum = sum_dp(proj_part, proj_dp)
-    fence(block_delta, down_new, proj_sum)
+        now(down_weight), down_grad, down_first, down_second, DOWN_RATE, WEIGHT_DECAY
+    )
+    fence(proj_sum, down_new, block_delta)
+
+    input_moved = chain.take(input_moved)
+    proj_moved = chain.start_all(after(proj_sum, input_moved), "proj_grad_sp")
+    fence()
 
     gains_part = (gains_part + now(gains_y)).reshape(2, nx, nz, row_block).transpose(1, 2, 0, 3)
     gains_dp = to_dp(gains_part, "gains_dp")
-    feed_grad = jnp.stack([halves(gate_moved, 1), halves(up_moved, 1)])
+    feed_grad = jnp.stack([halves(now(gate_moved), 1), halves(now(up_moved), 1)])
     feed_new, feed_first_new, feed_second_new = adamw(
         now(feed_weight), feed_grad, feed_first, feed_second, FEED_RATE, WEIGHT_DECAY
     )
-    input_moved = chain.take(input_moved)
-    proj_moved = chain.start_all(after(proj_sum, input_moved), "proj_grad_sp")
-    fence(feed_new)
-
+    input_grad = now(cotangent).astype(F32) + input_moved.astype(F32)
+    fence(feed_new, input_grad)
+
+    proj_moved = chain.take(proj_moved)
+    block_moved = chain.start_all(after(block_delta, proj_moved), "block_sp")
     gains_sum = pick(gains_part, xi, 0)
     for block in gains_dp:
         gains_sum = gains_sum + now(block)
     gains_moved = {k: start(pick(gains_sum, zi ^ k, 0), SP, k, "gains_sp") for k in (1, 2, 3)}
-    input_grad = cotangent.astype(F32) + input_moved.astype(F32)
-    proj_moved = chain.take(proj_moved).astype(F32)
-    proj_grad = proj_moved[0] + proj_moved[1] + proj_moved[2] + proj_moved[3]
-    block_moved = chain.start_all(after(block_delta, proj_moved), "block_sp")
-    fence(input_grad)
+    fence()
+
+    proj_grad = sum(now(proj_moved)[i].astype(F32) for i in range(nz))
     qkv_grad = now(qkv_grad).reshape(row_block, groups, columns).transpose(1, 0, 2)
     qkv_grad = after(qkv_grad).astype(F32)
     gains_grad = pick(gains_sum, zi, 0)

time: 800 us -> 767 us (0.959)
  waiting for transfers between devices: 267 us -> 238 us
  Pallas kernels: 159 us -> 184 us
  other arithmetic: 105 us -> 88.4 us
  matrix products: 65.3 us -> 52.3 us
  starting transfers between devices: 103 us -> 114 us
  local copies, waits for them, and re-layouts: 76.9 us -> 66.9 us
    all_to_all x12 -> x13, waiting for transfers between devices: 114 us -> 56 us  [start_all(): return lax.all_to_all(blocks, SP, 0, 0, tiled=True)]
    ppermute x50 -> x51, waiting for transfers between devices: 152 us -> 182 us  [swap(): lax.ppermute(value, axis, [(i, i ^ mask) for i in range(lax.axis_size(axi...]
    pallas_call x3 -> x6, Pallas kernels: 71.1 us -> 94.9 us  [the longest x2 42.1 us: ffn_back(): pl.pallas_call(functools.partial(ffn_back_kernel, tf, len(downs), parts),...]
    dot_general x8 -> x7, matrix products: 65.3 us -> 52.3 us  [dot(): lax.dot_general(left, right, ((dims[0], dims[1]), ((), ())), preferred_el...]
    all_to_all x12 -> x13, starting transfers between devices: 56.2 us -> 62.8 us  [start_all(): return lax.all_to_all(blocks, SP, 0, 0, tiled=True)]
    ppermute x50 -> x51, starting transfers between devices: 46.5 us -> 50.9 us  [swap(): lax.ppermute(value, axis, [(i, i ^ mask) for i in range(lax.axis_size(axi...]
    unnamed x133 -> x163, local copies, waits for them, and re-layouts: 37.8 us -> 34.9 us
  transfers between devices with their start and end apart: 64 -> 66, of which waited for: 20 -> 20; matrix products, arithmetic and copies ran while one was open for 28% -> 24% of each run, Pallas kernels for 20% -> 24%
where the time goes in v3:
time: 767 us; the launch traced here: 759 us
  waiting for transfers between devices  238 us (31%)
  Pallas kernels  184 us (24%)
  starting transfers between devices  114 us (15%)
  other arithmetic  88.4 us (12%)
  local copies, waits for them, and re-layouts  66.9 us (9%)
  matrix products  52.3 us (7%)
  between operations  15.6 us (2%)
    ppermute x51, waiting for transfers between devices, swap(): lax.ppermute(value, axis, [(i, i ^ mask) for i in range(lax.axis_size(axi...  182 us
    all_to_all x13, starting transfers between devices, start_all(): return lax.all_to_all(blocks, SP, 0, 0, tiled=True)  62.8 us
    all_to_all x13, waiting for transfers between devices, start_all(): return lax.all_to_all(blocks, SP, 0, 0, tiled=True)  56 us
    dot_general x7, matrix products, dot(): lax.dot_general(left, right, ((dims[0], dims[1]), ((), ())), preferred_el...  52.3 us
    ppermute x51, starting transfers between devices, swap(): lax.ppermute(value, axis, [(i, i ^ mask) for i in range(lax.axis_size(axi...  50.9 us
    pallas_call x2, Pallas kernels, ffn_back(): pl.pallas_call(functools.partial(ffn_back_kernel, tf, len(downs), parts),...  42.1 us
    unnamed x163, local copies, waits for them, and re-layouts  34.9 us
    pallas_call x2, Pallas kernels, attend_back(): pl.pallas_call(functools.partial(attend_back_kernel, tile), grid=(1,), in...  31.7 us
  transfers between devices with their start and end apart: 66, of which 20 were waited for; matrix products, arithmetic and copies ran while one was open for 24% of the time, Pallas kernels for 24%

profile of v3, /device:TPU:0, one launch (start us, length us, event | category | flops | bytes accessed | tf_op | source)
XLA Modules:
  0.0 758.8 jit_solution(1848198541884189800)
XLA Ops:
  7.2 6.3 all-to-all-start
  39.2 12.0 %collective-permute-done.2 = bf16[2,256]{1,0:T(2,128)(2,1)S(1)} collective-permute-done((bf16[2,256]{1,0:T(2,128)(2,1)S(1)}, bf16[2,256]{1,0:T(2,128)(2,1)S(1)}, u32[]{:S(2)}, u32[]{:S(2)}) %collective-permute-start.2) | collective-permute-done | bytes 1056 | tf_op jit(solution)/shard_map/gains_sp/ppermute | solution.py:42
  58.8 19.9 %collective-permute-done.4.refs_2_ = bf16[4,64,2048]{2,1,0:T(8,128)(2,1)} collective-permute-done((bf16[4,64,2048]{2,1,0:T(8,128)(2,1)S(1)}, bf16[4,64,2048]{2,1,0:T(8,128)(2,1)}, u32[]{:S(2)}, u32[]{:S(2)}) %collective-permute-start.4) | collective-permute-done | bytes 1048608 | tf_op jit(solution)/shard_map/x_y/ppermute | solution.py:42
  83.2 20.5 %all-to-all-done.1.refs_0_ = bf16[4,2,32,2048]{3,2,1,0:T(8,128)(2,1)} async-done(((bf16[4,2,32,2048]{3,2,1,0:T(8,128)(2,1)}), bf16[4,2,32,2048]{3,2,1,0:T(8,128)(2,1)}, u32[]{:S(2)}, u32[]{:S(2)}) %all-to-all-start.1) | async-done | bytes 1048608 | tf_op jit(solution)/shard_map/proj_sp/all_to_all | solution.py:540
  109.1 8.7 %project.1 = (bf16[1024,2048]{1,0:T(8,128)(2,1)}, f32[1024,768]{1,0:T(8,128)}) custom-call(s32[4]{0:T(128)} %pad_add_fusion.at_ref, bf16[4,64,2048]{2,1,0:T(8,128)(2,1)} %copy-done.9, bf16[4,64,2048]{2,1,0:T(8,128)(2,1)} %collective-permute-done.refs_1_, bf16[4,64,2048]{2,1,0:T(8,128)(2,1)} %collective-permute-done.4.refs_2_, ...), custom_call_target="tpu_custom_call" | custom-call | flops 4294967296 | bytes 1048576 | tf_op jit(solution)/shard_map/project/pallas_call | solution.py:385
  117.9 21.0 %attend.1 = (bf16[1024,768]{1,0:T(8,128)(2,1)}, bf16[1024,512]{1,0:T(8,128)(2,1)}, f32[2,4,1024]{2,1,0:T(4,128)}) custom-call(f32[1024,768]{1,0:T(8,128)} %get-tuple-element.264.p_ref, f32[1024,128]{1,0:T(8,128)} %get-tuple-element.518.cos_ref, f32[1024,128]{1,0:T(8,128)} %get-tuple-element.519.sin_ref), custom_call_target="tpu_custom_call" | custom-call | flops 68719476736 | bytes 1048576 | tf_op jit(solution)/shard_map/attend/pallas_call | solution.py:119
  162.1 17.4 %collective-permute-done.9 = bf16[4,64,2048]{2,1,0:T(8,128)(2,1)} collective-permute-done((bf16[4,64,2048]{2,1,0:T(8,128)(2,1)S(1)}, bf16[4,64,2048]{2,1,0:T(8,128)(2,1)}, u32[]{:S(2)}, u32[]{:S(2)}) %collective-permute-start.9) | collective-permute-done | bytes 1048608 | tf_op jit(solution)/shard_map/attn_y/ppermute | solution.py:42
  187.1 18.8 %collective-permute-done.11 = bf16[128,2048]{1,0:T(8,128)(2,1)S(1)} collective-permute-done((bf16[128,2048]{1,0:T(8,128)(2,1)S(1)}, bf16[128,2048]{1,0:T(8,128)(2,1)S(1)}, u32[]{:S(2)}, u32[]{:S(2)}) %collective-permute-start.11) | collective-permute-done | bytes 524320 | tf_op jit(solution)/shard_map/normed/ppermute | solution.py:42
  218.0 14.8 %collective-permute-done.13 = bf16[256,2048]{1,0:T(8,128)(2,1)S(1)} collective-permute-done((bf16[256,2048]{1,0:T(8,128)(2,1)}, bf16[256,2048]{1,0:T(8,128)(2,1)S(1)}, u32[]{:S(2)}, u32[]{:S(2)}) %collective-permute-start.13) | collective-permute-done | bytes 1048608 | tf_op jit(solution)/shard_map/normed/ppermute | solution.py:42
  232.9 14.2 %collective-permute-done.12 = bf16[256,2048]{1,0:T(8,128)(2,1)} collective-permute-done((bf16[256,2048]{1,0:T(8,128)(2,1)S(1)}, bf16[256,2048]{1,0:T(8,128)(2,1)}, u32[]{:S(2)}, u32[]{:S(2)}) %collective-permute-start.12) | collective-permute-done | bytes 1048608 | tf_op jit(solution)/shard_map/normed/ppermute | solution.py:42
  261.0 19.2 %gate_rows.1 = (f32[2048,1024]{1,0:T(8,128)}, bf16[2048,2048]{1,0:T(8,128)(2,1)}) custom-call(s32[2]{0:T(128)} %pad_add_fusion.1.at_ref, bf16[512,2048]{1,0:T(8,128)(2,1)} %pad_maximum_fusion.1.refs_0_, bf16[512,2048]{1,0:T(8,128)(2,1)} %constant_dynamic-update-slice_fusion.refs_1_, bf16[512,2048]{1,0:T(8,128)(2,1)} %collective-permute-done.15.refs_2_, ...), custom_call_target="tpu_custom_call" | custom-call | flops 68719476736 | bytes 1048576 | tf_op jit(solution)/shard_map/gate_rows/pallas_call | solution.py:265
  280.2 7.9 %collective-permute-done.19 = bf16[128,2048]{1,0:T(8,128)(2,1)S(1)} collective-permute-done((bf16[128,2048]{1,0:T(8,128)(2,1)S(1)}, bf16[128,2048]{1,0:T(8,128)(2,1)S(1)}, u32[]{:S(2)}, u32[]{:S(2)}) %collective-permute-start.19) | collective-permute-done | bytes 524320 | tf_op jit(solution)/shard_map/dy/ppermute | solution.py:42
  300.1 24.4 %up_rows.1 = (bf16[2048,1024]{1,0:T(8,128)(2,1)}, f32[2048,1024]{1,0:T(8,128)}, f32[2048,1024]{1,0:T(8,128)}) custom-call(s32[2]{0:T(128)} %pad_add_fusion.1.at_ref, bf16[2048,2048]{1,0:T(8,128)(2,1)} %get-tuple-element.357.rows_ref, f32[2048,1024]{1,0:T(8,128)} %get-tuple-element.307.gate_ref, bf16[1024,1024]{1,0:T(8,128)(2,1)} %bitcast.34.refs_0_.refs_4_, ...), custom_call_target="tpu_custom_call" | custom-call | flops 68719476736 | bytes 1048576 | tf_op jit(solution)/shard_map/up_rows/pallas_call | solution.py:301
  324.5 6.1 collective-permute-done.20
  339.7 7.1 join.1.dy_ref
  346.8 11.4 %convolution_convert_fusion = bf16[1024,2048]{1,0:T(8,128)(2,1)S(1)} fusion(bf16[2048,1024]{1,0:T(8,128)(2,1)S(1)} %copy-done.44, bf16[2048,2048]{1,0:T(8,128)(2,1)} %join.1.dy_ref), kind=kOutput, calls=%fused_computation.17 | convolution fusion | flops 8592031744 | bytes 16777216 | tf_op jit(solution)/shard_map/dot_general | solution.py:50
  369.0 21.0 %ffn_back.2 = (bf16[2048,1024]{1,0:T(8,128)(2,1)}, bf16[2048,1024]{1,0:T(8,128)(2,1)}, bf16[1024,2048]{1,0:T(8,128)(2,1)}) custom-call(s32[2]{0:T(128)} %pad_add_fusion.1.at_ref, bf16[2048,2048]{1,0:T(8,128)(2,1)} %join.1.dy_ref, f32[2048,1024]{1,0:T(8,128)} %get-tuple-element.331.a_ref, f32[2048,1024]{1,0:T(8,128)} %get-tuple-element.332.b_ref, ...), custom_call_target="tpu_custom_call" | custom-call | flops 68719476736 | bytes 1048576 | tf_op jit(solution)/shard_map/ffn_back/pallas_call | solution.py:350
  390.0 21.1 %ffn_back.3 = (bf16[2048,1024]{1,0:T(8,128)(2,1)}, bf16[2048,1024]{1,0:T(8,128)(2,1)}, bf16[1024,2048]{1,0:T(8,128)(2,1)}) custom-call(s32[2]{0:T(128)} %pad_add_fusion.1.at_ref, bf16[2048,2048]{1,0:T(8,128)(2,1)} %join.1.dy_ref, f32[2048,1024]{1,0:T(8,128)} %get-tuple-element.331.a_ref, ...), custom_call_target="tpu_custom_call", output_to_operand_aliasing={{0}: (10, {}), {1}: (11, {})} | custom-call | flops 68719476736 | bytes 1048576 | tf_op jit(solution)/shard_map/ffn_back/pallas_call | solution.py:350
  418.9 11.6 %convolution_convert_fusion.4 = bf16[2048,1024]{1,0:T(8,128)(2,1)S(1)} fusion(bf16[2048,2048]{1,0:T(8,128)(2,1)} %get-tuple-element.357.rows_ref, bf16[2048,1024]{1,0:T(8,128)(2,1)S(1)} %copy-done.77), kind=kOutput, calls=%fused_computation.21 | convolution fusion | flops 8592031744 | bytes 16777216 | tf_op jit(solution)/shard_map/dot_general | solution.py:50
  433.9 7.7 %collective-permute-done.28 = bf16[2,128,2048]{2,1,0:T(8,128)(2,1)S(1)} collective-permute-done((bf16[2,128,2048]{2,1,0:T(8,128)(2,1)S(1)}, bf16[2,128,2048]{2,1,0:T(8,128)(2,1)S(1)}, u32[]{:S(2)}, u32[]{:S(2)}) %collective-permute-start.28) | collective-permute-done | bytes 1048608 | tf_op jit(solution)/shard_map/normed_grad/ppermute | solution.py:42
  455.8 12.7 %convolution_convert_fusion.3 = bf16[2048,1024]{1,0:T(8,128)(2,1)S(1)} fusion(bf16[2048,2048]{1,0:T(8,128)(2,1)} %get-tuple-element.357.rows_ref, bf16[2048,1024]{1,0:T(8,128)(2,1)} %get-tuple-element.358), kind=kOutput, calls=%fused_computation.20 | convolution fusion | flops 8592031744 | bytes 16777216 | tf_op jit(solution)/shard_map/dot_general | solution.py:50
  472.3 25.2 %collective-permute-done.30 = bf16[128,2048]{1,0:T(8,128)(2,1)S(1)} collective-permute-done((bf16[128,2048]{1,0:T(8,128)(2,1)S(1)}, bf16[128,2048]{1,0:T(8,128)(2,1)S(1)}, u32[]{:S(2)}, u32[]{:S(2)}) %collective-permute-start.30) | collective-permute-done | bytes 524320 | tf_op jit(solution)/shard_map/normed_grad/ppermute | solution.py:42
  510.8 6.3 all-to-all-start.8
  517.1 14.1 %out_rows.1 = bf16[2048,2048]{1,0:T(8,128)(2,1)} custom-call(bf16[2048,1024]{1,0:T(8,128)(2,1)} %get-tuple-element.370.hid_ref, bf16[512,2048]{1,0:T(8,128)(2,1)} %bitcast.306, bf16[512,2048]{1,0:T(8,128)(2,1)} %bitcast.309), custom_call_target="tpu_custom_call" | custom-call | flops 4294967296 | bytes 1048576 | tf_op jit(solution)/shard_map/out_rows/pallas_call | solution.py:442
  537.9 6.8 context_grad.1
  554.4 15.8 %attend_back.2.refs_0_ = bf16[1024,768]{1,0:T(8,128)(2,1)} custom-call(bf16[1024,768]{1,0:T(8,128)(2,1)} %get-tuple-element.382.qkv_ref, bf16[1024,512]{1,0:T(8,128)(2,1)} %get-tuple-element.390.grad_ref, f32[2,4,1024]{2,1,0:T(4,128)} %get-tuple-element.385.log_ref, f32[1024,128]{1,0:T(8,128)} %get-tuple-element.518.cos_ref, ...), custom_call_target="tpu_custom_call" | custom-call | flops 68719476736 | bytes 1048576 | tf_op jit(solution)/shard_map/attend_back/pallas_call | solution.py:200
  578.8 15.9 %attend_back.3 = bf16[1024,768]{1,0:T(8,128)(2,1)} custom-call(bf16[1024,768]{1,0:T(8,128)(2,1)} %get-tuple-element.382.qkv_ref, bf16[1024,512]{1,0:T(8,128)(2,1)} %get-tuple-element.390.grad_ref, f32[2,4,1024]{2,1,0:T(4,128)} %get-tuple-element.385.log_ref, f32[1024,128]{1,0:T(8,128)} %get-tuple-element.518.cos_ref, ...), custom_call_target="tpu_custom_call", output_to_operand_aliasing={{}: (5, {})} | custom-call | flops 68719476736 | bytes 1048576 | tf_op jit(solution)/shard_map/attend_back/pallas_call | solution.py:200
  594.7 6.3 convolution_convert_fusion.5
  629.2 23.7 %collective-permute-done.42 = bf16[4,64,2048]{2,1,0:T(8,128)(2,1)S(1)} collective-permute-done((bf16[4,64,2048]{2,1,0:T(8,128)(2,1)S(1)}, bf16[4,64,2048]{2,1,0:T(8,128)(2,1)S(1)}, u32[]{:S(2)}, u32[]{:S(2)}) %collective-permute-start.42) | collective-permute-done | bytes 1048608 | tf_op jit(solution)/shard_map/dn_y/ppermute | solution.py:42
  677.2 11.5 %all-to-all-done.10 = bf16[4,64,2048]{2,1,0:T(8,128)(2,1)} async-done(((bf16[4,64,2048]{2,1,0:T(8,128)(2,1)}), bf16[4,64,2048]{2,1,0:T(8,128)(2,1)}, u32[]{:S(2)}, u32[]{:S(2)}) %all-to-all-start.10) | async-done | bytes 1048608 | tf_op jit(solution)/shard_map/input_sp/all_to_all | solution.py:540
  704.1 7.5 multiply_subtract_fusion
  731.2 18.9 %all-to-all-done.12 = bf16[4,64,2048]{2,1,0:T(8,128)(2,1)S(1)} async-done(((bf16[4,64,2048]{2,1,0:T(8,128)(2,1)}), bf16[4,64,2048]{2,1,0:T(8,128)(2,1)S(1)}, u32[]{:S(2)}, u32[]{:S(2)}) %all-to-all-start.12) | async-done | bytes 1048608 | tf_op jit(solution)/shard_map/block_sp/all_to_all | solution.py:540
  (394 shorter events, 287.6 us)
Async XLA Ops:
  7.2 45.7 %all-to-all-start = ((bf16[4,64,2048]{2,1,0:T(8,128)(2,1)}), bf16[4,64,2048]{2,1,0:T(8,128)(2,1)S(1)}, u32[]{:S(2)}, u32[]{:S(2)}) async-start(bf16[4,64,2048]{2,1,0:T(8,128)(2,1)} %param.17), calls=%async_computation | async-start | bytes 2097152 | tf_op jit(solution)/shard_map/x_sp/all_to_all | solution.py:540
  13.5 95.6 %all-gather.2.cloned.1.call-start = ((), (), s32[]{:S(2)}) async-start(), calls=%async_computation.14 | async-start | bytes 3538944 | tf_op jit(solution)/shard_map/all_gather | solution.py:671
  52.9 50.7 %all-to-all-start.1 = ((bf16[4,2,32,2048]{3,2,1,0:T(8,128)(2,1)}), bf16[4,2,32,2048]{3,2,1,0:T(8,128)(2,1)}, u32[]{:S(2)}, u32[]{:S(2)}) async-start(bf16[4,2,32,2048]{3,2,1,0:T(8,128)(2,1)} %tile.16), calls=%async_computation.1 | async-start | bytes 2097152 | tf_op jit(solution)/shard_map/proj_sp/all_to_all | solution.py:540
  58.8 50.3 %collective-permute-start = (bf16[4,64,2048]{2,1,0:T(8,128)(2,1)S(1)}, bf16[4,64,2048]{2,1,0:T(8,128)(2,1)}, u32[]{:S(2)}, u32[]{:S(2)}) collective-permute-start(bf16[4,64,2048]{2,1,0:T(8,128)(2,1)S(1)} %all-to-all-done.refs_0_), channel_id=1, source_target_pairs={{0,1},{1,0},{2,3},{3,2},{4,5},{5,4},{6,7},{7,6},{8,9},{9,8},{10,11... | collective-permute-start | bytes 3145736 | tf_op jit(solution)/shard_map/x_c/ppermute | solution.py:42
  103.6 50.4 %all-to-all-start.2 = ((bf16[4,256,1024]{2,1,0:T(8,128)(2,1)}), bf16[4,256,1024]{2,1,0:T(8,128)(2,1)}, u32[]{:S(2)}, u32[]{:S(2)}) async-start(bf16[4,256,1024]{2,1,0:T(8,128)(2,1)} %bitcast.11), calls=%async_computation.2 | async-start | bytes 4194304 | tf_op jit(solution)/shard_map/gate_sp/all_to_all | solution.py:540
  155.7 56.0 %all-to-all-start.3 = ((bf16[4,256,1024]{2,1,0:T(8,128)(2,1)}), bf16[4,256,1024]{2,1,0:T(8,128)(2,1)}, u32[]{:S(2)}, u32[]{:S(2)}) async-start(bf16[4,256,1024]{2,1,0:T(8,128)(2,1)} %bitcast.14), calls=%async_computation.3 | async-start | bytes 4194304 | tf_op jit(solution)/shard_map/up_sp/all_to_all | solution.py:540
  160.7 89.7 %collective-permute-start.14 = (bf16[4,256,1024]{2,1,0:T(8,128)(2,1)}, bf16[4,256,1024]{2,1,0:T(8,128)(2,1)}, u32[]{:S(2)}, u32[]{:S(2)}) collective-permute-start(bf16[4,256,1024]{2,1,0:T(8,128)(2,1)} %all-to-all-done.2), channel_id=1, source_target_pairs={{0,16},{16,0},{1,17},{17,1},{2,18},{18,2},{3,19},{19,3},{4,20},{20... | collective-permute-start | bytes 6291464 | tf_op jit(solution)/shard_map/gate_dp/ppermute | solution.py:42
  209.2 37.9 %collective-permute-start.12 = (bf16[256,2048]{1,0:T(8,128)(2,1)S(1)}, bf16[256,2048]{1,0:T(8,128)(2,1)}, u32[]{:S(2)}, u32[]{:S(2)}) collective-permute-start(bf16[256,2048]{1,0:T(8,128)(2,1)S(1)} %pad_maximum_fusion.6), channel_id=1, source_target_pairs={{0,4},{4,0},{8,12},{12,8},{1,5},{5,1},{9,13},{13,9},{2,6},{6,2},{1... | collective-permute-start | bytes 3145736 | tf_op jit(solution)/shard_map/normed/ppermute | solution.py:42
  211.7 49.3 %collective-permute-start.15 = (bf16[512,2048]{1,0:T(8,128)(2,1)}, bf16[512,2048]{1,0:T(8,128)(2,1)}, u32[]{:S(2)}, u32[]{:S(2)}) collective-permute-start(bf16[512,2048]{1,0:T(8,128)(2,1)} %pad_maximum_fusion.1.refs_0_), channel_id=1, source_target_pairs={{0,1},{1,0},{2,3},{3,2},{4,5},{5,4},{6,7},{7,6},{8,9},{9,8},{10,11... | collective-permute-start | bytes 6291464 | tf_op jit(solution)/shard_map/normed/ppermute | solution.py:42
  211.7 39.1 %all-to-all-start.4 = ((bf16[4,64,2048]{2,1,0:T(8,128)(2,1)}), bf16[4,64,2048]{2,1,0:T(8,128)(2,1)S(1)}, u32[]{:S(2)}, u32[]{:S(2)}) async-start(bf16[4,64,2048]{2,1,0:T(8,128)(2,1)} %param.18), calls=%async_computation.4 | async-start | bytes 2097152 | tf_op jit(solution)/shard_map/dy_sp/all_to_all | solution.py:540
  216.7 71.5 %collective-permute-start.17 = (bf16[4,256,1024]{2,1,0:T(8,128)(2,1)}, bf16[4,256,1024]{2,1,0:T(8,128)(2,1)}, u32[]{:S(2)}, u32[]{:S(2)}) collective-permute-start(bf16[4,256,1024]{2,1,0:T(8,128)(2,1)} %all-to-all-done.3), channel_id=1, source_target_pairs={{0,16},{16,0},{1,17},{17,1},{2,18},{18,2},{3,19},{19,3},{4,20},{20... | collective-permute-start | bytes 6291464 | tf_op jit(solution)/shard_map/up_dp/ppermute | solution.py:42
  251.8 41.4 %all-to-all-start.5 = ((bf16[4,2,32,2048]{3,2,1,0:T(8,128)(2,1)}), bf16[4,2,32,2048]{3,2,1,0:T(8,128)(2,1)}, u32[]{:S(2)}, u32[]{:S(2)}) async-start(bf16[4,2,32,2048]{3,2,1,0:T(8,128)(2,1)} %get-tuple-element.302), calls=%async_computation.5 | async-start | bytes 2097152 | tf_op jit(solution)/shard_map/down_sp/all_to_all | solution.py:540
  291.6 32.9 %collective-permute-start.21 = (bf16[256,2048]{1,0:T(8,128)(2,1)}, bf16[256,2048]{1,0:T(8,128)(2,1)}, u32[]{:S(2)}, u32[]{:S(2)}) collective-permute-start(bf16[256,2048]{1,0:T(8,128)(2,1)} %pad_maximum_fusion.9), channel_id=1, source_target_pairs={{0,2},{1,3},{2,0},{3,1},{4,6},{5,7},{6,4},{7,5},{8,10},{9,11},{10,... | collective-permute-start | bytes 3145736 | tf_op jit(solution)/shard_map/dy/ppermute | solution.py:42
  292.9 37.6 %collective-permute-start.20 = (bf16[256,2048]{1,0:T(8,128)(2,1)}, bf16[256,2048]{1,0:T(8,128)(2,1)}, u32[]{:S(2)}, u32[]{:S(2)}) collective-permute-start(bf16[256,2048]{1,0:T(8,128)(2,1)} %pad_maximum_fusion.8), channel_id=1, source_target_pairs={{0,4},{4,0},{8,12},{12,8},{1,5},{5,1},{9,13},{13,9},{2,6},{6,2},{1... | collective-permute-start | bytes 3145736 | tf_op jit(solution)/shard_map/dy/ppermute | solution.py:42
  293.3 43.4 %collective-permute-start.22 = (bf16[512,2048]{1,0:T(8,128)(2,1)S(1)}, bf16[512,2048]{1,0:T(8,128)(2,1)}, u32[]{:S(2)}, u32[]{:S(2)}) collective-permute-start(bf16[512,2048]{1,0:T(8,128)(2,1)S(1)} %pad_maximum_fusion.2.refs_0_), channel_id=1, source_target_pairs={{0,1},{1,0},{2,3},{3,2},{4,5},{5,4},{6,7},{7,6},{8,9},{9,8},{10,11... | collective-permute-start | bytes 6291464 | tf_op jit(solution)/shard_map/dy/ppermute | solution.py:42
  293.3 41.9 %all-to-all-start.6 = ((bf16[4,2,32,2048]{3,2,1,0:T(8,128)(2,1)}), bf16[4,2,32,2048]{3,2,1,0:T(8,128)(2,1)S(1)}, u32[]{:S(2)}, u32[]{:S(2)}) async-start(bf16[4,2,32,2048]{3,2,1,0:T(8,128)(2,1)} %get-tuple-element.312), calls=%async_computation.6 | async-start | bytes 2097152 | tf_op jit(solution)/shard_map/down_sp/all_to_all | solution.py:540
  298.7 64.3 %collective-permute-start.24 = (bf16[4,2,32,2048]{3,2,1,0:T(8,128)(2,1)}, bf16[4,2,32,2048]{3,2,1,0:T(8,128)(2,1)}, u32[]{:S(2)}, u32[]{:S(2)}) collective-permute-start(bf16[4,2,32,2048]{3,2,1,0:T(8,128)(2,1)} %all-to-all-done.5.refs_0_), channel_id=1, source_target_pairs={{0,16},{16,0},{1,17},{17,1},{2,18},{18,2},{3,19},{19,3},{4,20},{20... | collective-permute-start | bytes 3145736 | tf_op jit(solution)/shard_map/down_dp/ppermute | solution.py:42
  361.6 82.2 %collective-permute-start.29 = (bf16[4,4,32,2048]{3,2,1,0:T(8,128)(2,1)}, bf16[4,4,32,2048]{3,2,1,0:T(8,128)(2,1)}, u32[]{:S(2)}, u32[]{:S(2)}) collective-permute-start(bf16[4,4,32,2048]{3,2,1,0:T(8,128)(2,1)} %bitcast.289), channel_id=1, source_target_pairs={{0,16},{16,0},{1,17},{17,1},{2,18},{18,2},{3,19},{19,3},{4,20},{20... | collective-permute-start | bytes 6291464 | tf_op jit(solution)/shard_map/down_grad_dp/ppermute | solution.py:42
  433.2 72.4 %collective-permute-start.32 = (bf16[4,256,1024]{2,1,0:T(8,128)(2,1)}, bf16[4,256,1024]{2,1,0:T(8,128)(2,1)}, u32[]{:S(2)}, u32[]{:S(2)}) collective-permute-start(bf16[4,256,1024]{2,1,0:T(8,128)(2,1)} %dynamic-slice_bitcast_fusion.1), channel_id=1, source_target_pairs={{0,16},{16,0},{1,17},{17,1},{2,18},{18,2},{3,19},{19,3},{4,20},{20... | collective-permute-start | bytes 6291464 | tf_op jit(solution)/shard_map/gate_grad_dp/ppermute | solution.py:42
  448.6 60.8 %all-to-all-start.7 = ((bf16[4,4,32,2048]{3,2,1,0:T(8,128)(2,1)}), bf16[4,4,32,2048]{3,2,1,0:T(8,128)(2,1)S(1)}, u32[]{:S(2)}, u32[]{:S(2)}) async-start(bf16[4,4,32,2048]{3,2,1,0:T(8,128)(2,1)} %fusion.4), calls=%async_computation.7 | async-start | bytes 4194304 | tf_op jit(solution)/shard_map/down_grad_sp/all_to_all | solution.py:540
  452.5 45.0 %collective-permute-start.30 = (bf16[128,2048]{1,0:T(8,128)(2,1)S(1)}, bf16[128,2048]{1,0:T(8,128)(2,1)S(1)}, u32[]{:S(2)}, u32[]{:S(2)}) collective-permute-start(bf16[128,2048]{1,0:T(8,128)(2,1)S(1)} %get-tuple-element.350), channel_id=1, source_target_pairs={{0,4},{4,0},{8,12},{12,8},{1,5},{5,1},{9,13},{13,9},{2,6},{6,2},{1... | collective-permute-start | bytes 1572872 | tf_op jit(solution)/shard_map/normed_grad/ppermute | solution.py:42
  471.6 98.6 %collective-permute-start.38 = (bf16[4,256,1024]{2,1,0:T(8,128)(2,1)}, bf16[4,256,1024]{2,1,0:T(8,128)(2,1)}, u32[]{:S(2)}, u32[]{:S(2)}) collective-permute-start(bf16[4,256,1024]{2,1,0:T(8,128)(2,1)} %dynamic-slice_bitcast_fusion), channel_id=1, source_target_pairs={{0,16},{16,0},{1,17},{17,1},{2,18},{18,2},{3,19},{19,3},{4,20},{20... | collective-permute-start | bytes 6291464 | tf_op jit(solution)/shard_map/up_grad_dp/ppermute | solution.py:42
  510.8 63.3 %all-to-all-start.8 = ((bf16[4,256,1024]{2,1,0:T(8,128)(2,1)}), bf16[4,256,1024]{2,1,0:T(8,128)(2,1)}, u32[]{:S(2)}, u32[]{:S(2)}) async-start(bf16[4,256,1024]{2,1,0:T(8,128)(2,1)} %fusion.3), calls=%async_computation.8 | async-start | bytes 4194304 | tf_op jit(solution)/shard_map/gate_grad_sp/all_to_all | solution.py:540
  551.5 49.6 %collective-permute-start.40 = (bf16[2,128,2048]{2,1,0:T(8,128)(2,1)}, bf16[2,128,2048]{2,1,0:T(8,128)(2,1)}, u32[]{:S(2)}, u32[]{:S(2)}) collective-permute-start(bf16[2,128,2048]{2,1,0:T(8,128)(2,1)} %get-tuple-element.383), channel_id=1, source_target_pairs={{0,4},{4,0},{8,12},{12,8},{1,5},{5,1},{9,13},{13,9},{2,6},{6,2},{1... | collective-permute-start | bytes 3145736 | tf_op jit(solution)/shard_map/out/ppermute | solution.py:42
  553.5 47.6 %collective-permute-start.37 = (bf16[2,128,2048]{2,1,0:T(8,128)(2,1)}, bf16[2,128,2048]{2,1,0:T(8,128)(2,1)}, u32[]{:S(2)}, u32[]{:S(2)}) collective-permute-start(bf16[2,128,2048]{2,1,0:T(8,128)(2,1)} %get-tuple-element.381), channel_id=1, source_target_pairs={{0,2},{1,3},{2,0},{3,1},{4,6},{5,7},{6,4},{7,5},{8,10},{9,11},{10,... | collective-permute-start | bytes 3145736 | tf_op jit(solution)/shard_map/out/ppermute | solution.py:42
  574.1 82.0 %all-to-all-start.9 = ((bf16[4,256,1024]{2,1,0:T(8,128)(2,1)}), bf16[4,256,1024]{2,1,0:T(8,128)(2,1)}, u32[]{:S(2)}, u32[]{:S(2)}) async-start(bf16[4,256,1024]{2,1,0:T(8,128)(2,1)} %fusion.2), calls=%async_computation.9 | async-start | bytes 4194304 | tf_op jit(solution)/shard_map/up_grad_sp/all_to_all | solution.py:540
  578.8 145.8 %reduce-scatter.2.cloned.1.call-start = ((), (), s32[]{:S(2)}) async-start(), calls=%async_computation.15 | async-start | bytes 3538944 | tf_op jit(solution)/shard_map/reduce_scatter | solution.py:853
  608.2 52.5 %collective-permute-start.43 = (bf16[128,2048]{1,0:T(8,128)(2,1)}, bf16[128,2048]{1,0:T(8,128)(2,1)}, u32[]{:S(2)}, u32[]{:S(2)}) collective-permute-start(bf16[128,2048]{1,0:T(8,128)(2,1)} %get-tuple-element.394), channel_id=1, source_target_pairs={{0,2},{1,3},{2,0},{3,1},{4,6},{5,7},{6,4},{7,5},{8,10},{9,11},{10,... | collective-permute-start | bytes 1572872 | tf_op jit(solution)/shard_map/out/ppermute | solution.py:42
  609.1 52.0 %collective-permute-start.39 = (bf16[128,2048]{1,0:T(8,128)(2,1)}, bf16[128,2048]{1,0:T(8,128)(2,1)}, u32[]{:S(2)}, u32[]{:S(2)}) collective-permute-start(bf16[128,2048]{1,0:T(8,128)(2,1)} %get-tuple-element.392), channel_id=1, source_target_pairs={{0,4},{4,0},{8,12},{12,8},{1,5},{5,1},{9,13},{13,9},{2,6},{6,2},{1... | collective-permute-start | bytes 1572872 | tf_op jit(solution)/shard_map/out/ppermute | solution.py:42
  627.2 33.4 %collective-permute-start.44 = (bf16[4,2,32,2048]{3,2,1,0:T(8,128)(2,1)}, bf16[4,2,32,2048]{3,2,1,0:T(8,128)(2,1)}, u32[]{:S(2)}, u32[]{:S(2)}) collective-permute-start(bf16[4,2,32,2048]{3,2,1,0:T(8,128)(2,1)} %bitcast.292), channel_id=1, source_target_pairs={{0,16},{16,0},{1,17},{17,1},{2,18},{18,2},{3,19},{19,3},{4,20},{20... | collective-permute-start | bytes 3145736 | tf_op jit(solution)/shard_map/proj_grad_dp/ppermute | solution.py:42
  656.1 32.5 %all-to-all-start.10 = ((bf16[4,64,2048]{2,1,0:T(8,128)(2,1)}), bf16[4,64,2048]{2,1,0:T(8,128)(2,1)}, u32[]{:S(2)}, u32[]{:S(2)}) async-start(bf16[4,64,2048]{2,1,0:T(8,128)(2,1)} %fusion.14), calls=%async_computation.10 | async-start | bytes 2097152 | tf_op jit(solution)/shard_map/input_sp/all_to_all | solution.py:540
  688.6 32.4 %all-to-all-start.11 = ((bf16[4,2,32,2048]{3,2,1,0:T(8,128)(2,1)}), bf16[4,2,32,2048]{3,2,1,0:T(8,128)(2,1)S(1)}, u32[]{:S(2)}, u32[]{:S(2)}) async-start(bf16[4,2,32,2048]{3,2,1,0:T(8,128)(2,1)} %fusion.17), calls=%async_computation.11 | async-start | bytes 2097152 | tf_op jit(solution)/shard_map/proj_grad_sp/all_to_all | solution.py:540
  (112 other events, 1577.3 us)
Sparse Core Ops, SparseCore 0:
  17.0 88.3 all-gather.1
  601.2 106.3 reduce-scatter.1

commit v4 on v3

--- a/solution.py
+++ b/solution.py
@@ -112,7 +112,7 @@
     lax.fori_loop(0, QPK, head, 0)
     ctx_ref[...] = jnp.transpose(c_s[...]).astype(BF)
 
-def attend(projected, cosine, sine, groups, tile=256):
+def attend(projected, cosine, sine, groups, tile=512):
     length, columns = projected.shape[0], projected.shape[1] // groups
     qw = QPK * HD
     table = pl.BlockSpec((length, LANES), lambda g: (0, 0))
@@ -192,7 +192,7 @@
     block = jnp.concatenate([dk_s[...], dv_s[...]], axis=1)
     out_ref[:, QPK * HD :] = turn(block, k_cos, -k_sin).astype(BF)
 
-def attend_back(qkv, grad, log, cosine, sine, groups, group, earlier, tile=256):
+def attend_back(qkv, grad, log, cosine, sine, groups, group, earlier, tile=512):
     length, columns = qkv.shape[0], qkv.shape[1] // groups
     qw = QPK * HD
     table = pl.BlockSpec((length, LANES), lambda g: (0, 0))
@@ -258,7 +258,7 @@
     gate_ref[...] = by_parts(at_ref, rows_ref, weights)
 
 
-def gate_rows(at, rows, gates, tf=512):
+def gate_rows(at, rows, gates, tf=1024):
     tm, k = rows[0].shape
     f = gates[0].shape[1]
     parts, blocks = len(gates), len(rows)
@@ -293,7 +293,7 @@
     b_ref[...] = up * s * (1.0 + gate * (1.0 - s))
 
 
-def up_rows(at, rows, gate, ups, tm=512, tf=512):
+def up_rows(at, rows, gate, ups, tm=512, tf=1024):
     m, k = rows.shape
     f = gate.shape[1]
     parts = len(ups)
@@ -436,16 +436,17 @@
     out_ref[...] = total.astype(BF)
 
 
-def out_rows(hidden, weights, tm=256):
+def out_rows(hidden, weights, part, tm=256):
     m, f = hidden.shape
+    steps = m // 2 // tm
     each, d = weights[0].shape
     return pl.pallas_call(
         out_kernel,
-        grid=(m // tm,),
-        in_specs=[pl.BlockSpec((tm, f), lambda i: (i, 0))]
+        grid=(steps,),
+        in_specs=[pl.BlockSpec((tm, f), lambda i: (i + part * steps, 0))]
         + [pl.BlockSpec((each, d), lambda i: (0, 0), pipeline_mode=pl.Buffered(1))] * len(weights),
         out_specs=pl.BlockSpec((tm, d), lambda i: (i, 0)),
-        out_shape=jax.ShapeDtypeStruct((m, d), BF),
+        out_shape=jax.ShapeDtypeStruct((m // 2, d), BF),
         compiler_params=pltpu.CompilerParams(vmem_limit_bytes=VMEM_LIMIT),
         cost_estimate=LIGHT,
         name="out_rows",
@@ -799,13 +800,12 @@
 
     reduce.first(grad_mine)
     fence()
+    down_moved = chain.start_all(sum_dp(down_part, down_dp), "down_grad_sp")
     gate_part = mm_tn(now(normed_all), grad_gate).astype(BF)
     gate_part = gate_part.reshape(nx, nz, row_block, feed_columns)
     gate_dp = to_dp(gate_part, "gate_grad_dp")
     fence()
     reduce.second()
-    fence()
-    down_moved = chain.start_all(sum_dp(down_part, down_dp), "down_grad_sp")
     fence()
     up_part = mm_tn(now(normed_all), grad_up).astype(BF).reshape(nx, nz, row_block, feed_columns)
     up_dp = to_dp(up_part, "up_grad_dp")
@@ -825,8 +825,9 @@
     gate_sum = sum_dp(gate_part, gate_dp)
     gate_moved = chain.start_all(after(gate_sum, down_moved), "gate_grad_sp")
     fence()
-    out_part = out_rows(now(hidden), downs)
-    fence(out_part)
+    out_other = out_rows(now(hidden), downs, 1)
+    out_mine = out_rows(now(hidden), downs, 0)
+    fence(out_other, out_mine)
     rows_y = now(rows_y)
     rows_yc = start(rows_y, "tp", 1, "rows_yc")
     fence()
@@ -834,10 +835,9 @@
     grad_rows, grad_context = context_grad(
         at_tp, [rows_mine, now(rows_c), rows_y, now(rows_yc)], proj_all
     )
-    rows_half = out_part.shape[0] // 2
-    out_reduce = Reduce(chain, out_part[rows_half:], "out")
+    out_reduce = Reduce(chain, out_other, "out")
     fence(grad_context)
-    out_reduce.first(out_part[:rows_half])
+    out_reduce.first(out_mine)
     grad_projected = None
     for group in range(groups):
         grad_projected = attend_back(
@@ -849,20 +849,17 @@
             up_sum = sum_dp(up_part, up_dp)
             up_moved = chain.start_all(after(up_sum, gate_moved), "up_grad_sp")
 
+    dn_part = mm_nt(now(grad_projected), qkv_all).astype(BF).reshape(nz, 2, 2, span, width)
+    dn_core = start(pick(dn_part, 1 - c, 2), "tp", 1, "dn_c")
+    fence()
+    dn_sum = (pick(dn_part, c, 2).astype(F32) + now(dn_core).astype(F32)).astype(BF)
+    dn_y = start(pick(dn_sum, 1 - y, 1), "tp", 2, "dn_y")
     qkv_part = mm_tn(normed_one, now(grad_projected)).astype(BF)
     qkv_grad = lax.psum_scatter(qkv_part, ("dp",) + SP, tiled=True)
     out_reduce.second()
-    fence(qkv_part)
-    dn_part = mm_nt(now(grad_projected), qkv_all).astype(BF).reshape(nz, 2, 2, span, width)
-    dn_core = start(pick(dn_part, 1 - c, 2), "tp", 1, "dn_c")
-    fence()
-    dn_sum = (pick(dn_part, c, 2).astype(F32) + now(dn_core).astype(F32)).astype(BF)
-    dn_y = start(pick(dn_sum, 1 - y, 1), "tp", 2, "dn_y")
-    fence()
     proj_part = mm_tn(context, now(grad_rows)).astype(BF)
     proj_part = proj_part.reshape(groups, nx, nz, proj_rows, width).transpose(1, 2, 0, 3, 4)
     proj_dp = to_dp(proj_part, "proj_grad_dp")
-    fence()
 
     grad_normed_one = (pick(dn_sum, y, 1).astype(F32) + now(dn_y).astype(F32)).reshape(-1, width)
     inverse_one = lax.rsqrt(jnp.mean(inputs * inputs, axis=-1, keepdims=True) + NORM_EPSILON)
@@ -874,7 +871,7 @@
     input_delta = (back_two + back_one).astype(BF).reshape(nz, span, width)
     gains_part = jnp.stack([gain_one_part, gain_two_part])
     gains_c = start(gains_part, "tp", 1, "gains_c")
-    fence(input_delta)
+    fence(input_delta, qkv_part)
     up_moved = chain.take(up_moved)
     input_moved = chain.start_all(after(input_delta, up_moved), "input_sp")
     fence()

time: 767 us -> 753 us (0.982)
  Pallas kernels: 184 us -> 175 us
    unnamed x163 -> x151, local copies, waits for them, and re-layouts: 34.9 us -> 30.4 us
    pallas_call x1 -> x2, Pallas kernels: 14.1 us -> 17.3 us  [out_rows(): pl.pallas_call(out_kernel, grid=(steps,), in_specs=[pl.BlockSpec((tm, f),...]
  transfers between devices with their start and end apart: 66 -> 66, of which waited for: 20 -> 22; matrix products, arithmetic and copies ran while one was open for 24% -> 24% of each run, Pallas kernels for 24% -> 23%
where the time goes in v4:
time: 753 us; the launch traced here: 745 us
  waiting for transfers between devices  244 us (32%)
  Pallas kernels  175 us (23%)
  starting transfers between devices  107 us (14%)
  other arithmetic  88.3 us (12%)
  local copies, waits for them, and re-layouts  61.6 us (8%)
  matrix products  53.5 us (7%)
  between operations  15.5 us (2%)
    ppermute x51, waiting for transfers between devices, swap(): lax.ppermute(value, axis, [(i, i ^ mask) for i in range(lax.axis_size(axi...  188 us
    all_to_all x13, starting transfers between devices, start_all(): return lax.all_to_all(blocks, SP, 0, 0, tiled=True)  59.9 us
    all_to_all x13, waiting for transfers between devices, start_all(): return lax.all_to_all(blocks, SP, 0, 0, tiled=True)  56.4 us
    dot_general x7, matrix products, dot(): lax.dot_general(left, right, ((dims[0], dims[1]), ((), ())), preferred_el...  53.5 us
    ppermute x51, starting transfers between devices, swap(): lax.ppermute(value, axis, [(i, i ^ mask) for i in range(lax.axis_size(axi...  46.8 us
    pallas_call x2, Pallas kernels, ffn_back(): pl.pallas_call(functools.partial(ffn_back_kernel, tf, len(downs), parts),...  42.1 us
    pallas_call x2, Pallas kernels, attend_back(): pl.pallas_call(functools.partial(attend_back_kernel, tile), grid=(1,), in...  31.1 us
    unnamed x151, local copies, waits for them, and re-layouts  30.4 us
  transfers between devices with their start and end apart: 66, of which 22 were waited for; matrix products, arithmetic and copies ran while one was open for 24% of the time, Pallas kernels for 23%

profile of v4, /device:TPU:0, one launch (start us, length us, event | category | flops | bytes accessed | tf_op | source)
XLA Modules:
  0.0 745.2 jit_solution(12875893685467318073)
XLA Ops:
  7.2 6.3 all-to-all-start
  39.2 12.0 %collective-permute-done.2 = bf16[2,256]{1,0:T(2,128)(2,1)S(1)} collective-permute-done((bf16[2,256]{1,0:T(2,128)(2,1)S(1)}, bf16[2,256]{1,0:T(2,128)(2,1)S(1)}, u32[]{:S(2)}, u32[]{:S(2)}) %collective-permute-start.2) | collective-permute-done | bytes 1056 | tf_op jit(solution)/shard_map/gains_sp/ppermute | solution.py:42
  58.9 19.9 %collective-permute-done.4.refs_2_ = bf16[4,64,2048]{2,1,0:T(8,128)(2,1)} collective-permute-done((bf16[4,64,2048]{2,1,0:T(8,128)(2,1)S(1)}, bf16[4,64,2048]{2,1,0:T(8,128)(2,1)}, u32[]{:S(2)}, u32[]{:S(2)}) %collective-permute-start.4) | collective-permute-done | bytes 1048608 | tf_op jit(solution)/shard_map/x_y/ppermute | solution.py:42
  83.2 20.5 %all-to-all-done.1.refs_0_ = bf16[4,2,32,2048]{3,2,1,0:T(8,128)(2,1)} async-done(((bf16[4,2,32,2048]{3,2,1,0:T(8,128)(2,1)}), bf16[4,2,32,2048]{3,2,1,0:T(8,128)(2,1)}, u32[]{:S(2)}, u32[]{:S(2)}) %all-to-all-start.1) | async-done | bytes 1048608 | tf_op jit(solution)/shard_map/proj_sp/all_to_all | solution.py:541
  109.0 8.7 %project.1 = (bf16[1024,2048]{1,0:T(8,128)(2,1)}, f32[1024,768]{1,0:T(8,128)}) custom-call(s32[4]{0:T(128)} %pad_add_fusion.at_ref, bf16[4,64,2048]{2,1,0:T(8,128)(2,1)} %copy-done.10, bf16[4,64,2048]{2,1,0:T(8,128)(2,1)} %collective-permute-done.refs_1_, bf16[4,64,2048]{2,1,0:T(8,128)(2,1)} %collective-permute-done.4.refs_2_, ...), custom_call_target="tpu_custom_call" | custom-call | flops 4294967296 | bytes 1048576 | tf_op jit(solution)/shard_map/project/pallas_call | solution.py:385
  117.7 17.6 %attend.1 = (bf16[1024,768]{1,0:T(8,128)(2,1)}, bf16[1024,512]{1,0:T(8,128)(2,1)}, f32[2,4,1024]{2,1,0:T(4,128)}) custom-call(f32[1024,768]{1,0:T(8,128)} %get-tuple-element.260.p_ref, f32[1024,128]{1,0:T(8,128)} %get-tuple-element.510.cos_ref, f32[1024,128]{1,0:T(8,128)} %get-tuple-element.511.sin_ref), custom_call_target="tpu_custom_call" | custom-call | flops 68719476736 | bytes 1048576 | tf_op jit(solution)/shard_map/attend/pallas_call | solution.py:119
  159.2 17.7 %collective-permute-done.9 = bf16[4,64,2048]{2,1,0:T(8,128)(2,1)} collective-permute-done((bf16[4,64,2048]{2,1,0:T(8,128)(2,1)S(1)}, bf16[4,64,2048]{2,1,0:T(8,128)(2,1)}, u32[]{:S(2)}, u32[]{:S(2)}) %collective-permute-start.9) | collective-permute-done | bytes 1048608 | tf_op jit(solution)/shard_map/attn_y/ppermute | solution.py:42
  183.6 19.5 %collective-permute-done.11 = bf16[128,2048]{1,0:T(8,128)(2,1)S(1)} collective-permute-done((bf16[128,2048]{1,0:T(8,128)(2,1)S(1)}, bf16[128,2048]{1,0:T(8,128)(2,1)S(1)}, u32[]{:S(2)}, u32[]{:S(2)}) %collective-permute-start.11) | collective-permute-done | bytes 524320 | tf_op jit(solution)/shard_map/normed/ppermute | solution.py:42
  214.4 14.8 %collective-permute-done.13 = bf16[256,2048]{1,0:T(8,128)(2,1)S(1)} collective-permute-done((bf16[256,2048]{1,0:T(8,128)(2,1)}, bf16[256,2048]{1,0:T(8,128)(2,1)S(1)}, u32[]{:S(2)}, u32[]{:S(2)}) %collective-permute-start.13) | collective-permute-done | bytes 1048608 | tf_op jit(solution)/shard_map/normed/ppermute | solution.py:42
  229.2 14.9 %collective-permute-done.12 = bf16[256,2048]{1,0:T(8,128)(2,1)} collective-permute-done((bf16[256,2048]{1,0:T(8,128)(2,1)S(1)}, bf16[256,2048]{1,0:T(8,128)(2,1)}, u32[]{:S(2)}, u32[]{:S(2)}) %collective-permute-start.12) | collective-permute-done | bytes 1048608 | tf_op jit(solution)/shard_map/normed/ppermute | solution.py:42
  257.4 16.1 %gate_rows.1 = (f32[2048,1024]{1,0:T(8,128)}, bf16[2048,2048]{1,0:T(8,128)(2,1)}) custom-call(s32[2]{0:T(128)} %pad_add_fusion.1.at_ref, bf16[512,2048]{1,0:T(8,128)(2,1)} %pad_maximum_fusion.1.refs_0_, bf16[512,2048]{1,0:T(8,128)(2,1)} %constant_dynamic-update-slice_fusion.refs_1_, bf16[512,2048]{1,0:T(8,128)(2,1)} %collective-permute-done.15.refs_2_, ...), custom_call_target="tpu_custom_call" | custom-call | flops 68719476736 | bytes 1048576 | tf_op jit(solution)/shard_map/gate_rows/pallas_call | solution.py:265
  273.4 10.7 %collective-permute-done.19 = bf16[128,2048]{1,0:T(8,128)(2,1)S(1)} collective-permute-done((bf16[128,2048]{1,0:T(8,128)(2,1)S(1)}, bf16[128,2048]{1,0:T(8,128)(2,1)S(1)}, u32[]{:S(2)}, u32[]{:S(2)}) %collective-permute-start.19) | collective-permute-done | bytes 524320 | tf_op jit(solution)/shard_map/dy/ppermute | solution.py:42
  288.4 5.2 all-to-all-start.6
  294.6 19.2 %up_rows.1 = (bf16[2048,1024]{1,0:T(8,128)(2,1)}, f32[2048,1024]{1,0:T(8,128)}, f32[2048,1024]{1,0:T(8,128)}) custom-call(s32[2]{0:T(128)} %pad_add_fusion.1.at_ref, bf16[2048,2048]{1,0:T(8,128)(2,1)} %get-tuple-element.352.rows_ref, f32[2048,1024]{1,0:T(8,128)} %get-tuple-element.303.gate_ref, bf16[1024,1024]{1,0:T(8,128)(2,1)} %bitcast.34.refs_0_.refs_4_, ...), custom_call_target="tpu_custom_call" | custom-call | flops 68719476736 | bytes 1048576 | tf_op jit(solution)/shard_map/up_rows/pallas_call | solution.py:301
  313.8 11.9 %collective-permute-done.20 = bf16[256,2048]{1,0:T(8,128)(2,1)} collective-permute-done((bf16[256,2048]{1,0:T(8,128)(2,1)}, bf16[256,2048]{1,0:T(8,128)(2,1)}, u32[]{:S(2)}, u32[]{:S(2)}) %collective-permute-start.20) | collective-permute-done | bytes 1048608 | tf_op jit(solution)/shard_map/dy/ppermute | solution.py:42
  334.8 7.1 join.1.dy_ref
  341.9 11.4 %convolution_convert_fusion = bf16[1024,2048]{1,0:T(8,128)(2,1)S(1)} fusion(bf16[2048,1024]{1,0:T(8,128)(2,1)S(1)} %copy-done.66, bf16[2048,2048]{1,0:T(8,128)(2,1)} %join.1.dy_ref), kind=kOutput, calls=%fused_computation.17 | convolution fusion | flops 8592031744 | bytes 16777216 | tf_op jit(solution)/shard_map/dot_general | solution.py:50
  364.6 21.0 %ffn_back.2 = (bf16[2048,1024]{1,0:T(8,128)(2,1)}, bf16[2048,1024]{1,0:T(8,128)(2,1)}, bf16[1024,2048]{1,0:T(8,128)(2,1)}) custom-call(s32[2]{0:T(128)} %pad_add_fusion.1.at_ref, bf16[2048,2048]{1,0:T(8,128)(2,1)} %join.1.dy_ref, f32[2048,1024]{1,0:T(8,128)} %get-tuple-element.327.a_ref, f32[2048,1024]{1,0:T(8,128)} %get-tuple-element.328.b_ref, ...), custom_call_target="tpu_custom_call" | custom-call | flops 68719476736 | bytes 1048576 | tf_op jit(solution)/shard_map/ffn_back/pallas_call | solution.py:350
  385.6 21.1 %ffn_back.3 = (bf16[2048,1024]{1,0:T(8,128)(2,1)}, bf16[2048,1024]{1,0:T(8,128)(2,1)}, bf16[1024,2048]{1,0:T(8,128)(2,1)}) custom-call(s32[2]{0:T(128)} %pad_add_fusion.1.at_ref, bf16[2048,2048]{1,0:T(8,128)(2,1)} %join.1.dy_ref, f32[2048,1024]{1,0:T(8,128)} %get-tuple-element.327.a_ref, ...), custom_call_target="tpu_custom_call", output_to_operand_aliasing={{0}: (10, {}), {1}: (11, {})} | custom-call | flops 68719476736 | bytes 1048576 | tf_op jit(solution)/shard_map/ffn_back/pallas_call | solution.py:350
  420.8 12.7 %convolution_convert_fusion.4 = bf16[2048,1024]{1,0:T(8,128)(2,1)S(1)} fusion(bf16[2048,2048]{1,0:T(8,128)(2,1)} %get-tuple-element.352.rows_ref, bf16[2048,1024]{1,0:T(8,128)(2,1)} %get-tuple-element.344), kind=kOutput, calls=%fused_computation.21 | convolution fusion | flops 8592031744 | bytes 16777216 | tf_op jit(solution)/shard_map/dot_general | solution.py:50
  434.5 28.9 %collective-permute-done.29 = bf16[2,128,2048]{2,1,0:T(8,128)(2,1)} collective-permute-done((bf16[2,128,2048]{2,1,0:T(8,128)(2,1)}, bf16[2,128,2048]{2,1,0:T(8,128)(2,1)}, u32[]{:S(2)}, u32[]{:S(2)}) %collective-permute-start.29) | collective-permute-done | bytes 1048608 | tf_op jit(solution)/shard_map/normed_grad/ppermute | solution.py:42
  468.0 11.5 %convolution_convert_fusion.3 = bf16[2048,1024]{1,0:T(8,128)(2,1)S(1)} fusion(bf16[2048,2048]{1,0:T(8,128)(2,1)} %get-tuple-element.352.rows_ref, bf16[2048,1024]{1,0:T(8,128)(2,1)S(1)} %copy-done.71), kind=kOutput, calls=%fused_computation.20 | convolution fusion | flops 8592031744 | bytes 16777216 | tf_op jit(solution)/shard_map/dot_general | solution.py:50
  499.5 8.6 %out_rows.3 = bf16[1024,2048]{1,0:T(8,128)(2,1)} custom-call(bf16[2048,1024]{1,0:T(8,128)(2,1)} %get-tuple-element.365.hid_ref, bf16[512,2048]{1,0:T(8,128)(2,1)} %bitcast.325, bf16[512,2048]{1,0:T(8,128)(2,1)} %bitcast.329), custom_call_target="tpu_custom_call" | custom-call | flops 4294967296 | bytes 1048576 | tf_op jit(solution)/shard_map/out_rows/pallas_call | solution.py:443
  508.1 8.6 %out_rows.2 = bf16[1024,2048]{1,0:T(8,128)(2,1)} custom-call(bf16[2048,1024]{1,0:T(8,128)(2,1)} %get-tuple-element.365.hid_ref, bf16[512,2048]{1,0:T(8,128)(2,1)} %bitcast.326, bf16[512,2048]{1,0:T(8,128)(2,1)} %bitcast.330), custom_call_target="tpu_custom_call" | custom-call | flops 4294967296 | bytes 1048576 | tf_op jit(solution)/shard_map/out_rows/pallas_call | solution.py:443
  520.6 6.9 context_grad.1
  537.9 15.5 %attend_back.2.refs_0_ = bf16[1024,768]{1,0:T(8,128)(2,1)} custom-call(bf16[1024,768]{1,0:T(8,128)(2,1)} %get-tuple-element.377.qkv_ref, bf16[1024,512]{1,0:T(8,128)(2,1)} %get-tuple-element.385.grad_ref, f32[2,4,1024]{2,1,0:T(4,128)} %get-tuple-element.380.log_ref, f32[1024,128]{1,0:T(8,128)} %get-tuple-element.510.cos_ref, ...), custom_call_target="tpu_custom_call" | custom-call | flops 68719476736 | bytes 1048576 | tf_op jit(solution)/shard_map/attend_back/pallas_call | solution.py:200
  561.8 15.6 %attend_back.3 = bf16[1024,768]{1,0:T(8,128)(2,1)} custom-call(bf16[1024,768]{1,0:T(8,128)(2,1)} %get-tuple-element.377.qkv_ref, bf16[1024,512]{1,0:T(8,128)(2,1)} %get-tuple-element.385.grad_ref, f32[2,4,1024]{2,1,0:T(4,128)} %get-tuple-element.380.log_ref, f32[1024,128]{1,0:T(8,128)} %get-tuple-element.510.cos_ref, ...), custom_call_target="tpu_custom_call", output_to_operand_aliasing={{}: (5, {})} | custom-call | flops 68719476736 | bytes 1048576 | tf_op jit(solution)/shard_map/attend_back/pallas_call | solution.py:200
  616.4 7.9 %collective-permute-done.42 = bf16[4,64,2048]{2,1,0:T(8,128)(2,1)} collective-permute-done((bf16[4,64,2048]{2,1,0:T(8,128)(2,1)}, bf16[4,64,2048]{2,1,0:T(8,128)(2,1)}, u32[]{:S(2)}, u32[]{:S(2)}) %collective-permute-start.42) | collective-permute-done | bytes 1048608 | tf_op jit(solution)/shard_map/dn_y/ppermute | solution.py:42
  639.0 11.5 %collective-permute-done.39 = bf16[128,2048]{1,0:T(8,128)(2,1)} collective-permute-done((bf16[128,2048]{1,0:T(8,128)(2,1)}, bf16[128,2048]{1,0:T(8,128)(2,1)}, u32[]{:S(2)}, u32[]{:S(2)}) %collective-permute-start.39) | collective-permute-done | bytes 524320 | tf_op jit(solution)/shard_map/out/ppermute | solution.py:42
  685.1 7.5 %multiply_subtract_fusion = (f32[2,256,2048]{2,1,0:T(8,128)}, f32[2,256,2048]{2,1,0:T(8,128)}, f32[2,256,2048]{2,1,0:T(8,128)}, f32[2,256,2048]{2,1,0:T(8,128)}) fusion(f32[2,256,2048]{2,1,0:T(8,128)S(1)} %copy-done.18, f32[2,256,2048]{2,1,0:T(8,128)S(1)} %copy-done.36, f32[2,256,2048]{2,1,0:T(8,128)S(1)} %copy-done.37, ...), kind=kLoop, calls=%fused_computation.15 | loop fusion | flops 16777216 | bytes 33554432 | tf_op jit(solution)/shard_map/sub | solution.py:512
  697.1 13.2 %all-to-all-done.11 = bf16[4,2,32,2048]{3,2,1,0:T(8,128)(2,1)S(1)} async-done(((bf16[4,2,32,2048]{3,2,1,0:T(8,128)(2,1)}), bf16[4,2,32,2048]{3,2,1,0:T(8,128)(2,1)S(1)}, u32[]{:S(2)}, u32[]{:S(2)}) %all-to-all-start.11) | async-done | bytes 1048608 | tf_op jit(solution)/shard_map/proj_grad_sp/all_to_all | solution.py:541
  720.4 15.9 %all-to-all-done.12 = bf16[4,64,2048]{2,1,0:T(8,128)(2,1)S(1)} async-done(((bf16[4,64,2048]{2,1,0:T(8,128)(2,1)}), bf16[4,64,2048]{2,1,0:T(8,128)(2,1)S(1)}, u32[]{:S(2)}, u32[]{:S(2)}) %all-to-all-start.12) | async-done | bytes 1048608 | tf_op jit(solution)/shard_map/block_sp/all_to_all | solution.py:541
  (382 shorter events, 289.8 us)
Async XLA Ops:
  7.2 45.7 %all-to-all-start = ((bf16[4,64,2048]{2,1,0:T(8,128)(2,1)}), bf16[4,64,2048]{2,1,0:T(8,128)(2,1)S(1)}, u32[]{:S(2)}, u32[]{:S(2)}) async-start(bf16[4,64,2048]{2,1,0:T(8,128)(2,1)} %param.17), calls=%async_computation | async-start | bytes 2097152 | tf_op jit(solution)/shard_map/x_sp/all_to_all | solution.py:541
  13.5 95.5 %all-gather.2.cloned.1.call-start = ((), (), s32[]{:S(2)}) async-start(), calls=%async_computation.14 | async-start | bytes 3538944 | tf_op jit(solution)/shard_map/all_gather | solution.py:672
  19.6 31.6 %collective-permute-start.2 = (bf16[2,256]{1,0:T(2,128)(2,1)S(1)}, bf16[2,256]{1,0:T(2,128)(2,1)S(1)}, u32[]{:S(2)}, u32[]{:S(2)}) collective-permute-start(bf16[2,256]{1,0:T(2,128)(2,1)S(1)} %convert_element_type.375), channel_id=1, source_target_pairs={{0,8},{4,12},{8,0},{12,4},{1,9},{5,13},{9,1},{13,5},{2,10},{6,14},... | collective-permute-start | bytes 3080 | tf_op jit(solution)/shard_map/gains_sp/ppermute | solution.py:42
  52.9 50.7 %all-to-all-start.1 = ((bf16[4,2,32,2048]{3,2,1,0:T(8,128)(2,1)}), bf16[4,2,32,2048]{3,2,1,0:T(8,128)(2,1)}, u32[]{:S(2)}, u32[]{:S(2)}) async-start(bf16[4,2,32,2048]{3,2,1,0:T(8,128)(2,1)} %tile.16), calls=%async_computation.1 | async-start | bytes 2097152 | tf_op jit(solution)/shard_map/proj_sp/all_to_all | solution.py:541
  58.8 50.2 %collective-permute-start = (bf16[4,64,2048]{2,1,0:T(8,128)(2,1)S(1)}, bf16[4,64,2048]{2,1,0:T(8,128)(2,1)}, u32[]{:S(2)}, u32[]{:S(2)}) collective-permute-start(bf16[4,64,2048]{2,1,0:T(8,128)(2,1)S(1)} %all-to-all-done.refs_0_), channel_id=1, source_target_pairs={{0,1},{1,0},{2,3},{3,2},{4,5},{5,4},{6,7},{7,6},{8,9},{9,8},{10,11... | collective-permute-start | bytes 3145736 | tf_op jit(solution)/shard_map/x_c/ppermute | solution.py:42
  103.7 49.1 %all-to-all-start.2 = ((bf16[4,256,1024]{2,1,0:T(8,128)(2,1)}), bf16[4,256,1024]{2,1,0:T(8,128)(2,1)}, u32[]{:S(2)}, u32[]{:S(2)}) async-start(bf16[4,256,1024]{2,1,0:T(8,128)(2,1)} %bitcast.11), calls=%async_computation.2 | async-start | bytes 4194304 | tf_op jit(solution)/shard_map/gate_sp/all_to_all | solution.py:541
  154.3 54.5 %all-to-all-start.3 = ((bf16[4,256,1024]{2,1,0:T(8,128)(2,1)}), bf16[4,256,1024]{2,1,0:T(8,128)(2,1)}, u32[]{:S(2)}, u32[]{:S(2)}) async-start(bf16[4,256,1024]{2,1,0:T(8,128)(2,1)} %bitcast.14), calls=%async_computation.3 | async-start | bytes 4194304 | tf_op jit(solution)/shard_map/up_sp/all_to_all | solution.py:541
  158.7 88.8 %collective-permute-start.14 = (bf16[4,256,1024]{2,1,0:T(8,128)(2,1)}, bf16[4,256,1024]{2,1,0:T(8,128)(2,1)}, u32[]{:S(2)}, u32[]{:S(2)}) collective-permute-start(bf16[4,256,1024]{2,1,0:T(8,128)(2,1)} %all-to-all-done.2), channel_id=1, source_target_pairs={{0,16},{16,0},{1,17},{17,1},{2,18},{18,2},{3,19},{19,3},{4,20},{20... | collective-permute-start | bytes 6291464 | tf_op jit(solution)/shard_map/gate_dp/ppermute | solution.py:42
  206.3 37.9 %collective-permute-start.12 = (bf16[256,2048]{1,0:T(8,128)(2,1)S(1)}, bf16[256,2048]{1,0:T(8,128)(2,1)}, u32[]{:S(2)}, u32[]{:S(2)}) collective-permute-start(bf16[256,2048]{1,0:T(8,128)(2,1)S(1)} %pad_maximum_fusion.6), channel_id=1, source_target_pairs={{0,4},{4,0},{8,12},{12,8},{1,5},{5,1},{9,13},{13,9},{2,6},{6,2},{1... | collective-permute-start | bytes 3145736 | tf_op jit(solution)/shard_map/normed/ppermute | solution.py:42
  208.7 48.6 %collective-permute-start.15 = (bf16[512,2048]{1,0:T(8,128)(2,1)}, bf16[512,2048]{1,0:T(8,128)(2,1)}, u32[]{:S(2)}, u32[]{:S(2)}) collective-permute-start(bf16[512,2048]{1,0:T(8,128)(2,1)} %pad_maximum_fusion.1.refs_0_), channel_id=1, source_target_pairs={{0,1},{1,0},{2,3},{3,2},{4,5},{5,4},{6,7},{7,6},{8,9},{9,8},{10,11... | collective-permute-start | bytes 6291464 | tf_op jit(solution)/shard_map/normed/ppermute | solution.py:42
  208.8 38.8 %all-to-all-start.4 = ((bf16[4,64,2048]{2,1,0:T(8,128)(2,1)}), bf16[4,64,2048]{2,1,0:T(8,128)(2,1)S(1)}, u32[]{:S(2)}, u32[]{:S(2)}) async-start(bf16[4,64,2048]{2,1,0:T(8,128)(2,1)} %param.18), calls=%async_computation.4 | async-start | bytes 2097152 | tf_op jit(solution)/shard_map/dy_sp/all_to_all | solution.py:541
  213.6 70.5 %collective-permute-start.17 = (bf16[4,256,1024]{2,1,0:T(8,128)(2,1)}, bf16[4,256,1024]{2,1,0:T(8,128)(2,1)}, u32[]{:S(2)}, u32[]{:S(2)}) collective-permute-start(bf16[4,256,1024]{2,1,0:T(8,128)(2,1)} %all-to-all-done.3), channel_id=1, source_target_pairs={{0,16},{16,0},{1,17},{17,1},{2,18},{18,2},{3,19},{19,3},{4,20},{20... | collective-permute-start | bytes 6291464 | tf_op jit(solution)/shard_map/up_dp/ppermute | solution.py:42
  248.5 39.9 %all-to-all-start.5 = ((bf16[4,2,32,2048]{3,2,1,0:T(8,128)(2,1)}), bf16[4,2,32,2048]{3,2,1,0:T(8,128)(2,1)}, u32[]{:S(2)}, u32[]{:S(2)}) async-start(bf16[4,2,32,2048]{3,2,1,0:T(8,128)(2,1)} %get-tuple-element.298), calls=%async_computation.5 | async-start | bytes 2097152 | tf_op jit(solution)/shard_map/down_sp/all_to_all | solution.py:541
  288.1 37.6 %collective-permute-start.20 = (bf16[256,2048]{1,0:T(8,128)(2,1)}, bf16[256,2048]{1,0:T(8,128)(2,1)}, u32[]{:S(2)}, u32[]{:S(2)}) collective-permute-start(bf16[256,2048]{1,0:T(8,128)(2,1)} %pad_maximum_fusion.8), channel_id=1, source_target_pairs={{0,4},{4,0},{8,12},{12,8},{1,5},{5,1},{9,13},{13,9},{2,6},{6,2},{1... | collective-permute-start | bytes 3145736 | tf_op jit(solution)/shard_map/dy/ppermute | solution.py:42
  288.4 42.8 %collective-permute-start.22 = (bf16[512,2048]{1,0:T(8,128)(2,1)S(1)}, bf16[512,2048]{1,0:T(8,128)(2,1)}, u32[]{:S(2)}, u32[]{:S(2)}) collective-permute-start(bf16[512,2048]{1,0:T(8,128)(2,1)S(1)} %pad_maximum_fusion.2.refs_0_), channel_id=1, source_target_pairs={{0,1},{1,0},{2,3},{3,2},{4,5},{5,4},{6,7},{7,6},{8,9},{9,8},{10,11... | collective-permute-start | bytes 6291464 | tf_op jit(solution)/shard_map/dy/ppermute | solution.py:42
  288.4 41.9 %all-to-all-start.6 = ((bf16[4,2,32,2048]{3,2,1,0:T(8,128)(2,1)}), bf16[4,2,32,2048]{3,2,1,0:T(8,128)(2,1)S(1)}, u32[]{:S(2)}, u32[]{:S(2)}) async-start(bf16[4,2,32,2048]{3,2,1,0:T(8,128)(2,1)} %get-tuple-element.308), calls=%async_computation.6 | async-start | bytes 2097152 | tf_op jit(solution)/shard_map/down_sp/all_to_all | solution.py:541
  293.7 63.9 %collective-permute-start.24 = (bf16[4,2,32,2048]{3,2,1,0:T(8,128)(2,1)}, bf16[4,2,32,2048]{3,2,1,0:T(8,128)(2,1)}, u32[]{:S(2)}, u32[]{:S(2)}) collective-permute-start(bf16[4,2,32,2048]{3,2,1,0:T(8,128)(2,1)} %all-to-all-done.5.refs_0_), channel_id=1, source_target_pairs={{0,16},{16,0},{1,17},{17,1},{2,18},{18,2},{3,19},{19,3},{4,20},{20... | collective-permute-start | bytes 3145736 | tf_op jit(solution)/shard_map/down_dp/ppermute | solution.py:42
  356.7 57.8 %collective-permute-start.27 = (bf16[4,4,32,2048]{3,2,1,0:T(8,128)(2,1)}, bf16[4,4,32,2048]{3,2,1,0:T(8,128)(2,1)S(1)}, u32[]{:S(2)}, u32[]{:S(2)}) collective-permute-start(bf16[4,4,32,2048]{3,2,1,0:T(8,128)(2,1)} %bitcast.289), channel_id=1, source_target_pairs={{0,16},{16,0},{1,17},{17,1},{2,18},{18,2},{3,19},{19,3},{4,20},{20... | collective-permute-start | bytes 6291464 | tf_op jit(solution)/shard_map/down_grad_dp/ppermute | solution.py:42
  413.6 49.7 %collective-permute-start.28 = (bf16[2,128,2048]{2,1,0:T(8,128)(2,1)}, bf16[2,128,2048]{2,1,0:T(8,128)(2,1)S(1)}, u32[]{:S(2)}, u32[]{:S(2)}) collective-permute-start(bf16[2,128,2048]{2,1,0:T(8,128)(2,1)} %get-tuple-element.338), channel_id=1, source_target_pairs={{0,2},{1,3},{2,0},{3,1},{4,6},{5,7},{6,4},{7,5},{8,10},{9,11},{10,... | collective-permute-start | bytes 3145736 | tf_op jit(solution)/shard_map/normed_grad/ppermute | solution.py:42
  414.6 48.8 %collective-permute-start.29 = (bf16[2,128,2048]{2,1,0:T(8,128)(2,1)}, bf16[2,128,2048]{2,1,0:T(8,128)(2,1)}, u32[]{:S(2)}, u32[]{:S(2)}) collective-permute-start(bf16[2,128,2048]{2,1,0:T(8,128)(2,1)} %get-tuple-element.339), channel_id=1, source_target_pairs={{0,4},{4,0},{8,12},{12,8},{1,5},{5,1},{9,13},{13,9},{2,6},{6,2},{1... | collective-permute-start | bytes 3145736 | tf_op jit(solution)/shard_map/normed_grad/ppermute | solution.py:42
  416.7 76.6 %all-to-all-start.7 = ((bf16[4,4,32,2048]{3,2,1,0:T(8,128)(2,1)}), bf16[4,4,32,2048]{3,2,1,0:T(8,128)(2,1)S(1)}, u32[]{:S(2)}, u32[]{:S(2)}) async-start(bf16[4,4,32,2048]{3,2,1,0:T(8,128)(2,1)} %fusion.4), calls=%async_computation.7 | async-start | bytes 4194304 | tf_op jit(solution)/shard_map/down_grad_sp/all_to_all | solution.py:541
  433.7 57.2 %collective-permute-start.32 = (bf16[4,256,1024]{2,1,0:T(8,128)(2,1)S(1)}, bf16[4,256,1024]{2,1,0:T(8,128)(2,1)S(1)}, u32[]{:S(2)}, u32[]{:S(2)}) collective-permute-start(bf16[4,256,1024]{2,1,0:T(8,128)(2,1)S(1)} %dynamic-slice_bitcast_fusion.1), channel_id=1, source_target_pairs={{0,16},{16,0},{1,17},{17,1},{2,18},{18,2},{3,19},{19,3},{4,20},{20... | collective-permute-start | bytes 6291464 | tf_op jit(solution)/shard_map/gate_grad_dp/ppermute | solution.py:42
  482.2 71.2 %collective-permute-start.38 = (bf16[4,256,1024]{2,1,0:T(8,128)(2,1)}, bf16[4,256,1024]{2,1,0:T(8,128)(2,1)}, u32[]{:S(2)}, u32[]{:S(2)}) collective-permute-start(bf16[4,256,1024]{2,1,0:T(8,128)(2,1)} %dynamic-slice_bitcast_fusion), channel_id=1, source_target_pairs={{0,16},{16,0},{1,17},{17,1},{2,18},{18,2},{3,19},{19,3},{4,20},{20... | collective-permute-start | bytes 6291464 | tf_op jit(solution)/shard_map/up_grad_dp/ppermute | solution.py:42
  494.6 62.7 %all-to-all-start.8 = ((bf16[4,256,1024]{2,1,0:T(8,128)(2,1)}), bf16[4,256,1024]{2,1,0:T(8,128)(2,1)}, u32[]{:S(2)}, u32[]{:S(2)}) async-start(bf16[4,256,1024]{2,1,0:T(8,128)(2,1)} %fusion.3), calls=%async_computation.8 | async-start | bytes 4194304 | tf_op jit(solution)/shard_map/gate_grad_sp/all_to_all | solution.py:541
  534.3 72.4 %collective-permute-start.41 = (bf16[2,128,2048]{2,1,0:T(8,128)(2,1)}, bf16[2,128,2048]{2,1,0:T(8,128)(2,1)}, u32[]{:S(2)}, u32[]{:S(2)}) collective-permute-start(bf16[2,128,2048]{2,1,0:T(8,128)(2,1)} %get-tuple-element.378), channel_id=1, source_target_pairs={{0,4},{4,0},{8,12},{12,8},{1,5},{5,1},{9,13},{13,9},{2,6},{6,2},{1... | collective-permute-start | bytes 3145736 | tf_op jit(solution)/shard_map/out/ppermute | solution.py:42
  537.0 69.7 %collective-permute-start.37 = (bf16[2,128,2048]{2,1,0:T(8,128)(2,1)}, bf16[2,128,2048]{2,1,0:T(8,128)(2,1)}, u32[]{:S(2)}, u32[]{:S(2)}) collective-permute-start(bf16[2,128,2048]{2,1,0:T(8,128)(2,1)} %get-tuple-element.376), channel_id=1, source_target_pairs={{0,2},{1,3},{2,0},{3,1},{4,6},{5,7},{6,4},{7,5},{8,10},{9,11},{10,... | collective-permute-start | bytes 3145736 | tf_op jit(solution)/shard_map/out/ppermute | solution.py:42
  557.3 72.7 %all-to-all-start.9 = ((bf16[4,256,1024]{2,1,0:T(8,128)(2,1)}), bf16[4,256,1024]{2,1,0:T(8,128)(2,1)}, u32[]{:S(2)}, u32[]{:S(2)}) async-start(bf16[4,256,1024]{2,1,0:T(8,128)(2,1)} %fusion.2), calls=%async_computation.9 | async-start | bytes 4194304 | tf_op jit(solution)/shard_map/up_grad_sp/all_to_all | solution.py:541
  561.8 152.1 %reduce-scatter.2.cloned.1.call-start = ((), (), s32[]{:S(2)}) async-start(), calls=%async_computation.15 | async-start | bytes 3538944 | tf_op jit(solution)/shard_map/reduce_scatter | solution.py:858
  605.6 33.1 %collective-permute-start.44 = (bf16[4,2,32,2048]{3,2,1,0:T(8,128)(2,1)}, bf16[4,2,32,2048]{3,2,1,0:T(8,128)(2,1)}, u32[]{:S(2)}, u32[]{:S(2)}) collective-permute-start(bf16[4,2,32,2048]{3,2,1,0:T(8,128)(2,1)} %bitcast.292), channel_id=1, source_target_pairs={{0,16},{16,0},{1,17},{17,1},{2,18},{18,2},{3,19},{19,3},{4,20},{20... | collective-permute-start | bytes 3145736 | tf_op jit(solution)/shard_map/proj_grad_dp/ppermute | solution.py:42
  614.5 35.9 %collective-permute-start.39 = (bf16[128,2048]{1,0:T(8,128)(2,1)}, bf16[128,2048]{1,0:T(8,128)(2,1)}, u32[]{:S(2)}, u32[]{:S(2)}) collective-permute-start(bf16[128,2048]{1,0:T(8,128)(2,1)} %get-tuple-element.390), channel_id=1, source_target_pairs={{0,4},{4,0},{8,12},{12,8},{1,5},{5,1},{9,13},{13,9},{2,6},{6,2},{1... | collective-permute-start | bytes 1572872 | tf_op jit(solution)/shard_map/out/ppermute | solution.py:42
  630.0 39.9 %all-to-all-start.10 = ((bf16[4,64,2048]{2,1,0:T(8,128)(2,1)}), bf16[4,64,2048]{2,1,0:T(8,128)(2,1)}, u32[]{:S(2)}, u32[]{:S(2)}) async-start(bf16[4,64,2048]{2,1,0:T(8,128)(2,1)} %fusion.14), calls=%async_computation.10 | async-start | bytes 2097152 | tf_op jit(solution)/shard_map/input_sp/all_to_all | solution.py:541
  669.8 40.5 %all-to-all-start.11 = ((bf16[4,2,32,2048]{3,2,1,0:T(8,128)(2,1)}), bf16[4,2,32,2048]{3,2,1,0:T(8,128)(2,1)S(1)}, u32[]{:S(2)}, u32[]{:S(2)}) async-start(bf16[4,2,32,2048]{3,2,1,0:T(8,128)(2,1)} %fusion.17), calls=%async_computation.11 | async-start | bytes 2097152 | tf_op jit(solution)/shard_map/proj_grad_sp/all_to_all | solution.py:541
  (106 other events, 1357.0 us)
Sparse Core Ops, SparseCore 0:
  17.0 88.3 all-gather.1
  603.0 109.3 reduce-scatter.1

commit v5 on v4

--- a/solution.py
+++ b/solution.py
@@ -848,6 +848,9 @@
             gate_moved = chain.take(gate_moved)
             up_sum = sum_dp(up_part, up_dp)
             up_moved = chain.start_all(after(up_sum, gate_moved), "up_grad_sp")
+            proj_part = mm_tn(context, now(grad_rows)).astype(BF)
+            proj_part = proj_part.reshape(groups, nx, nz, proj_rows, width).transpose(1, 2, 0, 3, 4)
+            proj_dp = to_dp(proj_part, "proj_grad_dp")
 
     dn_part = mm_nt(now(grad_projected), qkv_all).astype(BF).reshape(nz, 2, 2, span, width)
     dn_core = start(pick(dn_part, 1 - c, 2), "tp", 1, "dn_c")
@@ -857,9 +860,8 @@
     qkv_part = mm_tn(normed_one, now(grad_projected)).astype(BF)
     qkv_grad = lax.psum_scatter(qkv_part, ("dp",) + SP, tiled=True)
     out_reduce.second()
-    proj_part = mm_tn(context, now(grad_rows)).astype(BF)
-    proj_part = proj_part.reshape(groups, nx, nz, proj_rows, width).transpose(1, 2, 0, 3, 4)
-    proj_dp = to_dp(proj_part, "proj_grad_dp")
+    proj_sum = sum_dp(proj_part, proj_dp)
+    proj_moved = chain.start_all(after(proj_sum, chain.take(up_moved)), "proj_grad_sp")
 
     grad_normed_one = (pick(dn_sum, y, 1).astype(F32) + now(dn_y).astype(F32)).reshape(-1, width)
     inverse_one = lax.rsqrt(jnp.mean(inputs * inputs, axis=-1, keepdims=True) + NORM_EPSILON)
@@ -872,8 +874,8 @@
     gains_part = jnp.stack([gain_one_part, gain_two_part])
     gains_c = start(gains_part, "tp", 1, "gains_c")
     fence(input_delta, qkv_part)
-    up_moved = chain.take(up_moved)
-    input_moved = chain.start_all(after(input_delta, up_moved), "input_sp")
+    proj_moved = chain.take(proj_moved)
+    input_moved = chain.start_all(after(input_delta, proj_moved), "input_sp")
     fence()
 
     def halves(blocks, axis):
@@ -882,17 +884,16 @@
         return jnp.concatenate(parity, axis=axis)
 
     block_delta = (attn_mine + out_reduce.result()).astype(BF).reshape(nz, span, width)
-    proj_sum = sum_dp(proj_part, proj_dp)
     gains_part = gains_part + now(gains_c)
     gains_y = start(gains_part, "tp", 2, "gains_y")
     down_grad = halves(now(down_moved), 0)
     down_new, down_first_new, down_second_new = adamw(
         now(down_weight), down_grad, down_first, down_second, DOWN_RATE, WEIGHT_DECAY
     )
-    fence(proj_sum, down_new, block_delta)
+    fence(down_new, block_delta)
 
     input_moved = chain.take(input_moved)
-    proj_moved = chain.start_all(after(proj_sum, input_moved), "proj_grad_sp")
+    block_moved = chain.start_all(after(block_delta, input_moved), "block_sp")
     fence()
 
     gains_part = (gains_part + now(gains_y)).reshape(2, nx, nz, row_block).transpose(1, 2, 0, 3)
@@ -904,8 +905,6 @@
     input_grad = now(cotangent).astype(F32) + input_moved.astype(F32)
     fence(feed_new, input_grad)
 
-    proj_moved = chain.take(proj_moved)
-    block_moved = chain.start_all(after(block_delta, proj_moved), "block_sp")
     gains_sum = pick(gains_part, xi, 0)
     for block in gains_dp:
         gains_sum = gains_sum + now(block)

time: 753 us -> 760 us (level)
  waiting for transfers between devices: 244 us -> 256 us
    all_to_all x13, waiting for transfers between devices: 56.4 us -> 88 us  [start_all(): return lax.all_to_all(blocks, SP, 0, 0, tiled=True)]
    ppermute x51, waiting for transfers between devices: 188 us -> 168 us  [swap(): lax.ppermute(value, axis, [(i, i ^ mask) for i in range(lax.axis_size(axi...]
  transfers between devices with their start and end apart: 66 -> 66, of which waited for: 22 -> 20; matrix products, arithmetic and copies ran while one was open for 24% -> 23% of each run, Pallas kernels for 23% -> 23%
where the time goes in v5:
time: 760 us; the launch traced here: 752 us
  waiting for transfers between devices  256 us (34%)
  Pallas kernels  175 us (23%)
  starting transfers between devices  105 us (14%)
  other arithmetic  88.2 us (12%)
  local copies, waits for them, and re-layouts  60.4 us (8%)
  matrix products  52.4 us (7%)
  between operations  15.5 us (2%)
    ppermute x51, waiting for transfers between devices, swap(): lax.ppermute(value, axis, [(i, i ^ mask) for i in range(lax.axis_size(axi...  168 us
    all_to_all x13, waiting for transfers between devices, start_all(): return lax.all_to_all(blocks, SP, 0, 0, tiled=True)  88 us
    all_to_all x13, starting transfers between devices, start_all(): return lax.all_to_all(blocks, SP, 0, 0, tiled=True)  58.7 us
    dot_general x7, matrix products, dot(): lax.dot_general(left, right, ((dims[0], dims[1]), ((), ())), preferred_el...  52.4 us
    ppermute x51, starting transfers between devices, swap(): lax.ppermute(value, axis, [(i, i ^ mask) for i in range(lax.axis_size(axi...  45.8 us
    pallas_call x2, Pallas kernels, ffn_back(): pl.pallas_call(functools.partial(ffn_back_kernel, tf, len(downs), parts),...  42.3 us
    unnamed x151, local copies, waits for them, and re-layouts  31.9 us
    pallas_call x2, Pallas kernels, attend_back(): pl.pallas_call(functools.partial(attend_back_kernel, tile), grid=(1,), in...  31.2 us
  transfers between devices with their start and end apart: 66, of which 20 were waited for; matrix products, arithmetic and copies ran while one was open for 23% of the time, Pallas kernels for 23%

profile of v5, /device:TPU:0, one launch (start us, length us, event | category | flops | bytes accessed | tf_op | source)
XLA Modules:
  0.0 752.1 jit_solution(11509643193376632326)
XLA Ops:
  7.2 6.3 all-to-all-start
  39.2 12.0 %collective-permute-done.2 = bf16[2,256]{1,0:T(2,128)(2,1)S(1)} collective-permute-done((bf16[2,256]{1,0:T(2,128)(2,1)S(1)}, bf16[2,256]{1,0:T(2,128)(2,1)S(1)}, u32[]{:S(2)}, u32[]{:S(2)}) %collective-permute-start.2) | collective-permute-done | bytes 1056 | tf_op jit(solution)/shard_map/gains_sp/ppermute | solution.py:42
  58.9 19.9 %collective-permute-done.4.refs_2_ = bf16[4,64,2048]{2,1,0:T(8,128)(2,1)} collective-permute-done((bf16[4,64,2048]{2,1,0:T(8,128)(2,1)S(1)}, bf16[4,64,2048]{2,1,0:T(8,128)(2,1)}, u32[]{:S(2)}, u32[]{:S(2)}) %collective-permute-start.4) | collective-permute-done | bytes 1048608 | tf_op jit(solution)/shard_map/x_y/ppermute | solution.py:42
  83.2 20.5 %all-to-all-done.1.refs_0_ = bf16[4,2,32,2048]{3,2,1,0:T(8,128)(2,1)} async-done(((bf16[4,2,32,2048]{3,2,1,0:T(8,128)(2,1)}), bf16[4,2,32,2048]{3,2,1,0:T(8,128)(2,1)}, u32[]{:S(2)}, u32[]{:S(2)}) %all-to-all-start.1) | async-done | bytes 1048608 | tf_op jit(solution)/shard_map/proj_sp/all_to_all | solution.py:541
  109.0 8.7 %project.1 = (bf16[1024,2048]{1,0:T(8,128)(2,1)}, f32[1024,768]{1,0:T(8,128)}) custom-call(s32[4]{0:T(128)} %pad_add_fusion.at_ref, bf16[4,64,2048]{2,1,0:T(8,128)(2,1)} %copy-done.10, bf16[4,64,2048]{2,1,0:T(8,128)(2,1)} %collective-permute-done.refs_1_, bf16[4,64,2048]{2,1,0:T(8,128)(2,1)} %collective-permute-done.4.refs_2_, ...), custom_call_target="tpu_custom_call" | custom-call | flops 4294967296 | bytes 1048576 | tf_op jit(solution)/shard_map/project/pallas_call | solution.py:385
  117.7 17.6 %attend.1 = (bf16[1024,768]{1,0:T(8,128)(2,1)}, bf16[1024,512]{1,0:T(8,128)(2,1)}, f32[2,4,1024]{2,1,0:T(4,128)}) custom-call(f32[1024,768]{1,0:T(8,128)} %get-tuple-element.260.p_ref, f32[1024,128]{1,0:T(8,128)} %get-tuple-element.510.cos_ref, f32[1024,128]{1,0:T(8,128)} %get-tuple-element.511.sin_ref), custom_call_target="tpu_custom_call" | custom-call | flops 68719476736 | bytes 1048576 | tf_op jit(solution)/shard_map/attend/pallas_call | solution.py:119
  159.2 17.7 %collective-permute-done.9 = bf16[4,64,2048]{2,1,0:T(8,128)(2,1)} collective-permute-done((bf16[4,64,2048]{2,1,0:T(8,128)(2,1)S(1)}, bf16[4,64,2048]{2,1,0:T(8,128)(2,1)}, u32[]{:S(2)}, u32[]{:S(2)}) %collective-permute-start.9) | collective-permute-done | bytes 1048608 | tf_op jit(solution)/shard_map/attn_y/ppermute | solution.py:42
  183.6 19.5 %collective-permute-done.11 = bf16[128,2048]{1,0:T(8,128)(2,1)S(1)} collective-permute-done((bf16[128,2048]{1,0:T(8,128)(2,1)S(1)}, bf16[128,2048]{1,0:T(8,128)(2,1)S(1)}, u32[]{:S(2)}, u32[]{:S(2)}) %collective-permute-start.11) | collective-permute-done | bytes 524320 | tf_op jit(solution)/shard_map/normed/ppermute | solution.py:42
  214.4 14.8 %collective-permute-done.13 = bf16[256,2048]{1,0:T(8,128)(2,1)S(1)} collective-permute-done((bf16[256,2048]{1,0:T(8,128)(2,1)}, bf16[256,2048]{1,0:T(8,128)(2,1)S(1)}, u32[]{:S(2)}, u32[]{:S(2)}) %collective-permute-start.13) | collective-permute-done | bytes 1048608 | tf_op jit(solution)/shard_map/normed/ppermute | solution.py:42
  229.2 14.9 %collective-permute-done.12 = bf16[256,2048]{1,0:T(8,128)(2,1)} collective-permute-done((bf16[256,2048]{1,0:T(8,128)(2,1)S(1)}, bf16[256,2048]{1,0:T(8,128)(2,1)}, u32[]{:S(2)}, u32[]{:S(2)}) %collective-permute-start.12) | collective-permute-done | bytes 1048608 | tf_op jit(solution)/shard_map/normed/ppermute | solution.py:42
  257.4 16.1 %gate_rows.1 = (f32[2048,1024]{1,0:T(8,128)}, bf16[2048,2048]{1,0:T(8,128)(2,1)}) custom-call(s32[2]{0:T(128)} %pad_add_fusion.1.at_ref, bf16[512,2048]{1,0:T(8,128)(2,1)} %pad_maximum_fusion.1.refs_0_, bf16[512,2048]{1,0:T(8,128)(2,1)} %constant_dynamic-update-slice_fusion.refs_1_, bf16[512,2048]{1,0:T(8,128)(2,1)} %collective-permute-done.15.refs_2_, ...), custom_call_target="tpu_custom_call" | custom-call | flops 68719476736 | bytes 1048576 | tf_op jit(solution)/shard_map/gate_rows/pallas_call | solution.py:265
  273.4 10.7 %collective-permute-done.19 = bf16[128,2048]{1,0:T(8,128)(2,1)S(1)} collective-permute-done((bf16[128,2048]{1,0:T(8,128)(2,1)S(1)}, bf16[128,2048]{1,0:T(8,128)(2,1)S(1)}, u32[]{:S(2)}, u32[]{:S(2)}) %collective-permute-start.19) | collective-permute-done | bytes 524320 | tf_op jit(solution)/shard_map/dy/ppermute | solution.py:42
  288.4 5.1 all-to-all-start.6
  294.4 19.2 %up_rows.1 = (bf16[2048,1024]{1,0:T(8,128)(2,1)}, f32[2048,1024]{1,0:T(8,128)}, f32[2048,1024]{1,0:T(8,128)}) custom-call(s32[2]{0:T(128)} %pad_add_fusion.1.at_ref, bf16[2048,2048]{1,0:T(8,128)(2,1)} %get-tuple-element.352.rows_ref, f32[2048,1024]{1,0:T(8,128)} %get-tuple-element.303.gate_ref, bf16[1024,1024]{1,0:T(8,128)(2,1)} %bitcast.34.refs_0_.refs_4_, ...), custom_call_target="tpu_custom_call" | custom-call | flops 68719476736 | bytes 1048576 | tf_op jit(solution)/shard_map/up_rows/pallas_call | solution.py:301
  313.6 12.2 %collective-permute-done.20 = bf16[256,2048]{1,0:T(8,128)(2,1)} collective-permute-done((bf16[256,2048]{1,0:T(8,128)(2,1)}, bf16[256,2048]{1,0:T(8,128)(2,1)}, u32[]{:S(2)}, u32[]{:S(2)}) %collective-permute-start.20) | collective-permute-done | bytes 1048608 | tf_op jit(solution)/shard_map/dy/ppermute | solution.py:42
  334.8 7.1 join.1.dy_ref
  341.9 11.4 %convolution_convert_fusion = bf16[1024,2048]{1,0:T(8,128)(2,1)S(1)} fusion(bf16[2048,1024]{1,0:T(8,128)(2,1)S(1)} %copy-done.66, bf16[2048,2048]{1,0:T(8,128)(2,1)} %join.1.dy_ref), kind=kOutput, calls=%fused_computation.17 | convolution fusion | flops 8592031744 | bytes 16777216 | tf_op jit(solution)/shard_map/dot_general | solution.py:50
  364.6 21.0 %ffn_back.2 = (bf16[2048,1024]{1,0:T(8,128)(2,1)}, bf16[2048,1024]{1,0:T(8,128)(2,1)}, bf16[1024,2048]{1,0:T(8,128)(2,1)}) custom-call(s32[2]{0:T(128)} %pad_add_fusion.1.at_ref, bf16[2048,2048]{1,0:T(8,128)(2,1)} %join.1.dy_ref, f32[2048,1024]{1,0:T(8,128)} %get-tuple-element.327.a_ref, f32[2048,1024]{1,0:T(8,128)} %get-tuple-element.328.b_ref, ...), custom_call_target="tpu_custom_call" | custom-call | flops 68719476736 | bytes 1048576 | tf_op jit(solution)/shard_map/ffn_back/pallas_call | solution.py:350
  385.5 21.4 %ffn_back.3 = (bf16[2048,1024]{1,0:T(8,128)(2,1)}, bf16[2048,1024]{1,0:T(8,128)(2,1)}, bf16[1024,2048]{1,0:T(8,128)(2,1)}) custom-call(s32[2]{0:T(128)} %pad_add_fusion.1.at_ref, bf16[2048,2048]{1,0:T(8,128)(2,1)} %join.1.dy_ref, f32[2048,1024]{1,0:T(8,128)} %get-tuple-element.327.a_ref, ...), custom_call_target="tpu_custom_call", output_to_operand_aliasing={{0}: (10, {}), {1}: (11, {})} | custom-call | flops 68719476736 | bytes 1048576 | tf_op jit(solution)/shard_map/ffn_back/pallas_call | solution.py:350
  421.3 12.7 %convolution_convert_fusion.4 = bf16[2048,1024]{1,0:T(8,128)(2,1)S(1)} fusion(bf16[2048,2048]{1,0:T(8,128)(2,1)} %get-tuple-element.352.rows_ref, bf16[2048,1024]{1,0:T(8,128)(2,1)} %get-tuple-element.344), kind=kOutput, calls=%fused_computation.21 | convolution fusion | flops 8592031744 | bytes 16777216 | tf_op jit(solution)/shard_map/dot_general | solution.py:50
  434.9 28.7 %collective-permute-done.29 = bf16[2,128,2048]{2,1,0:T(8,128)(2,1)} collective-permute-done((bf16[2,128,2048]{2,1,0:T(8,128)(2,1)}, bf16[2,128,2048]{2,1,0:T(8,128)(2,1)}, u32[]{:S(2)}, u32[]{:S(2)}) %collective-permute-start.29) | collective-permute-done | bytes 1048608 | tf_op jit(solution)/shard_map/normed_grad/ppermute | solution.py:42
  468.3 11.9 %convolution_convert_fusion.3 = bf16[2048,1024]{1,0:T(8,128)(2,1)S(1)} fusion(bf16[2048,2048]{1,0:T(8,128)(2,1)} %get-tuple-element.352.rows_ref, bf16[2048,1024]{1,0:T(8,128)(2,1)S(1)} %copy-done.71), kind=kOutput, calls=%fused_computation.20 | convolution fusion | flops 8592031744 | bytes 16777216 | tf_op jit(solution)/shard_map/dot_general | solution.py:50
  499.3 8.6 %out_rows.3 = bf16[1024,2048]{1,0:T(8,128)(2,1)} custom-call(bf16[2048,1024]{1,0:T(8,128)(2,1)} %get-tuple-element.365.hid_ref, bf16[512,2048]{1,0:T(8,128)(2,1)} %bitcast.325, bf16[512,2048]{1,0:T(8,128)(2,1)} %bitcast.329), custom_call_target="tpu_custom_call" | custom-call | flops 4294967296 | bytes 1048576 | tf_op jit(solution)/shard_map/out_rows/pallas_call | solution.py:443
  508.0 8.6 %out_rows.2 = bf16[1024,2048]{1,0:T(8,128)(2,1)} custom-call(bf16[2048,1024]{1,0:T(8,128)(2,1)} %get-tuple-element.365.hid_ref, bf16[512,2048]{1,0:T(8,128)(2,1)} %bitcast.326, bf16[512,2048]{1,0:T(8,128)(2,1)} %bitcast.330), custom_call_target="tpu_custom_call" | custom-call | flops 4294967296 | bytes 1048576 | tf_op jit(solution)/shard_map/out_rows/pallas_call | solution.py:443
  520.4 6.9 context_grad.1
  537.7 15.5 %attend_back.2.refs_0_ = bf16[1024,768]{1,0:T(8,128)(2,1)} custom-call(bf16[1024,768]{1,0:T(8,128)(2,1)} %get-tuple-element.377.qkv_ref, bf16[1024,512]{1,0:T(8,128)(2,1)} %get-tuple-element.388.grad_ref, f32[2,4,1024]{2,1,0:T(4,128)} %get-tuple-element.380.log_ref, f32[1024,128]{1,0:T(8,128)} %get-tuple-element.510.cos_ref, ...), custom_call_target="tpu_custom_call" | custom-call | flops 68719476736 | bytes 1048576 | tf_op jit(solution)/shard_map/attend_back/pallas_call | solution.py:200
  567.9 15.7 %attend_back.3 = bf16[1024,768]{1,0:T(8,128)(2,1)} custom-call(bf16[1024,768]{1,0:T(8,128)(2,1)} %get-tuple-element.377.qkv_ref, bf16[1024,512]{1,0:T(8,128)(2,1)} %get-tuple-element.388.grad_ref, f32[2,4,1024]{2,1,0:T(4,128)} %get-tuple-element.380.log_ref, f32[1024,128]{1,0:T(8,128)} %get-tuple-element.510.cos_ref, ...), custom_call_target="tpu_custom_call", output_to_operand_aliasing={{}: (5, {})} | custom-call | flops 68719476736 | bytes 1048576 | tf_op jit(solution)/shard_map/attend_back/pallas_call | solution.py:200
  583.6 5.1 convolution_convert_fusion.2
  614.4 10.7 %all-to-all-done.9 = bf16[4,256,1024]{2,1,0:T(8,128)(2,1)} async-done(((bf16[4,256,1024]{2,1,0:T(8,128)(2,1)}), bf16[4,256,1024]{2,1,0:T(8,128)(2,1)}, u32[]{:S(2)}, u32[]{:S(2)}) %all-to-all-start.9) | async-done | bytes 2097184 | tf_op jit(solution)/shard_map/up_grad_sp/all_to_all | solution.py:541
  638.0 29.6 %all-to-all-done.10 = bf16[4,2,32,2048]{3,2,1,0:T(8,128)(2,1)S(1)} async-done(((bf16[4,2,32,2048]{3,2,1,0:T(8,128)(2,1)}), bf16[4,2,32,2048]{3,2,1,0:T(8,128)(2,1)S(1)}, u32[]{:S(2)}, u32[]{:S(2)}) %all-to-all-start.10) | async-done | bytes 1048608 | tf_op jit(solution)/shard_map/proj_grad_sp/all_to_all | solution.py:541
  685.1 25.0 %all-to-all-done.11 = bf16[4,64,2048]{2,1,0:T(8,128)(2,1)} async-done(((bf16[4,64,2048]{2,1,0:T(8,128)(2,1)}), bf16[4,64,2048]{2,1,0:T(8,128)(2,1)}, u32[]{:S(2)}, u32[]{:S(2)}) %all-to-all-start.11) | async-done | bytes 1048608 | tf_op jit(solution)/shard_map/input_sp/all_to_all | solution.py:541
  724.9 7.5 multiply_subtract_fusion
  (382 shorter events, 274.3 us)
Async XLA Ops:
  7.2 45.7 %all-to-all-start = ((bf16[4,64,2048]{2,1,0:T(8,128)(2,1)}), bf16[4,64,2048]{2,1,0:T(8,128)(2,1)S(1)}, u32[]{:S(2)}, u32[]{:S(2)}) async-start(bf16[4,64,2048]{2,1,0:T(8,128)(2,1)} %param.17), calls=%async_computation | async-start | bytes 2097152 | tf_op jit(solution)/shard_map/x_sp/all_to_all | solution.py:541
  13.5 95.5 %all-gather.2.cloned.1.call-start = ((), (), s32[]{:S(2)}) async-start(), calls=%async_computation.14 | async-start | bytes 3538944 | tf_op jit(solution)/shard_map/all_gather | solution.py:672
  52.9 50.7 %all-to-all-start.1 = ((bf16[4,2,32,2048]{3,2,1,0:T(8,128)(2,1)}), bf16[4,2,32,2048]{3,2,1,0:T(8,128)(2,1)}, u32[]{:S(2)}, u32[]{:S(2)}) async-start(bf16[4,2,32,2048]{3,2,1,0:T(8,128)(2,1)} %tile.16), calls=%async_computation.1 | async-start | bytes 2097152 | tf_op jit(solution)/shard_map/proj_sp/all_to_all | solution.py:541
  58.8 50.2 %collective-permute-start = (bf16[4,64,2048]{2,1,0:T(8,128)(2,1)S(1)}, bf16[4,64,2048]{2,1,0:T(8,128)(2,1)}, u32[]{:S(2)}, u32[]{:S(2)}) collective-permute-start(bf16[4,64,2048]{2,1,0:T(8,128)(2,1)S(1)} %all-to-all-done.refs_0_), channel_id=1, source_target_pairs={{0,1},{1,0},{2,3},{3,2},{4,5},{5,4},{6,7},{7,6},{8,9},{9,8},{10,11... | collective-permute-start | bytes 3145736 | tf_op jit(solution)/shard_map/x_c/ppermute | solution.py:42
  103.7 49.1 %all-to-all-start.2 = ((bf16[4,256,1024]{2,1,0:T(8,128)(2,1)}), bf16[4,256,1024]{2,1,0:T(8,128)(2,1)}, u32[]{:S(2)}, u32[]{:S(2)}) async-start(bf16[4,256,1024]{2,1,0:T(8,128)(2,1)} %bitcast.11), calls=%async_computation.2 | async-start | bytes 4194304 | tf_op jit(solution)/shard_map/gate_sp/all_to_all | solution.py:541
  154.3 54.5 %all-to-all-start.3 = ((bf16[4,256,1024]{2,1,0:T(8,128)(2,1)}), bf16[4,256,1024]{2,1,0:T(8,128)(2,1)}, u32[]{:S(2)}, u32[]{:S(2)}) async-start(bf16[4,256,1024]{2,1,0:T(8,128)(2,1)} %bitcast.14), calls=%async_computation.3 | async-start | bytes 4194304 | tf_op jit(solution)/shard_map/up_sp/all_to_all | solution.py:541
  158.7 88.8 %collective-permute-start.14 = (bf16[4,256,1024]{2,1,0:T(8,128)(2,1)}, bf16[4,256,1024]{2,1,0:T(8,128)(2,1)}, u32[]{:S(2)}, u32[]{:S(2)}) collective-permute-start(bf16[4,256,1024]{2,1,0:T(8,128)(2,1)} %all-to-all-done.2), channel_id=1, source_target_pairs={{0,16},{16,0},{1,17},{17,1},{2,18},{18,2},{3,19},{19,3},{4,20},{20... | collective-permute-start | bytes 6291464 | tf_op jit(solution)/shard_map/gate_dp/ppermute | solution.py:42
  206.3 37.9 %collective-permute-start.12 = (bf16[256,2048]{1,0:T(8,128)(2,1)S(1)}, bf16[256,2048]{1,0:T(8,128)(2,1)}, u32[]{:S(2)}, u32[]{:S(2)}) collective-permute-start(bf16[256,2048]{1,0:T(8,128)(2,1)S(1)} %pad_maximum_fusion.6), channel_id=1, source_target_pairs={{0,4},{4,0},{8,12},{12,8},{1,5},{5,1},{9,13},{13,9},{2,6},{6,2},{1... | collective-permute-start | bytes 3145736 | tf_op jit(solution)/shard_map/normed/ppermute | solution.py:42
  208.7 48.6 %collective-permute-start.15 = (bf16[512,2048]{1,0:T(8,128)(2,1)}, bf16[512,2048]{1,0:T(8,128)(2,1)}, u32[]{:S(2)}, u32[]{:S(2)}) collective-permute-start(bf16[512,2048]{1,0:T(8,128)(2,1)} %pad_maximum_fusion.1.refs_0_), channel_id=1, source_target_pairs={{0,1},{1,0},{2,3},{3,2},{4,5},{5,4},{6,7},{7,6},{8,9},{9,8},{10,11... | collective-permute-start | bytes 6291464 | tf_op jit(solution)/shard_map/normed/ppermute | solution.py:42
  208.7 38.8 %all-to-all-start.4 = ((bf16[4,64,2048]{2,1,0:T(8,128)(2,1)}), bf16[4,64,2048]{2,1,0:T(8,128)(2,1)S(1)}, u32[]{:S(2)}, u32[]{:S(2)}) async-start(bf16[4,64,2048]{2,1,0:T(8,128)(2,1)} %param.18), calls=%async_computation.4 | async-start | bytes 2097152 | tf_op jit(solution)/shard_map/dy_sp/all_to_all | solution.py:541
  213.6 70.5 %collective-permute-start.17 = (bf16[4,256,1024]{2,1,0:T(8,128)(2,1)}, bf16[4,256,1024]{2,1,0:T(8,128)(2,1)}, u32[]{:S(2)}, u32[]{:S(2)}) collective-permute-start(bf16[4,256,1024]{2,1,0:T(8,128)(2,1)} %all-to-all-done.3), channel_id=1, source_target_pairs={{0,16},{16,0},{1,17},{17,1},{2,18},{18,2},{3,19},{19,3},{4,20},{20... | collective-permute-start | bytes 6291464 | tf_op jit(solution)/shard_map/up_dp/ppermute | solution.py:42
  248.5 39.9 %all-to-all-start.5 = ((bf16[4,2,32,2048]{3,2,1,0:T(8,128)(2,1)}), bf16[4,2,32,2048]{3,2,1,0:T(8,128)(2,1)}, u32[]{:S(2)}, u32[]{:S(2)}) async-start(bf16[4,2,32,2048]{3,2,1,0:T(8,128)(2,1)} %get-tuple-element.298), calls=%async_computation.5 | async-start | bytes 2097152 | tf_op jit(solution)/shard_map/down_sp/all_to_all | solution.py:541
  288.4 42.8 %collective-permute-start.22 = (bf16[512,2048]{1,0:T(8,128)(2,1)S(1)}, bf16[512,2048]{1,0:T(8,128)(2,1)}, u32[]{:S(2)}, u32[]{:S(2)}) collective-permute-start(bf16[512,2048]{1,0:T(8,128)(2,1)S(1)} %pad_maximum_fusion.2.refs_0_), channel_id=1, source_target_pairs={{0,1},{1,0},{2,3},{3,2},{4,5},{5,4},{6,7},{7,6},{8,9},{9,8},{10,11... | collective-permute-start | bytes 6291464 | tf_op jit(solution)/shard_map/dy/ppermute | solution.py:42
  288.4 41.9 %all-to-all-start.6 = ((bf16[4,2,32,2048]{3,2,1,0:T(8,128)(2,1)}), bf16[4,2,32,2048]{3,2,1,0:T(8,128)(2,1)S(1)}, u32[]{:S(2)}, u32[]{:S(2)}) async-start(bf16[4,2,32,2048]{3,2,1,0:T(8,128)(2,1)} %get-tuple-element.308), calls=%async_computation.6 | async-start | bytes 2097152 | tf_op jit(solution)/shard_map/down_sp/all_to_all | solution.py:541
  293.5 64.1 %collective-permute-start.24 = (bf16[4,2,32,2048]{3,2,1,0:T(8,128)(2,1)}, bf16[4,2,32,2048]{3,2,1,0:T(8,128)(2,1)}, u32[]{:S(2)}, u32[]{:S(2)}) collective-permute-start(bf16[4,2,32,2048]{3,2,1,0:T(8,128)(2,1)} %all-to-all-done.5.refs_0_), channel_id=1, source_target_pairs={{0,16},{16,0},{1,17},{17,1},{2,18},{18,2},{3,19},{19,3},{4,20},{20... | collective-permute-start | bytes 3145736 | tf_op jit(solution)/shard_map/down_dp/ppermute | solution.py:42
  356.7 58.1 %collective-permute-start.27 = (bf16[4,4,32,2048]{3,2,1,0:T(8,128)(2,1)}, bf16[4,4,32,2048]{3,2,1,0:T(8,128)(2,1)S(1)}, u32[]{:S(2)}, u32[]{:S(2)}) collective-permute-start(bf16[4,4,32,2048]{3,2,1,0:T(8,128)(2,1)} %bitcast.289), channel_id=1, source_target_pairs={{0,16},{16,0},{1,17},{17,1},{2,18},{18,2},{3,19},{19,3},{4,20},{20... | collective-permute-start | bytes 6291464 | tf_op jit(solution)/shard_map/down_grad_dp/ppermute | solution.py:42
  413.8 49.8 %collective-permute-start.28 = (bf16[2,128,2048]{2,1,0:T(8,128)(2,1)}, bf16[2,128,2048]{2,1,0:T(8,128)(2,1)S(1)}, u32[]{:S(2)}, u32[]{:S(2)}) collective-permute-start(bf16[2,128,2048]{2,1,0:T(8,128)(2,1)} %get-tuple-element.338), channel_id=1, source_target_pairs={{0,2},{1,3},{2,0},{3,1},{4,6},{5,7},{6,4},{7,5},{8,10},{9,11},{10,... | collective-permute-start | bytes 3145736 | tf_op jit(solution)/shard_map/normed_grad/ppermute | solution.py:42
  414.8 48.8 %collective-permute-start.29 = (bf16[2,128,2048]{2,1,0:T(8,128)(2,1)}, bf16[2,128,2048]{2,1,0:T(8,128)(2,1)}, u32[]{:S(2)}, u32[]{:S(2)}) collective-permute-start(bf16[2,128,2048]{2,1,0:T(8,128)(2,1)} %get-tuple-element.339), channel_id=1, source_target_pairs={{0,4},{4,0},{8,12},{12,8},{1,5},{5,1},{9,13},{13,9},{2,6},{6,2},{1... | collective-permute-start | bytes 3145736 | tf_op jit(solution)/shard_map/normed_grad/ppermute | solution.py:42
  416.9 76.6 %all-to-all-start.7 = ((bf16[4,4,32,2048]{3,2,1,0:T(8,128)(2,1)}), bf16[4,4,32,2048]{3,2,1,0:T(8,128)(2,1)S(1)}, u32[]{:S(2)}, u32[]{:S(2)}) async-start(bf16[4,4,32,2048]{3,2,1,0:T(8,128)(2,1)} %fusion.4), calls=%async_computation.7 | async-start | bytes 4194304 | tf_op jit(solution)/shard_map/down_grad_sp/all_to_all | solution.py:541
  434.1 57.0 %collective-permute-start.32 = (bf16[4,256,1024]{2,1,0:T(8,128)(2,1)S(1)}, bf16[4,256,1024]{2,1,0:T(8,128)(2,1)S(1)}, u32[]{:S(2)}, u32[]{:S(2)}) collective-permute-start(bf16[4,256,1024]{2,1,0:T(8,128)(2,1)S(1)} %dynamic-slice_bitcast_fusion.1), channel_id=1, source_target_pairs={{0,16},{16,0},{1,17},{17,1},{2,18},{18,2},{3,19},{19,3},{4,20},{20... | collective-permute-start | bytes 6291464 | tf_op jit(solution)/shard_map/gate_grad_dp/ppermute | solution.py:42
  482.9 70.3 %collective-permute-start.38 = (bf16[4,256,1024]{2,1,0:T(8,128)(2,1)}, bf16[4,256,1024]{2,1,0:T(8,128)(2,1)}, u32[]{:S(2)}, u32[]{:S(2)}) collective-permute-start(bf16[4,256,1024]{2,1,0:T(8,128)(2,1)} %dynamic-slice_bitcast_fusion), channel_id=1, source_target_pairs={{0,16},{16,0},{1,17},{17,1},{2,18},{18,2},{3,19},{19,3},{4,20},{20... | collective-permute-start | bytes 6291464 | tf_op jit(solution)/shard_map/up_grad_dp/ppermute | solution.py:42
  494.9 66.8 %all-to-all-start.8 = ((bf16[4,256,1024]{2,1,0:T(8,128)(2,1)}), bf16[4,256,1024]{2,1,0:T(8,128)(2,1)}, u32[]{:S(2)}, u32[]{:S(2)}) async-start(bf16[4,256,1024]{2,1,0:T(8,128)(2,1)} %fusion.3), calls=%async_computation.8 | async-start | bytes 4194304 | tf_op jit(solution)/shard_map/gate_grad_sp/all_to_all | solution.py:541
  534.1 63.1 %collective-permute-start.41 = (bf16[2,128,2048]{2,1,0:T(8,128)(2,1)}, bf16[2,128,2048]{2,1,0:T(8,128)(2,1)}, u32[]{:S(2)}, u32[]{:S(2)}) collective-permute-start(bf16[2,128,2048]{2,1,0:T(8,128)(2,1)} %get-tuple-element.378), channel_id=1, source_target_pairs={{0,4},{4,0},{8,12},{12,8},{1,5},{5,1},{9,13},{13,9},{2,6},{6,2},{1... | collective-permute-start | bytes 3145736 | tf_op jit(solution)/shard_map/out/ppermute | solution.py:42
  536.8 60.5 %collective-permute-start.37 = (bf16[2,128,2048]{2,1,0:T(8,128)(2,1)}, bf16[2,128,2048]{2,1,0:T(8,128)(2,1)}, u32[]{:S(2)}, u32[]{:S(2)}) collective-permute-start(bf16[2,128,2048]{2,1,0:T(8,128)(2,1)} %get-tuple-element.376), channel_id=1, source_target_pairs={{0,2},{1,3},{2,0},{3,1},{4,6},{5,7},{6,4},{7,5},{8,10},{9,11},{10,... | collective-permute-start | bytes 3145736 | tf_op jit(solution)/shard_map/out/ppermute | solution.py:42
  561.7 63.4 %all-to-all-start.9 = ((bf16[4,256,1024]{2,1,0:T(8,128)(2,1)}), bf16[4,256,1024]{2,1,0:T(8,128)(2,1)}, u32[]{:S(2)}, u32[]{:S(2)}) async-start(bf16[4,256,1024]{2,1,0:T(8,128)(2,1)} %fusion.2), calls=%async_computation.9 | async-start | bytes 4194304 | tf_op jit(solution)/shard_map/up_grad_sp/all_to_all | solution.py:541
  566.1 170.8 %reduce-scatter.2.cloned.1.call-start = ((), (), s32[]{:S(2)}) async-start(), calls=%async_computation.15 | async-start | bytes 3538944 | tf_op jit(solution)/shard_map/reduce_scatter | solution.py:861
  609.0 63.1 %collective-permute-start.44 = (bf16[128,2048]{1,0:T(8,128)(2,1)}, bf16[128,2048]{1,0:T(8,128)(2,1)}, u32[]{:S(2)}, u32[]{:S(2)}) collective-permute-start(bf16[128,2048]{1,0:T(8,128)(2,1)} %get-tuple-element.397), channel_id=1, source_target_pairs={{0,2},{1,3},{2,0},{3,1},{4,6},{5,7},{6,4},{7,5},{8,10},{9,11},{10,... | collective-permute-start | bytes 1572872 | tf_op jit(solution)/shard_map/out/ppermute | solution.py:42
  609.7 62.4 %collective-permute-start.39 = (bf16[128,2048]{1,0:T(8,128)(2,1)}, bf16[128,2048]{1,0:T(8,128)(2,1)}, u32[]{:S(2)}, u32[]{:S(2)}) collective-permute-start(bf16[128,2048]{1,0:T(8,128)(2,1)} %get-tuple-element.393), channel_id=1, source_target_pairs={{0,4},{4,0},{8,12},{12,8},{1,5},{5,1},{9,13},{13,9},{2,6},{6,2},{1... | collective-permute-start | bytes 1572872 | tf_op jit(solution)/shard_map/out/ppermute | solution.py:42
  625.0 42.6 %all-to-all-start.10 = ((bf16[4,2,32,2048]{3,2,1,0:T(8,128)(2,1)}), bf16[4,2,32,2048]{3,2,1,0:T(8,128)(2,1)S(1)}, u32[]{:S(2)}, u32[]{:S(2)}) async-start(bf16[4,2,32,2048]{3,2,1,0:T(8,128)(2,1)} %fusion.17), calls=%async_computation.10 | async-start | bytes 2097152 | tf_op jit(solution)/shard_map/proj_grad_sp/all_to_all | solution.py:541
  637.9 41.4 %collective-permute-start.45 = (f32[2,2048]{1,0:T(2,128)S(1)}, f32[2,2048]{1,0:T(2,128)S(1)}, u32[]{:S(2)}, u32[]{:S(2)}) collective-permute-start(f32[2,2048]{1,0:T(2,128)S(1)} %pad_maximum_fusion.12), channel_id=1, source_target_pairs={{0,1},{1,0},{2,3},{3,2},{4,5},{5,4},{6,7},{7,6},{8,9},{9,8},{10,11... | collective-permute-start | bytes 49160 | tf_op jit(solution)/shard_map/gains_c/ppermute | solution.py:42
  667.7 42.5 %all-to-all-start.11 = ((bf16[4,64,2048]{2,1,0:T(8,128)(2,1)}), bf16[4,64,2048]{2,1,0:T(8,128)(2,1)}, u32[]{:S(2)}, u32[]{:S(2)}) async-start(bf16[4,64,2048]{2,1,0:T(8,128)(2,1)} %fusion.14), calls=%async_computation.11 | async-start | bytes 2097152 | tf_op jit(solution)/shard_map/input_sp/all_to_all | solution.py:541
  679.4 38.2 %collective-permute-start.46 = (f32[2,2048]{1,0:T(2,128)S(1)}, f32[2,2048]{1,0:T(2,128)S(1)}, u32[]{:S(2)}, u32[]{:S(2)}) collective-permute-start(f32[2,2048]{1,0:T(2,128)S(1)} %fusion.48), channel_id=1, source_target_pairs={{0,2},{1,3},{2,0},{3,1},{4,6},{5,7},{6,4},{7,5},{8,10},{9,11},{10,... | collective-permute-start | bytes 49160 | tf_op jit(solution)/shard_map/gains_y/ppermute | solution.py:42
  (106 other events, 1276.9 us)
Sparse Core Ops, SparseCore 0:
  17.0 88.3 all-gather.1
  597.4 114.3 reduce-scatter.1
